TPU v7x, 512 devices: a whole 4x8x8 slice. The times are simulated.
512 devices in a mesh: leaf: 512 (over y, z, x, core).
Axes of the slice: x: 4, y: 8, z: 8, core: 2. Of those that a mesh axis runs over, the one named last changes fastest.
Arguments:
- points: float32 [3, 2097152], P(None, 'leaf'), may hold values from 0 to 1
- charges: float32 [16, 2097152], P(None, 'leaf'), may hold values from -6 to 6
- basis: float32 [64, 2097152], P(None, 'leaf'), may hold values from -0.5 to 0.5
- transfer: float32 [2, 64, 64], replicated, may hold values from -0.75 to 0.75
- near_list: int32 [12, 16384], P(None, 'leaf'), may hold values from 0 to 16383, as said below
- coupling_list: int32 [4, 32760], replicated, may hold values from 0 to 16383, as said below
- ordering: int32 [2097152], P('leaf'), may hold values from 0 to 127, as said below
Outputs:
- potential: float32 [16, 2097152], P(None, 'leaf')
Inputs may be any that keep to these rules, and one draw needn't show every extreme that they name: `near_list`: entry 0 of leaf b is b; the 12 entries of a leaf are distinct and each is (b + w) mod 16384 with 1 <= |w| <= 32. `coupling_list`: column 2 * 16384 - 2 n + t, for a level with n = 16384 >> l clusters (l from 0 while n >= 8), lists clusters (t + o) mod n of that level with each o one of 2, 3, -3, -2; entries may repeat. `ordering`: the 128 entries of each leaf are a permutation of 0 to 127.
All inputs are finite; a program needn't handle non-finite values.
Results may differ from a plain program's by a relative error of at most 0.0003.
Values sent between devices are 32-bit elements; how exact they have to be, the bound alone decides.
No kernel may reach another device: no remote copies, remote signals or barrier semaphores. Data moves between devices by JAX's collectives and lax.ppermute only.
A program may use at most 128 MiB of HBM per device.

v0:
```python
import math

import jax
import jax.numpy as jnp
from jax import lax
from jax.sharding import PartitionSpec as P

ORDER = 4


HIGHEST = lax.Precision.HIGHEST
OFFSETS = (2, 3, -3, -2)
DELTA = 0.05
PROXY = 0.35


def padded(cells, sides, width):
    for axis, dim in sides:
        count = lax.axis_size(axis)
        head = lax.slice_in_dim(cells, 0, width, axis=dim)
        tail = lax.slice_in_dim(cells, cells.shape[dim] - width, cells.shape[dim], axis=dim)
        cells = jnp.concatenate(
            [
                lax.ppermute(tail, axis, [(i, (i + 1) % count) for i in range(count)]),
                cells,
                lax.ppermute(head, axis, [((i + 1) % count, i) for i in range(count)]),
            ],
            axis=dim,
        )
    return cells


def from_behind(block, axis, distance):
    devices = range(lax.axis_size(axis))
    route = [((i - distance) % len(devices), i) for i in devices]
    return lax.ppermute(block, axis, route)


def from_partner(value, axis, bit):
    mask = 2**bit
    pairs = [(source, source ^ mask) for source in range(lax.axis_size(axis))]
    return lax.ppermute(value, axis, pairs)


def unit_nodes(node_order):
    counter = jnp.arange(node_order, dtype=jnp.float32)
    cheb_nodes = jnp.cos((2.0 * counter + 1.0) * (math.pi / (2.0 * node_order)))
    coord_one = jnp.repeat(cheb_nodes, node_order * node_order)
    coord_two = jnp.tile(jnp.repeat(cheb_nodes, node_order), node_order)
    coord_three = jnp.tile(cheb_nodes, node_order * node_order)
    return jnp.stack([coord_one, coord_two, coord_three])


def coupling_blocks(node_order):
    proxies = unit_nodes(node_order) * PROXY
    stacked = []
    for shift_by in OFFSETS:
        moved = proxies + jnp.array([float(shift_by), 0.0, 0.0], dtype=jnp.float32)[:, None]
        difference = proxies[:, :, None] - moved[:, None, :]
        distance = jnp.sqrt(jnp.sum(difference * difference, axis=0))
        stacked.append(0.25 / math.pi / distance)
    return jnp.stack(stacked)


def apply_up(left_part, right_part, transfer):
    return jnp.einsum("...ra,ab->...rb", left_part, transfer[0], precision=HIGHEST) + jnp.einsum(
        "...ra,ab->...rb", right_part, transfer[1], precision=HIGHEST
    )


def apply_down(parent, matrix):
    return jnp.einsum("...rb,ab->...ra", parent, matrix, precision=HIGHEST)


def offset_counts(row_ids, targets, clusters):
    relative = jnp.mod(row_ids - targets[None, :], clusters)
    return [
        jnp.sum((relative == shift_by % clusters).astype(jnp.float32), axis=0)
        for shift_by in OFFSETS
    ]


def combine(candidates, counts, blocks, level_id):
    summed = jnp.zeros(candidates[0].shape, jnp.float32)
    for slot_id in range(len(OFFSETS)):
        product = jnp.einsum("nrb,ab->nra", candidates[slot_id], blocks[slot_id], precision=HIGHEST)
        summed = summed + counts[slot_id][:, None, None] * product
    return summed * 0.5**level_id


def wrapped(delta_ids, total_leaves):
    half_cycle = total_leaves // 2
    return jnp.mod(delta_ids + half_cycle, total_leaves) - half_cycle


def near_group(targets, sources, offsets, leaf_pitch):
    shift_x = offsets.astype(jnp.float32) * leaf_pitch
    dist_sq = jnp.full(
        (sources.shape[0], sources.shape[1], targets.shape[2], sources.shape[3]),
        DELTA * DELTA,
        jnp.float32,
    )
    for axis_id in range(3):
        source_axis = sources[:, :, axis_id, :]
        if axis_id == 0:
            source_axis = source_axis + shift_x[:, :, None]
        difference = targets[axis_id][:, None, :, None] - source_axis[:, :, None, :]
        dist_sq = dist_sq + difference * difference
    kernel = lax.rsqrt(dist_sq) * (0.25 / math.pi)
    return jnp.einsum("gkij,gkrj->rgi", kernel, sources[:, :, 3:, :], precision=HIGHEST)


def local(points, charges, basis, transfer, near_list, coupling_list, ordering):
    device = lax.axis_index("leaf")
    device_count = lax.axis_size("leaf")
    local_leaves = near_list.shape[1]
    leaf_size = ordering.shape[0] // local_leaves
    rhs_count = charges.shape[0]
    rank_count = basis.shape[0]
    flat_width = rhs_count * rank_count
    row_count = coupling_list.shape[0]
    total_leaves = local_leaves * device_count
    log_dev = local_leaves.bit_length() - 1
    top_level = log_dev + device_count.bit_length() - 1 - 3
    leaf_pitch = 1.0 / local_leaves
    blocks = coupling_blocks(ORDER)
    permuted_ids = ordering.reshape(local_leaves, leaf_size)
    inverse_ids = jnp.argsort(permuted_ids, axis=1)

    def to_tree(values):
        shaped = values.reshape(values.shape[0], local_leaves, leaf_size)
        return jnp.take_along_axis(shaped, permuted_ids[None], axis=2)

    data = jnp.concatenate([to_tree(points), to_tree(charges)], axis=0)
    channels = data.shape[0]
    extended = padded(
        data.reshape(channels, local_leaves * leaf_size), (("leaf", 1),), local_leaves * leaf_size
    )
    extended = extended.reshape(channels, 3 * local_leaves, leaf_size)
    first_leaf = device * local_leaves

    def near_block(group_id):
        leaf_ids = group_id * 4 + jnp.arange(4, dtype=jnp.int32)
        source_ids = jnp.take(near_list, leaf_ids, axis=1).T
        offsets = wrapped(source_ids - (first_leaf + leaf_ids)[:, None], total_leaves)
        local_ids = local_leaves + leaf_ids[:, None] + offsets
        sources = jnp.transpose(jnp.take(extended, local_ids, axis=1), (1, 2, 0, 3))
        targets = jnp.take(data[:3], leaf_ids, axis=1)
        return near_group(targets, sources, offsets, leaf_pitch)

    near_part = lax.map(near_block, jnp.arange(local_leaves // 4, dtype=jnp.int32))
    near_part = jnp.transpose(near_part, (1, 0, 2, 3)).reshape(rhs_count, local_leaves, leaf_size)
    basis_leaf = basis.reshape(rank_count, local_leaves, leaf_size)
    current = jnp.einsum("anl,rnl->nra", basis_leaf, data[3:], precision=HIGHEST)

    def neighbour_blocks(values, count):
        flattened = values.reshape(count, flat_width)
        if count >= 4:
            widened = padded(flattened, (("leaf", 0),), 3)
            pieces = [widened[3 + shift_by : 3 + shift_by + count] for shift_by in OFFSETS]
        else:
            beside_all = {}
            for step_by in (2, 1, -1, -2):
                beside_all[step_by] = from_behind(flattened, "leaf", step_by)
            widened = jnp.concatenate(
                [beside_all[2], beside_all[1], flattened, beside_all[-1], beside_all[-2]], axis=0
            )
            pieces = [widened[4 + shift_by : 4 + shift_by + count] for shift_by in OFFSETS]
        return [piece.reshape(count, rhs_count, rank_count) for piece in pieces]

    local_terms = []
    for level_id in range(log_dev):
        count = local_leaves >> level_id
        clusters = total_leaves >> level_id
        start = 2 * total_leaves - 2 * clusters
        first_cluster = device * count
        row_ids = lax.dynamic_slice(coupling_list, (0, start + first_cluster), (row_count, count))
        targets = first_cluster + jnp.arange(count, dtype=jnp.int32)
        counts = offset_counts(row_ids, targets, clusters)
        local_terms.append(combine(neighbour_blocks(current, count), counts, blocks, level_id))
        paired = current.reshape(count // 2, 2, rhs_count, rank_count)
        current = apply_up(paired[:, 0], paired[:, 1], transfer)
    upper_terms = []
    for level_id in range(log_dev, top_level + 1):
        shift_level = level_id - log_dev
        clusters = total_leaves >> level_id
        start = 2 * total_leaves - 2 * clusters
        cluster_id = device >> shift_level
        flattened = current.reshape(1, flat_width)
        pieces = [
            from_behind(flattened, "leaf", -shift_by * (1 << shift_level)).reshape(
                1, rhs_count, rank_count
            )
            for shift_by in OFFSETS
        ]
        row_ids = lax.dynamic_slice(coupling_list, (0, start + cluster_id), (row_count, 1))
        counts = offset_counts(row_ids, jnp.reshape(cluster_id, (1,)), clusters)
        upper_terms.append(combine(pieces, counts, blocks, level_id))
        if level_id < top_level:
            partner = from_partner(flattened, "leaf", shift_level).reshape(1, rhs_count, rank_count)
            is_first = cluster_id % 2 == 0
            left_part = jnp.where(is_first, current, partner)
            right_part = jnp.where(is_first, partner, current)
            current = apply_up(left_part, right_part, transfer)
    summed_down = upper_terms[-1]
    for level_id in range(top_level, log_dev, -1):
        child_bit = (device >> level_id - 1 - log_dev) % 2
        from_parent = jnp.where(
            child_bit == 0,
            apply_down(summed_down, transfer[0]),
            apply_down(summed_down, transfer[1]),
        )
        summed_down = upper_terms[level_id - 1 - log_dev] + from_parent
    for level_id in range(log_dev, 0, -1):
        child = local_terms[level_id - 1].reshape(-1, 2, rhs_count, rank_count)
        first_child = child[:, 0] + apply_down(summed_down, transfer[0])
        second_child = child[:, 1] + apply_down(summed_down, transfer[1])
        summed_down = jnp.stack([first_child, second_child], axis=1).reshape(
            -1, rhs_count, rank_count
        )
    far_part = jnp.einsum("nra,anl->rnl", summed_down, basis_leaf, precision=HIGHEST)
    tree_total = near_part + far_part
    restored = jnp.take_along_axis(tree_total, inverse_ids[None], axis=2)
    return restored.reshape(rhs_count, local_leaves * leaf_size)


def solution(mesh):
    placed = (
        P(None, "leaf"),
        P(None, "leaf"),
        P(None, "leaf"),
        P(),
        P(None, "leaf"),
        P(),
        P("leaf"),
    )
    return jax.shard_map(
        local, mesh=mesh, in_specs=placed, out_specs=P(None, "leaf"), check_vma=False
    )
```

profile of v0, /device:TPU:1, one launch (start us, length us, event | category | flops | bytes accessed | tf_op | source)
XLA Modules:
  0.0 619.6 jit_solution(15917136241515207128)
XLA Ops:
  9.6 44.4 %gather_fusion.4 = f32[4096,16]{1,0:T(8,128)} fusion(f32[16,32,128]{0,2,1:T(8,128)S(1)} %bitcast.471, s32[4096]{0:T(1024)S(1)} %get-tuple-element.245), kind=kCustom, calls=%fused_computation.clone | custom fusion | bytes 557056 | tf_op jit(solution)/shard_map/jit(take_along_axis)/gather | solution.py:132
  60.1 8.8 %collective-permute-start.18 = (f32[1,1024]{1,0:T(1,128)S(1)}, f32[1,1024]{1,0:T(1,128)S(1)}, u32[]{:S(2)}, u32[]{:S(2)}) collective-permute-start(f32[1,1024]{1,0:T(1,128)S(1)} %reshape.1083), channel_id=1, source_target_pairs={{0,1},{1,0},{2,3},{3,2},{4,5},{5,4},{6,7},{7,6},{8,9},{9,8},{10,11... | collective-permute-start | bytes 12296 | tf_op jit(solution)/shard_map/ppermute | solution.py:42
  68.9 12.8 %collective-permute-start.15 = (f32[1,1024]{1,0:T(1,128)S(1)}, f32[1,1024]{1,0:T(1,128)S(1)}, u32[]{:S(2)}, u32[]{:S(2)}) collective-permute-start(f32[1,1024]{1,0:T(1,128)S(1)} %reshape.1083), channel_id=1, source_target_pairs={{3,0},{4,1},{5,2},{6,3},{7,4},{8,5},{9,6},{10,7},{11,8},{12,9},{13... | collective-permute-start | bytes 12296 | tf_op jit(solution)/shard_map/ppermute | solution.py:36
  88.9 16.5 %collective-permute-start.14 = (f32[1,1024]{1,0:T(1,128)S(1)}, f32[1,1024]{1,0:T(1,128)S(1)}, u32[]{:S(2)}, u32[]{:S(2)}) collective-permute-start(f32[1,1024]{1,0:T(1,128)S(1)} %reshape.1083), channel_id=1, source_target_pairs={{2,0},{3,1},{4,2},{5,3},{6,4},{7,5},{8,6},{9,7},{10,8},{11,9},{12,... | collective-permute-start | bytes 12296 | tf_op jit(solution)/shard_map/ppermute | solution.py:36
  114.6 59.6 %gather_fusion.3 = f32[4096,3]{1,0:T(8,128)} fusion(f32[3,32,128]{0,2,1:T(8,128)} %bitcast.472, s32[4096]{0:T(1024)S(1)} %get-tuple-element.244), kind=kCustom, calls=%fused_computation.5 | custom fusion | bytes 131072 | tf_op jit(solution)/shard_map/jit(take_along_axis)/gather | solution.py:132
  185.7 6.0 collective-permute-start.10
  193.4 13.0 %collective-permute-start.11 = (f32[2,1024]{1,0:T(2,128)S(1)}, f32[2,1024]{1,0:T(2,128)S(1)}, u32[]{:S(2)}, u32[]{:S(2)}) collective-permute-start(f32[2,1024]{1,0:T(2,128)S(1)} %reshape.1074), channel_id=1, source_target_pairs={{2,0},{3,1},{4,2},{5,3},{6,4},{7,5},{8,6},{9,7},{10,8},{11,9},{12,... | collective-permute-start | bytes 24584 | tf_op jit(solution)/shard_map/ppermute | solution.py:36
  222.4 10.8 %collective-permute-start.20 = (f32[1,1024]{1,0:T(1,128)S(1)}, f32[1,1024]{1,0:T(1,128)S(1)}, u32[]{:S(2)}, u32[]{:S(2)}) collective-permute-start(f32[1,1024]{1,0:T(1,128)S(1)} %reshape.1089), channel_id=1, source_target_pairs={{6,0},{7,1},{8,2},{9,3},{10,4},{11,5},{12,6},{13,7},{14,8},{15,9},... | collective-permute-start | bytes 12296 | tf_op jit(solution)/shard_map/ppermute | solution.py:36
  239.4 13.7 %collective-permute-start.19 = (f32[1,1024]{1,0:T(1,128)S(1)}, f32[1,1024]{1,0:T(1,128)S(1)}, u32[]{:S(2)}, u32[]{:S(2)}) collective-permute-start(f32[1,1024]{1,0:T(1,128)S(1)} %reshape.1089), channel_id=1, source_target_pairs={{4,0},{5,1},{6,2},{7,3},{8,4},{9,5},{10,6},{11,7},{12,8},{13,9},{1... | collective-permute-start | bytes 12296 | tf_op jit(solution)/shard_map/ppermute | solution.py:36
  259.4 10.9 %collective-permute-start.25 = (f32[1,1024]{1,0:T(1,128)S(1)}, f32[1,1024]{1,0:T(1,128)S(1)}, u32[]{:S(2)}, u32[]{:S(2)}) collective-permute-start(f32[1,1024]{1,0:T(1,128)S(1)} %reshape.1095), channel_id=1, source_target_pairs={{12,0},{13,1},{14,2},{15,3},{16,4},{17,5},{18,6},{19,7},{20,8},{21... | collective-permute-start | bytes 12296 | tf_op jit(solution)/shard_map/ppermute | solution.py:36
  276.5 7.9 %collective-permute-start.24 = (f32[1,1024]{1,0:T(1,128)S(1)}, f32[1,1024]{1,0:T(1,128)S(1)}, u32[]{:S(2)}, u32[]{:S(2)}) collective-permute-start(f32[1,1024]{1,0:T(1,128)S(1)} %reshape.1095), channel_id=1, source_target_pairs={{8,0},{9,1},{10,2},{11,3},{12,4},{13,5},{14,6},{15,7},{16,8},{17,9... | collective-permute-start | bytes 12296 | tf_op jit(solution)/shard_map/ppermute | solution.py:36
  293.6 8.6 %collective-permute-start.6 = (f32[3,1024]{1,0:T(4,128)S(1)}, f32[3,1024]{1,0:T(4,128)S(1)}, u32[]{:S(2)}, u32[]{:S(2)}) collective-permute-start(f32[3,1024]{1,0:T(4,128)S(1)} %slice.295), channel_id=1, source_target_pairs={{1,0},{2,1},{3,2},{4,3},{5,4},{6,5},{7,6},{8,7},{9,8},{10,9},{11,1... | collective-permute-start | bytes 36872 | tf_op jit(solution)/shard_map/ppermute | solution.py:26
  303.0 16.7 %collective-permute-start.8 = (f32[3,1024]{1,0:T(4,128)S(1)}, f32[3,1024]{1,0:T(4,128)S(1)}, u32[]{:S(2)}, u32[]{:S(2)}) collective-permute-start(f32[3,1024]{1,0:T(4,128)S(1)} %slice.306), channel_id=1, source_target_pairs={{1,0},{2,1},{3,2},{4,3},{5,4},{6,5},{7,6},{8,7},{9,8},{10,9},{11,1... | collective-permute-start | bytes 36872 | tf_op jit(solution)/shard_map/ppermute | solution.py:26
  332.3 7.3 %collective-permute-start.4 = (f32[3,1024]{1,0:T(4,128)S(1)}, f32[3,1024]{1,0:T(4,128)S(1)}, u32[]{:S(2)}, u32[]{:S(2)}) collective-permute-start(f32[3,1024]{1,0:T(4,128)S(1)} %slice.284), channel_id=1, source_target_pairs={{1,0},{2,1},{3,2},{4,3},{5,4},{6,5},{7,6},{8,7},{9,8},{10,9},{11,1... | collective-permute-start | bytes 36872 | tf_op jit(solution)/shard_map/ppermute | solution.py:26
  342.4 6.7 %collective-permute-start.2 = (f32[3,1024]{1,0:T(4,128)S(1)}, f32[3,1024]{1,0:T(4,128)S(1)}, u32[]{:S(2)}, u32[]{:S(2)}) collective-permute-start(f32[3,1024]{1,0:T(4,128)S(1)} %slice.271), channel_id=1, source_target_pairs={{1,0},{2,1},{3,2},{4,3},{5,4},{6,5},{7,6},{8,7},{9,8},{10,9},{11,1... | collective-permute-start | bytes 36872 | tf_op jit(solution)/shard_map/ppermute | solution.py:26
  353.1 6.3 %collective-permute-start.30 = (f32[1,1024]{1,0:T(1,128)}, f32[1,1024]{1,0:T(1,128)}, u32[]{:S(2)}, u32[]{:S(2)}) collective-permute-start(f32[1,1024]{1,0:T(1,128)} %reshape.1101), channel_id=1, source_target_pairs={{24,0},{25,1},{26,2},{27,3},{28,4},{29,5},{30,6},{31,7},{32,8},{33... | collective-permute-start | bytes 12296 | tf_op jit(solution)/shard_map/ppermute | solution.py:36
  377.7 6.9 %collective-permute-start.29 = (f32[1,1024]{1,0:T(1,128)}, f32[1,1024]{1,0:T(1,128)S(1)}, u32[]{:S(2)}, u32[]{:S(2)}) collective-permute-start(f32[1,1024]{1,0:T(1,128)} %reshape.1101), channel_id=1, source_target_pairs={{16,0},{17,1},{18,2},{19,3},{20,4},{21,5},{22,6},{23,7},{24,8},{25... | collective-permute-start | bytes 12296 | tf_op jit(solution)/shard_map/ppermute | solution.py:36
  408.3 7.9 %collective-permute-start.34 = (f32[1,1024]{1,0:T(1,128)S(1)}, f32[1,1024]{1,0:T(1,128)S(1)}, u32[]{:S(2)}, u32[]{:S(2)}) collective-permute-start(f32[1,1024]{1,0:T(1,128)S(1)} %reshape.1107), channel_id=1, source_target_pairs={{32,0},{33,1},{34,2},{35,3},{36,4},{37,5},{38,6},{39,7},{40,8},{41... | collective-permute-start | bytes 12296 | tf_op jit(solution)/shard_map/ppermute | solution.py:36
  419.9 6.5 %collective-permute-start.40 = (f32[1,1024]{1,0:T(1,128)S(1)}, f32[1,1024]{1,0:T(1,128)S(1)}, u32[]{:S(2)}, u32[]{:S(2)}) collective-permute-start(f32[1,1024]{1,0:T(1,128)S(1)} %reshape.1113), channel_id=1, source_target_pairs={{96,0},{97,1},{98,2},{99,3},{100,4},{101,5},{102,6},{103,7},{104,8... | collective-permute-start | bytes 12296 | tf_op jit(solution)/shard_map/ppermute | solution.py:36
  437.9 7.2 %collective-permute-start.39 = (f32[1,1024]{1,0:T(1,128)S(1)}, f32[1,1024]{1,0:T(1,128)S(1)}, u32[]{:S(2)}, u32[]{:S(2)}) collective-permute-start(f32[1,1024]{1,0:T(1,128)S(1)} %reshape.1113), channel_id=1, source_target_pairs={{64,0},{65,1},{66,2},{67,3},{68,4},{69,5},{70,6},{71,7},{72,8},{73... | collective-permute-start | bytes 12296 | tf_op jit(solution)/shard_map/ppermute | solution.py:36
  448.9 5.1 collective-permute-start.46
  466.7 10.7 %collective-permute-start.1 = (f32[19,4096]{1,0:T(8,128)}, f32[19,4096]{1,0:T(8,128)S(1)}, u32[]{:S(2)}, u32[]{:S(2)}) collective-permute-start(f32[19,4096]{1,0:T(8,128)} %bitcast.126), channel_id=1, source_target_pairs={{1,0},{2,1},{3,2},{4,3},{5,4},{6,5},{7,6},{8,7},{9,8},{10,9},{11,1... | collective-permute-start | bytes 933896 | tf_op jit(solution)/shard_map/ppermute | solution.py:26
  490.5 72.0 %while.12 = (s32[]{:T(128)}, f32[8,16,4,128]{3,1,2,0:T(8,128)}, s32[8]{0:T(128)S(1)}, s32[12,32]{0,1:T(8,128)S(1)}, s32[]{:T(128)}, /*index=5*/f32[19,96,128]{2,...) while((s32[]{:T(128)}, f32[8,16,4,128]{3,1,2,0:T(8,128)}, s32[8]{0:T(128)S(1)}, ...), condition=%wide.region_1.3_spmd, body=%wide.region_0.2_spmd.sunk | while | flops 158986944 | bytes 2888817 | solution.py:151
  565.1 44.4 %gather_fusion.5 = f32[4096,16]{1,0:T(8,128)} fusion(f32[16,32,128]{0,2,1:T(8,128)S(1)} %copy.160, s32[4096]{0:T(1024)S(1)} %fusion.199), kind=kCustom, calls=%fused_computation.4.clone | custom fusion | bytes 557056 | tf_op jit(solution)/shard_map/jit(take_along_axis)/gather | solution.py:223
  (608 shorter events, 259.3 us)
Async XLA Ops:
  60.1 125.6 %collective-permute-start.18 = (f32[1,1024]{1,0:T(1,128)S(1)}, f32[1,1024]{1,0:T(1,128)S(1)}, u32[]{:S(2)}, u32[]{:S(2)}) collective-permute-start(f32[1,1024]{1,0:T(1,128)S(1)} %reshape.1083), channel_id=1, source_target_pairs={{0,1},{1,0},{2,3},{3,2},{4,5},{5,4},{6,7},{7,6},{8,9},{9,8},{10,11... | collective-permute-start | bytes 12296 | tf_op jit(solution)/shard_map/ppermute | solution.py:42
  68.9 124.5 %collective-permute-start.15 = (f32[1,1024]{1,0:T(1,128)S(1)}, f32[1,1024]{1,0:T(1,128)S(1)}, u32[]{:S(2)}, u32[]{:S(2)}) collective-permute-start(f32[1,1024]{1,0:T(1,128)S(1)} %reshape.1083), channel_id=1, source_target_pairs={{3,0},{4,1},{5,2},{6,3},{7,4},{8,5},{9,6},{10,7},{11,8},{12,9},{13... | collective-permute-start | bytes 12296 | tf_op jit(solution)/shard_map/ppermute | solution.py:36
  81.7 125.4 %collective-permute-start.16 = (f32[1,1024]{1,0:T(1,128)S(1)}, f32[1,1024]{1,0:T(1,128)S(1)}, u32[]{:S(2)}, u32[]{:S(2)}) collective-permute-start(f32[1,1024]{1,0:T(1,128)S(1)} %reshape.1083), channel_id=1, source_target_pairs={{509,0},{510,1},{511,2},{0,3},{1,4},{2,5},{3,6},{4,7},{5,8},{6,9},... | collective-permute-start | bytes 12296 | tf_op jit(solution)/shard_map/ppermute | solution.py:36
  86.7 124.6 %collective-permute-start.17 = (f32[1,1024]{1,0:T(1,128)S(1)}, f32[1,1024]{1,0:T(1,128)S(1)}, u32[]{:S(2)}, u32[]{:S(2)}) collective-permute-start(f32[1,1024]{1,0:T(1,128)S(1)} %reshape.1083), channel_id=1, source_target_pairs={{510,0},{511,1},{0,2},{1,3},{2,4},{3,5},{4,6},{5,7},{6,8},{7,9},{8... | collective-permute-start | bytes 12296 | tf_op jit(solution)/shard_map/ppermute | solution.py:36
  88.9 126.3 %collective-permute-start.14 = (f32[1,1024]{1,0:T(1,128)S(1)}, f32[1,1024]{1,0:T(1,128)S(1)}, u32[]{:S(2)}, u32[]{:S(2)}) collective-permute-start(f32[1,1024]{1,0:T(1,128)S(1)} %reshape.1083), channel_id=1, source_target_pairs={{2,0},{3,1},{4,2},{5,3},{6,4},{7,5},{8,6},{9,7},{10,8},{11,9},{12,... | collective-permute-start | bytes 12296 | tf_op jit(solution)/shard_map/ppermute | solution.py:36
  185.7 50.5 %collective-permute-start.10 = (f32[2,1024]{1,0:T(2,128)S(1)}, f32[2,1024]{1,0:T(2,128)S(1)}, u32[]{:S(2)}, u32[]{:S(2)}) collective-permute-start(f32[2,1024]{1,0:T(2,128)S(1)} %reshape.1074), channel_id=1, source_target_pairs={{1,0},{2,1},{3,2},{4,3},{5,4},{6,5},{7,6},{8,7},{9,8},{10,9},{11,1... | collective-permute-start | bytes 24584 | tf_op jit(solution)/shard_map/ppermute | solution.py:36
  193.4 46.0 %collective-permute-start.11 = (f32[2,1024]{1,0:T(2,128)S(1)}, f32[2,1024]{1,0:T(2,128)S(1)}, u32[]{:S(2)}, u32[]{:S(2)}) collective-permute-start(f32[2,1024]{1,0:T(2,128)S(1)} %reshape.1074), channel_id=1, source_target_pairs={{2,0},{3,1},{4,2},{5,3},{6,4},{7,5},{8,6},{9,7},{10,8},{11,9},{12,... | collective-permute-start | bytes 24584 | tf_op jit(solution)/shard_map/ppermute | solution.py:36
  207.1 66.6 %collective-permute-start.13 = (f32[2,1024]{1,0:T(2,128)S(1)}, f32[2,1024]{1,0:T(2,128)S(1)}, u32[]{:S(2)}, u32[]{:S(2)}) collective-permute-start(f32[2,1024]{1,0:T(2,128)S(1)} %reshape.1074), channel_id=1, source_target_pairs={{511,0},{0,1},{1,2},{2,3},{3,4},{4,5},{5,6},{6,7},{7,8},{8,9},{9,1... | collective-permute-start | bytes 24584 | tf_op jit(solution)/shard_map/ppermute | solution.py:36
  211.4 65.1 %collective-permute-start.12 = (f32[2,1024]{1,0:T(2,128)S(1)}, f32[2,1024]{1,0:T(2,128)S(1)}, u32[]{:S(2)}, u32[]{:S(2)}) collective-permute-start(f32[2,1024]{1,0:T(2,128)S(1)} %reshape.1074), channel_id=1, source_target_pairs={{510,0},{511,1},{0,2},{1,3},{2,4},{3,5},{4,6},{5,7},{6,8},{7,9},{8... | collective-permute-start | bytes 24584 | tf_op jit(solution)/shard_map/ppermute | solution.py:36
  239.4 31.6 %collective-permute-start.19 = (f32[1,1024]{1,0:T(1,128)S(1)}, f32[1,1024]{1,0:T(1,128)S(1)}, u32[]{:S(2)}, u32[]{:S(2)}) collective-permute-start(f32[1,1024]{1,0:T(1,128)S(1)} %reshape.1089), channel_id=1, source_target_pairs={{4,0},{5,1},{6,2},{7,3},{8,4},{9,5},{10,6},{11,7},{12,8},{13,9},{1... | collective-permute-start | bytes 12296 | tf_op jit(solution)/shard_map/ppermute | solution.py:36
  253.9 35.4 %collective-permute-start.28 = (f32[1,1024]{1,0:T(1,128)S(1)}, f32[1,1024]{1,0:T(1,128)S(1)}, u32[]{:S(2)}, u32[]{:S(2)}) collective-permute-start(f32[1,1024]{1,0:T(1,128)S(1)} %reshape.1095), channel_id=1, source_target_pairs={{0,4},{1,5},{2,6},{3,7},{4,0},{5,1},{6,2},{7,3},{8,12},{9,13},{10,... | collective-permute-start | bytes 12296 | tf_op jit(solution)/shard_map/ppermute | solution.py:42
  259.4 34.2 %collective-permute-start.25 = (f32[1,1024]{1,0:T(1,128)S(1)}, f32[1,1024]{1,0:T(1,128)S(1)}, u32[]{:S(2)}, u32[]{:S(2)}) collective-permute-start(f32[1,1024]{1,0:T(1,128)S(1)} %reshape.1095), channel_id=1, source_target_pairs={{12,0},{13,1},{14,2},{15,3},{16,4},{17,5},{18,6},{19,7},{20,8},{21... | collective-permute-start | bytes 12296 | tf_op jit(solution)/shard_map/ppermute | solution.py:36
  271.0 32.0 %collective-permute-start.26 = (f32[1,1024]{1,0:T(1,128)S(1)}, f32[1,1024]{1,0:T(1,128)S(1)}, u32[]{:S(2)}, u32[]{:S(2)}) collective-permute-start(f32[1,1024]{1,0:T(1,128)S(1)} %reshape.1095), channel_id=1, source_target_pairs={{500,0},{501,1},{502,2},{503,3},{504,4},{505,5},{506,6},{507,7},{5... | collective-permute-start | bytes 12296 | tf_op jit(solution)/shard_map/ppermute | solution.py:36
  273.7 46.7 %collective-permute-start.27 = (f32[1,1024]{1,0:T(1,128)S(1)}, f32[1,1024]{1,0:T(1,128)S(1)}, u32[]{:S(2)}, u32[]{:S(2)}) collective-permute-start(f32[1,1024]{1,0:T(1,128)S(1)} %reshape.1095), channel_id=1, source_target_pairs={{504,0},{505,1},{506,2},{507,3},{508,4},{509,5},{510,6},{511,7},{0... | collective-permute-start | bytes 12296 | tf_op jit(solution)/shard_map/ppermute | solution.py:36
  276.5 48.2 %collective-permute-start.24 = (f32[1,1024]{1,0:T(1,128)S(1)}, f32[1,1024]{1,0:T(1,128)S(1)}, u32[]{:S(2)}, u32[]{:S(2)}) collective-permute-start(f32[1,1024]{1,0:T(1,128)S(1)} %reshape.1095), channel_id=1, source_target_pairs={{8,0},{9,1},{10,2},{11,3},{12,4},{13,5},{14,6},{15,7},{16,8},{17,9... | collective-permute-start | bytes 12296 | tf_op jit(solution)/shard_map/ppermute | solution.py:36
  289.3 53.1 %collective-permute-start.7 = (f32[3,1024]{1,0:T(4,128)S(1)}, f32[3,1024]{1,0:T(4,128)S(1)}, u32[]{:S(2)}, u32[]{:S(2)}) collective-permute-start(f32[3,1024]{1,0:T(4,128)S(1)} %slice.299), channel_id=1, source_target_pairs={{0,1},{1,2},{2,3},{3,4},{4,5},{5,6},{6,7},{7,8},{8,9},{9,10},{10,1... | collective-permute-start | bytes 36872 | tf_op jit(solution)/shard_map/ppermute | solution.py:24
  293.6 55.5 %collective-permute-start.6 = (f32[3,1024]{1,0:T(4,128)S(1)}, f32[3,1024]{1,0:T(4,128)S(1)}, u32[]{:S(2)}, u32[]{:S(2)}) collective-permute-start(f32[3,1024]{1,0:T(4,128)S(1)} %slice.295), channel_id=1, source_target_pairs={{1,0},{2,1},{3,2},{4,3},{5,4},{6,5},{7,6},{8,7},{9,8},{10,9},{11,1... | collective-permute-start | bytes 36872 | tf_op jit(solution)/shard_map/ppermute | solution.py:26
  303.0 50.1 %collective-permute-start.8 = (f32[3,1024]{1,0:T(4,128)S(1)}, f32[3,1024]{1,0:T(4,128)S(1)}, u32[]{:S(2)}, u32[]{:S(2)}) collective-permute-start(f32[3,1024]{1,0:T(4,128)S(1)} %slice.306), channel_id=1, source_target_pairs={{1,0},{2,1},{3,2},{4,3},{5,4},{6,5},{7,6},{8,7},{9,8},{10,9},{11,1... | collective-permute-start | bytes 36872 | tf_op jit(solution)/shard_map/ppermute | solution.py:26
  320.4 39.0 %collective-permute-start.9 = (f32[3,1024]{1,0:T(4,128)S(1)}, f32[3,1024]{1,0:T(4,128)S(1)}, u32[]{:S(2)}, u32[]{:S(2)}) collective-permute-start(f32[3,1024]{1,0:T(4,128)S(1)} %slice.310), channel_id=1, source_target_pairs={{0,1},{1,2},{2,3},{3,4},{4,5},{5,6},{6,7},{7,8},{8,9},{9,10},{10,1... | collective-permute-start | bytes 36872 | tf_op jit(solution)/shard_map/ppermute | solution.py:24
  349.1 139.5 %collective-permute-start = (f32[19,4096]{1,0:T(8,128)}, f32[19,4096]{1,0:T(8,128)}, u32[]{:S(2)}, u32[]{:S(2)}) collective-permute-start(f32[19,4096]{1,0:T(8,128)} %bitcast.126), channel_id=1, source_target_pairs={{0,1},{1,2},{2,3},{3,4},{4,5},{5,6},{6,7},{7,8},{8,9},{9,10},{10,1... | collective-permute-start | bytes 933896 | tf_op jit(solution)/shard_map/ppermute | solution.py:24
  353.1 32.7 %collective-permute-start.30 = (f32[1,1024]{1,0:T(1,128)}, f32[1,1024]{1,0:T(1,128)}, u32[]{:S(2)}, u32[]{:S(2)}) collective-permute-start(f32[1,1024]{1,0:T(1,128)} %reshape.1101), channel_id=1, source_target_pairs={{24,0},{25,1},{26,2},{27,3},{28,4},{29,5},{30,6},{31,7},{32,8},{33... | collective-permute-start | bytes 12296 | tf_op jit(solution)/shard_map/ppermute | solution.py:36
  359.4 29.7 %collective-permute-start.31 = (f32[1,1024]{1,0:T(1,128)}, f32[1,1024]{1,0:T(1,128)}, u32[]{:S(2)}, u32[]{:S(2)}) collective-permute-start(f32[1,1024]{1,0:T(1,128)} %reshape.1101), channel_id=1, source_target_pairs={{488,0},{489,1},{490,2},{491,3},{492,4},{493,5},{494,6},{495,7},{4... | collective-permute-start | bytes 12296 | tf_op jit(solution)/shard_map/ppermute | solution.py:36
  389.1 28.1 %collective-permute-start.35 = (f32[1,1024]{1,0:T(1,128)S(1)}, f32[1,1024]{1,0:T(1,128)S(1)}, u32[]{:S(2)}, u32[]{:S(2)}) collective-permute-start(f32[1,1024]{1,0:T(1,128)S(1)} %reshape.1107), channel_id=1, source_target_pairs={{48,0},{49,1},{50,2},{51,3},{52,4},{53,5},{54,6},{55,7},{56,8},{57... | collective-permute-start | bytes 12296 | tf_op jit(solution)/shard_map/ppermute | solution.py:36
  448.9 29.3 %collective-permute-start.46 = (f32[1,1024]{1,0:T(1,128)S(1)}, f32[1,1024]{1,0:T(1,128)S(1)}, u32[]{:S(2)}, u32[]{:S(2)}) collective-permute-start(f32[1,1024]{1,0:T(1,128)S(1)} %reshape.1119), channel_id=1, source_target_pairs={{320,0},{321,1},{322,2},{323,3},{324,4},{325,5},{326,6},{327,7},{3... | collective-permute-start | bytes 12296 | tf_op jit(solution)/shard_map/ppermute | solution.py:36
  (55 other events, 1770.3 us)
Sparse Core Ops, SparseCore 0:
  106.2 2.7 sort.21.cloned.1.call-done
  (1 shorter events, 0.0 us)
where the time goes:
time: 627 us; the launch traced here: 620 us
  starting transfers between devices  271 us (43%)
  local copies, waits for them, and re-layouts  202 us (32%)
  matrix products  78 us (12%)
  other arithmetic  45.5 us (7%)
  between operations  15.3 us (2%)
  loops' own time  6.38 us (1%)
    ppermute x32, starting transfers between devices, from_behind(): return lax.ppermute(block, axis, route)  186 us
    gather x4, local copies, waits for them, and re-layouts, to_tree(): return jnp.take_along_axis(shaped, permuted_ids[None], axis=2)  108 us
    ppermute x5, starting transfers between devices, padded(): lax.ppermute(head, axis, [((i + 1) % count, i) for i in range(count)])  50 us
    gather x1, local copies, waits for them, and re-layouts, local(): restored = jnp.take_along_axis(tree_total, inverse_ids[None], axis=2)  44.4 us
    dot_general x8, matrix products, near_group(): jnp.einsum('gkij,gkrj->rgi', kernel, sources[:, :, 3:, :], precision=HIGH...  34.6 us
    dot_general x48, matrix products, combine(): jnp.einsum('nrb,ab->nra', candidates[slot_id], blocks[slot_id], precision...  32 us
    ppermute x6, starting transfers between devices, from_partner(): return lax.ppermute(value, axis, pairs)  22.1 us
    ppermute x28, other arithmetic, from_behind(): return lax.ppermute(block, axis, route)  20.2 us
  transfers between devices with their start and end apart: 48, of which 1 were waited for; matrix products, arithmetic and copies ran while one was open for 25% of the time, Pallas kernels for 0%

commit v1 on v0

v1 whole, which is shorter than its diff:
```python
import math

import jax
import jax.numpy as jnp
import numpy as np
from jax import lax
from jax.experimental import pallas as pl
from jax.experimental.pallas import tpu as pltpu
from jax.sharding import PartitionSpec as P

ORDER = 4
OFFSETS = (2, 3, -3, -2)
DELTA = 0.05
PROXY = 0.35
HIGHEST = lax.Precision.HIGHEST
GROUP = 16
LANES = 128
VMEM_BYTES = 50 * 1024 * 1024


def coupling_stack():
    nodes = np.cos((2.0 * np.arange(ORDER) + 1.0) * (math.pi / (2.0 * ORDER)))
    grid = np.stack(np.meshgrid(nodes, nodes, nodes, indexing="ij")).reshape(3, -1) * PROXY
    stacked = []
    for shift_by in OFFSETS:
        moved = grid + np.array([float(shift_by), 0.0, 0.0])[:, None]
        difference = grid[:, :, None] - moved[:, None, :]
        stacked.append((0.25 / math.pi / np.sqrt((difference**2).sum(0))).T)
    table = np.concatenate(stacked, axis=0)
    return np.concatenate([table, table], axis=1).astype(np.float32)


def dot(left, right):
    return lax.dot_general(
        left, right, (((1,), (0,)), ((), ())), precision=HIGHEST, preferred_element_type=jnp.float32
    )


def dot_t(left, right):
    return lax.dot_general(
        left, right, (((1,), (1,)), ((), ())), precision=HIGHEST, preferred_element_type=jnp.float32
    )


def first_half(shape):
    return lax.broadcasted_iota(jnp.int32, shape, len(shape) - 1) < LANES // 2


def packed(left, right):
    return jnp.where(first_half(left.shape), left, right)


def unpacked(both):
    turned = pltpu.roll(both, LANES // 2, 1)
    return packed(both, turned), packed(turned, both)


def twice(matrix):
    return jnp.concatenate([matrix, matrix], axis=1)


def up_matrix(transfer_ref):
    return jnp.concatenate([twice(transfer_ref[0]), twice(transfer_ref[1])], axis=0)


def up(values, matrix):
    count, rows, lanes = values.shape
    paired = values.reshape(count // 2, 2, rows, lanes)
    both = packed(paired[:, 0], paired[:, 1]).reshape(count // 2 * rows, lanes)
    return dot(both, matrix).reshape(count // 2, rows, lanes)


def down(parents, transfer_ref, half):
    count, rows, lanes = parents.shape
    matrix = transfer_ref[half]
    doubled = jnp.concatenate([matrix, matrix], axis=0)
    flat = parents.reshape(count * rows, lanes)[:, : lanes // 2]
    return dot_t(flat, doubled).reshape(count, rows, lanes)


def down_all(parents, transfer_ref):
    count, rows, lanes = parents.shape
    children = jnp.stack(
        [down(parents, transfer_ref, 0), down(parents, transfer_ref, 1)], axis=1
    )
    return children.reshape(2 * count, rows, lanes)


def level_starts(total_leaves, levels):
    return [2 * total_leaves - 2 * (total_leaves >> level) for level in range(levels)]


def prepare_kernel(
    total_leaves,
    levels,
    dev_ref,
    points_ref,
    charges_ref,
    basis_ref,
    ordering_ref,
    transfer_ref,
    coupling_ref,
    pay_right_ref,
    pay_left_ref,
    message_ref,
    local_ref,
    counts_ref,
    inverse_ref,
):
    device = dev_ref[0]
    rhs = charges_ref.shape[0]
    leaves = ordering_ref.shape[0]
    data_rows = pay_right_ref.shape[0] - 12 * rhs
    block = data_rows // leaves
    filler = jnp.zeros((block - rhs - 3, LANES), jnp.float32)
    for leaf in range(leaves):
        cols = slice(leaf * LANES, (leaf + 1) * LANES)
        rows = slice(leaf * block, (leaf + 1) * block)
        value = jnp.concatenate([charges_ref[:, cols], points_ref[:, cols], filler], axis=0)
        pay_right_ref[rows, :] = value
        pay_left_ref[rows, :] = value
    zero = jnp.zeros((rhs, LANES), jnp.float32)
    expansions = []
    for pair in range(leaves // 2):
        gathered = []
        for leaf in (2 * pair, 2 * pair + 1):
            ids = jnp.broadcast_to(ordering_ref[leaf : leaf + 1, :], (rhs, LANES))
            cols = slice(leaf * LANES, (leaf + 1) * LANES)
            gathered.append(jnp.take_along_axis(charges_ref[:, cols], ids, axis=1))
        left = jnp.concatenate(
            [
                jnp.concatenate([gathered[0], zero], axis=1),
                jnp.concatenate([zero, gathered[1]], axis=1),
            ],
            axis=0,
        )
        part = basis_ref[:, 2 * pair * LANES : (2 * pair + 2) * LANES]
        both = dot_t(left, jnp.concatenate([part, part], axis=0))
        expansions.append(both.reshape(2, rhs, LANES))
    current = jnp.concatenate(expansions, axis=0)
    matrix = up_matrix(transfer_ref)
    base = 0
    edge = data_rows
    for level in range(4):
        count = leaves >> level
        local_ref[base : base + count * rhs, :] = current.reshape(count * rhs, LANES)
        pay_right_ref[edge : edge + 3 * rhs, :] = current[count - 3 :].reshape(3 * rhs, LANES)
        pay_left_ref[edge : edge + 3 * rhs, :] = current[:3].reshape(3 * rhs, LANES)
        base += count * rhs
        edge += 3 * rhs
        current = up(current, matrix)
    message = packed(current[0], current[1])
    for peer in range(message_ref.shape[0] // rhs):
        message_ref[peer * rhs : (peer + 1) * rhs, :] = message
    lane = lax.broadcasted_iota(jnp.int32, (1, LANES), 1)
    starts = level_starts(total_leaves, levels)
    last = starts[-1] // LANES * LANES
    width = coupling_ref.shape[1] - last
    for level in range(levels):
        clusters = total_leaves >> level
        if starts[level] >= last:
            ids = jnp.concatenate(
                [
                    coupling_ref[:, last : last + width],
                    jnp.zeros((coupling_ref.shape[0], LANES - width), jnp.int32),
                ],
                axis=1,
            )
            targets = lane + (last - starts[level])
        else:
            count = leaves >> level if level < 4 else 2 * GROUP >> (level - 4)
            unit = device if level < 4 else device // GROUP
            tile = unit * count // LANES
            ids = coupling_ref[
                :, pl.ds(pl.multiple_of(starts[level] + tile * LANES, LANES), LANES)
            ]
            targets = lane + tile * LANES
        relative = (ids - targets) & (clusters - 1)
        for slot, shift_by in enumerate(OFFSETS):
            hits = jnp.where(relative == (shift_by & (clusters - 1)), 0.5**level, 0.0)
            counts_ref[4 * level + slot : 4 * level + slot + 1, :] = jnp.sum(
                hits, axis=0, keepdims=True
            )
    slots = lax.broadcasted_iota(jnp.int32, (LANES, LANES), 0)
    numbers = lax.broadcasted_iota(jnp.int32, (8, LANES), 1).astype(jnp.float32)
    numbers = numbers.astype(jnp.bfloat16)
    for leaf in range(leaves):
        hit = jnp.where(ordering_ref[leaf : leaf + 1, :] == slots, 1.0, 0.0).astype(jnp.bfloat16)
        found = lax.dot_general(
            numbers, hit, (((1,), (1,)), ((), ())), preferred_element_type=jnp.float32
        )
        inverse_ref[leaf : leaf + 1, :] = found[0:1].astype(jnp.int32)


def near_kernel(
    total_leaves,
    first,
    dev_ref,
    near_ref,
    own_ref,
    before_ref,
    after_ref,
    *rest,
):
    out_ref, places, weights = rest[-3:]
    rhs = out_ref.shape[0]
    leaves = near_ref.shape[1]
    entries = near_ref.shape[0]
    targets = out_ref.shape[1] // LANES
    block = (own_ref.shape[0] - 12 * rhs) // leaves
    for part, ref in enumerate((before_ref, own_ref, after_ref)):

        def fill(leaf, carry, part=part, ref=ref):
            rows = pl.multiple_of(leaf * block, 8)
            charge = ref[pl.ds(rows, rhs), :] * (0.25 / math.pi)
            high = charge.astype(jnp.bfloat16)
            low = (charge - high.astype(jnp.float32)).astype(jnp.bfloat16)
            weights[part * leaves + leaf, 0:rhs, :] = high
            weights[part * leaves + leaf, rhs : 2 * rhs, :] = low
            places[part * leaves + leaf, :, :] = ref[pl.ds(rows + rhs, 8), :]
            return carry

        lax.fori_loop(0, leaves, fill, 0, unroll=4)

    device = dev_ref[0]
    half_cycle = total_leaves // 2

    def one(step, carry):
        leaf = step + first
        target = device * leaves + leaf
        columns = jnp.transpose(places[leaves + leaf, :, :])
        axes = [
            jnp.broadcast_to(columns[:, axis : axis + 1], (LANES, LANES)) for axis in range(3)
        ]
        total = jnp.zeros((LANES, 2 * rhs), jnp.float32)
        for pair in range(entries // 2):
            highs, lows, sides = [], [], []
            for entry in (2 * pair, 2 * pair + 1):
                window = (
                    (near_ref[entry, leaf] - target + half_cycle) & (total_leaves - 1)
                ) - half_cycle
                source = leaves + leaf + window
                shift = window.astype(jnp.float32) * (1.0 / leaves)
                place = places[source, :, :]
                dx = axes[0] - (place[0:1, :] + shift)
                dy = axes[1] - place[1:2, :]
                dz = axes[2] - place[2:3, :]
                value = lax.rsqrt(dx * dx + dy * dy + (dz * dz + DELTA * DELTA))
                high = value.astype(jnp.bfloat16)
                highs.append(high)
                lows.append((value - high.astype(jnp.float32)).astype(jnp.bfloat16))
                sides.append(weights[source, :, :])
            side = jnp.concatenate(sides, axis=1)
            for piece in (jnp.concatenate(highs, axis=1), jnp.concatenate(lows, axis=1)):
                total = total + lax.dot_general(
                    piece, side, (((1,), (1,)), ((), ())), preferred_element_type=jnp.float32
                )
        turned = jnp.transpose(total)
        out_ref[:, pl.ds(pl.multiple_of(step * LANES, LANES), LANES)] = (
            turned[0:rhs, :] + turned[rhs : 2 * rhs, :]
        )
        return carry

    lax.fori_loop(0, targets, one, 0)


def couple(window, count, level, lane0, counts_ref, x_ref, row0, rows):
    for t in range(count):
        parts = [
            window(t + shift_by, slot) * counts_ref[4 * level + slot, lane0 + t]
            for slot, shift_by in enumerate(OFFSETS)
        ]
        where = slice(row0 + t * rows, row0 + (t + 1) * rows)
        x_ref[where, 0:LANES] = packed(parts[0], parts[1])
        x_ref[where, LANES : 2 * LANES] = packed(parts[2], parts[3])


def local_kernel(
    dev_ref, counts_ref, local_ref, before_ref, after_ref, stack_ref, out_ref, x_ref
):
    device = dev_ref[0]
    rhs = (before_ref.shape[0] - local_ref.shape[0] // 60 * 48) // 12
    rhs = local_ref.shape[0] // 60
    edge = before_ref.shape[0] - 12 * rhs
    base = 0
    for level in range(4):
        count = 32 >> level

        def window(t, slot, count=count, base=base, edge=edge):
            if t < 0:
                return before_ref[edge + (t + 3) * rhs : edge + (t + 4) * rhs, :]
            if t >= count:
                return after_ref[edge + (t - count) * rhs : edge + (t - count + 1) * rhs, :]
            return local_ref[base + t * rhs : base + (t + 1) * rhs, :]

        lane0 = (device * count) & (LANES - 1)
        couple(window, count, level, lane0, counts_ref, x_ref, base, rhs)
        base += count * rhs
        edge += 3 * rhs
    out_ref[...] = dot(x_ref[...], stack_ref[...])


def upper_kernel(
    total_leaves,
    dev_ref,
    counts_ref,
    gathered_ref,
    transfer_ref,
    stack_ref,
    out_ref,
    x_ref,
    top_ref,
    *sparse,
):
    device = dev_ref[0]
    index = device % GROUP
    group = device // GROUP
    rhs = out_ref.shape[0] // GROUP
    groups = gathered_ref.shape[0] // rhs
    bits = [(index >> bit) & 1 for bit in range(4)]
    matrix = up_matrix(transfer_ref)
    half = LANES // 2

    path = dot(dot(transfer_ref[bits[0]], transfer_ref[bits[1]]),
               dot(transfer_ref[bits[2]], transfer_ref[bits[3]]))
    whole = dot(matrix[:, :half], twice(path))
    level9 = dot(gathered_ref[...], whole).reshape(groups, rhs, LANES)
    level10 = up(level9, matrix)
    level11 = up(level10, matrix)
    top_ref[0:groups] = level9
    top_ref[groups : groups + groups // 2] = level10
    top_ref[groups + groups // 2 : groups + groups // 2 + groups // 4] = level11

    beside = [
        gathered_ref[pl.ds(pl.multiple_of(((group + step) & (groups - 1)) * rhs, 8), rhs), :]
        for step in range(-2, 3)
    ]
    for ref in sparse:
        ref[...] = jnp.zeros(ref.shape, jnp.float32)

    def place(ref, count, position, value):
        inside = (position >= -3) & (position < count + 3)
        ref[jnp.where(inside, position + 3, count + 6)] = value

    for step in (-1, 0, 1):
        for side, value in enumerate(unpacked(beside[step + 2])):
            place(sparse[0], 2 * GROUP, step * 2 * GROUP + 2 * index + side, value)
    current = dot(jnp.concatenate(beside, axis=0), matrix)
    for level in range(5, 9):
        count = 2 * GROUP >> (level - 4)
        reach = (-1, 0, 1) if count >= 3 else (-2, -1, 0, 1, 2)
        for step in reach:
            place(
                sparse[level - 4],
                count,
                step * count + (index >> (level - 5)),
                current[(step + 2) * rhs : (step + 3) * rhs],
            )
        if level < 8:
            current = dot(current[:, :half], twice(transfer_ref[bits[level - 5]]))

    row0 = 0
    spans = []
    for level in range(4, 9):
        count = 2 * GROUP >> (level - 4)
        ref = sparse[level - 4]
        lane0 = (group * count) & (LANES - 1)
        couple(
            lambda t, slot, ref=ref: ref[t + 3], count, level, lane0, counts_ref, x_ref, row0, rhs
        )
        spans.append((row0, count))
        row0 += count * rhs
    lane_base = LANES // 2
    top_base = 0
    for level in range(9, 12):
        clusters = groups >> (level - 9)
        cluster = group >> (level - 9)
        couple(
            lambda t, slot: top_ref[top_base + ((cluster + t) & (clusters - 1))],
            1,
            level,
            lane_base + cluster,
            counts_ref,
            x_ref,
            row0,
            rhs,
        )
        spans.append((row0, 1))
        row0 += rhs
        lane_base += clusters
        top_base += clusters
    terms = dot(x_ref[...], stack_ref[...])

    def term(level):
        start, count = spans[level - 4]
        return terms[start : start + count * rhs].reshape(count, rhs, LANES)

    current = term(11)
    for level in (10, 9):
        current = term(level) + down(current, transfer_ref, (group >> (level - 9)) & 1)
    for level in (8, 7, 6, 5, 4):
        current = term(level) + down_all(current, transfer_ref)
    paired = current.reshape(GROUP, 2, rhs, LANES)
    out_ref[...] = packed(paired[:, 0], paired[:, 1]).reshape(GROUP * rhs, LANES)


def final_kernel(
    parts_ref, terms_ref, transfer_ref, basis_ref, inverse_ref, near_a_ref, near_b_ref, out_ref
):
    rhs = out_ref.shape[0]
    leaves = inverse_ref.shape[0]
    total = parts_ref[0:rhs, :]
    for sender in range(1, GROUP):
        total = total + parts_ref[sender * rhs : (sender + 1) * rhs, :]
    left, right = unpacked(total)
    current = jnp.stack([left, right])
    base = terms_ref.shape[0]
    for level in (3, 2, 1, 0):
        count = leaves >> level
        base -= count * rhs
        mine = terms_ref[base : base + count * rhs, :].reshape(count, rhs, LANES)
        current = mine + down_all(current, transfer_ref)
    lane = lax.broadcasted_iota(jnp.int32, (rhs, LANES), 1)
    low = lane < LANES // 2
    zero = jnp.zeros((rhs, LANES), jnp.float32)
    for four in range(leaves // 4):
        rows, sides = [], []
        for slot in range(4):
            leaf = 4 * four + slot
            value = jnp.where(low if slot % 2 == 0 else ~low, current[leaf], 0.0)
            rows.append(jnp.concatenate([value, zero] if slot < 2 else [zero, value], axis=1))
            sides.append(basis_ref[:, leaf * LANES : (leaf + 1) * LANES])
        far = dot(jnp.concatenate(rows, axis=0), jnp.concatenate(sides, axis=0))
        for slot in range(4):
            leaf = 4 * four + slot
            ids = jnp.broadcast_to(inverse_ref[leaf : leaf + 1, :], (rhs, LANES))
            value = jnp.take_along_axis(far[slot * rhs : (slot + 1) * rhs], ids, axis=1)
            near_ref = near_a_ref if leaf < leaves // 2 else near_b_ref
            at = leaf % (leaves // 2) * LANES
            out_ref[:, leaf * LANES : (leaf + 1) * LANES] = value + near_ref[:, at : at + LANES]


def call(kernel, outs, scalars, operands, scratch=(), cost=None):
    smem = pl.BlockSpec(memory_space=pltpu.SMEM)
    vmem = pl.BlockSpec(memory_space=pltpu.VMEM)
    return pl.pallas_call(
        kernel,
        out_shape=outs,
        in_specs=[smem] * len(scalars) + [vmem] * len(operands),
        out_specs=jax.tree.map(lambda _: vmem, outs),
        scratch_shapes=list(scratch),
        cost_estimate=cost,
        compiler_params=pltpu.CompilerParams(vmem_limit_bytes=VMEM_BYTES),
    )(*scalars, *operands)


def local(points, charges, basis, transfer, near_list, coupling_list, ordering):
    devices = lax.axis_size("leaf")
    device = jnp.reshape(lax.axis_index("leaf"), (1,)).astype(jnp.int32)
    leaves = near_list.shape[1]
    rhs = charges.shape[0]
    total_leaves = leaves * devices
    levels = total_leaves.bit_length() - 3
    groups = devices // GROUP
    f32 = jnp.float32
    ids = ordering.reshape(leaves, LANES)
    stack = jnp.asarray(coupling_stack())
    pay_rows = leaves * 24 + 12 * rhs
    local_rows = (leaves * 2 - 4) * rhs

    pay_right, pay_left, message, local_terms, counts, inverse = call(
        lambda *refs: prepare_kernel(total_leaves, levels, *refs),
        [
            jax.ShapeDtypeStruct((pay_rows, LANES), f32),
            jax.ShapeDtypeStruct((pay_rows, LANES), f32),
            jax.ShapeDtypeStruct((groups * rhs, LANES), f32),
            jax.ShapeDtypeStruct((local_rows, LANES), f32),
            jax.ShapeDtypeStruct((4 * levels, LANES), f32),
            jax.ShapeDtypeStruct((leaves, LANES), jnp.int32),
        ],
        [device],
        [points, charges, basis, ids, transfer, coupling_list],
    )
    before = lax.ppermute(pay_right, "leaf", [(i, (i + 1) % devices) for i in range(devices)])
    after = lax.ppermute(pay_left, "leaf", [((i + 1) % devices, i) for i in range(devices)])
    gathered = lax.all_to_all(
        message,
        "leaf",
        0,
        0,
        axis_index_groups=[[g * GROUP + i for g in range(groups)] for i in range(GROUP)],
        tiled=True,
    )

    def near(first, count, extra):
        return call(
            lambda *refs: near_kernel(total_leaves, first, *refs),
            jax.ShapeDtypeStruct((rhs, count * LANES), f32),
            [device, near_list],
            [pay_right, before, after, *extra],
            [
                pltpu.VMEM((3 * leaves, 8, LANES), f32),
                pltpu.VMEM((3 * leaves, 2 * rhs, LANES), jnp.bfloat16),
            ],
            pl.CostEstimate(
                flops=count * 12 * 128 * 128 * 100,
                bytes_accessed=8 << 20,
                transcendentals=count * 12 * 128 * 128,
            ),
        )

    near_a = near(0, leaves // 2, [])
    terms = call(
        local_kernel,
        jax.ShapeDtypeStruct((local_rows, LANES), f32),
        [device, counts],
        [local_terms, before, after, stack],
        [pltpu.VMEM((local_rows, 2 * LANES), f32)],
    )
    upper_rows = (4 * GROUP - 2 + 3) * rhs
    spread = call(
        lambda *refs: upper_kernel(total_leaves, *refs),
        jax.ShapeDtypeStruct((GROUP * rhs, LANES), f32),
        [device, counts],
        [gathered, transfer, stack],
        [
            pltpu.VMEM((upper_rows, 2 * LANES), f32),
            pltpu.VMEM((2 * groups, rhs, LANES), f32),
            *[
                pltpu.VMEM(((2 * GROUP >> step) + 7, rhs, LANES), f32)
                for step in range(5)
            ],
        ],
    )
    parts = lax.all_to_all(
        spread,
        "leaf",
        0,
        0,
        axis_index_groups=[[g * GROUP + i for i in range(GROUP)] for g in range(groups)],
        tiled=True,
    )
    near_b = near(leaves // 2, leaves // 2, [spread])
    return call(
        final_kernel,
        jax.ShapeDtypeStruct(charges.shape, f32),
        [],
        [parts, terms, transfer, basis, inverse, near_a, near_b],
    )


def solution(mesh):
    placed = (
        P(None, "leaf"),
        P(None, "leaf"),
        P(None, "leaf"),
        P(),
        P(None, "leaf"),
        P(),
        P("leaf"),
    )
    return jax.shard_map(
        local, mesh=mesh, in_specs=placed, out_specs=P(None, "leaf"), check_vma=False
    )
```

time: 627 us -> 84.1 us (0.13); the launches traced: 620 us -> 83.5 us
  starting transfers between devices: 271 us -> 31.2 us
  local copies, waits for them, and re-layouts: 202 us -> 5.63 us
  matrix products: 78 us -> 0 us
  other arithmetic: 45.5 us -> 0 us
  Pallas kernels: 0 us -> 40.4 us
  between operations: 15.3 us -> 0.08 us
  loops' own time: 6.38 us -> 0 us
    ppermute x48 -> x2, starting transfers between devices: 271 us -> 5.89 us  [the longest x1 3.96 us: local(): lax.ppermute(pay_right, 'leaf', [(i, (i + 1) % devices) for i in range(de...]
    gather x29 -> x0, local copies, waits for them, and re-layouts: 174 us -> none  [the longest x4 108 us: to_tree(): return jnp.take_along_axis(shaped, permuted_ids[None], axis=2)]
    dot_general x102 -> x0, matrix products: 78 us -> none  [the longest x8 34.6 us: near_group(): jnp.einsum('gkij,gkrj->rgi', kernel, sources[:, :, 3:, :], precision=HIGH...]
    pallas_call x0 -> x6, Pallas kernels: none -> 40.4 us  [call(): pl.pallas_call(kernel, out_shape=outs, in_specs=[smem] * len(scalars) + [...]
    all_to_all x0 -> x2, starting transfers between devices: none -> 25.3 us  [the longest x1 16.6 us: local(): lax.all_to_all(message, 'leaf', 0, 0, axis_index_groups=[[g * GROUP + i f...]
    ppermute x34 -> x0, other arithmetic: 24.1 us -> none  [the longest x28 20.2 us: from_behind(): return lax.ppermute(block, axis, route)]
    reduce_sum x13 -> x0, other arithmetic: 11.1 us -> none  [the longest x12 11 us: offset_counts(): jnp.sum((relative == shift_by % clusters).astype(jnp.float32), axis=0)]
    reshape x39 -> x0, local copies, waits for them, and re-layouts: 9.37 us -> none  [the longest x20 6.04 us: neighbour_blocks(): return [piece.reshape(count, rhs_count, rank_count) for piece in pieces]]
  transfers between devices with their start and end apart: 48 -> 4, of which waited for: 1 -> 1; matrix products, arithmetic and copies ran while one was open for 25% -> 0% of each run, Pallas kernels for 0% -> 41%
where the time goes in v1:
time: 84.1 us; the launch traced here: 83.5 us
  Pallas kernels  40.4 us (48%)
  starting transfers between devices  31.2 us (37%)
  waiting for transfers between devices  6.21 us (7%)
  local copies, waits for them, and re-layouts  5.63 us (7%)
    pallas_call x6, Pallas kernels, call(): pl.pallas_call(kernel, out_shape=outs, in_specs=[smem] * len(scalars) + [...  40.4 us
    all_to_all x1, starting transfers between devices, local(): lax.all_to_all(message, 'leaf', 0, 0, axis_index_groups=[[g * GROUP + i f...  16.6 us
    all_to_all x1, starting transfers between devices, local(): lax.all_to_all(spread, 'leaf', 0, 0, axis_index_groups=[[g * GROUP + i fo...  8.71 us
    all_to_all x1, waiting for transfers between devices, local(): lax.all_to_all(message, 'leaf', 0, 0, axis_index_groups=[[g * GROUP + i f...  6.2 us
    unnamed x20, local copies, waits for them, and re-layouts  5.63 us
    ppermute x1, starting transfers between devices, local(): lax.ppermute(pay_right, 'leaf', [(i, (i + 1) % devices) for i in range(de...  3.96 us
    ppermute x1, starting transfers between devices, local(): lax.ppermute(pay_left, 'leaf', [((i + 1) % devices, i) for i in range(dev...  1.92 us
  transfers between devices with their start and end apart: 4, of which 1 were waited for; matrix products, arithmetic and copies ran while one was open for 0% of the time, Pallas kernels for 41%

profile of v1, /device:TPU:1, one launch (start us, length us, event | category | flops | bytes accessed | tf_op | source)
XLA Modules:
  0.0 83.5 jit_solution(1925658696286917329)
XLA Ops:
  0.0 1.2 %copy-done = f32[64,4096]{1,0:T(8,128)S(1)} copy-done((f32[64,4096]{1,0:T(8,128)S(1)}, f32[64,4096]{1,0:T(8,128)}, u32[]{:S(2)}) %copy-start) | copy-done | bytes 1048600
  1.2 0.8 %copy-done.2 = f32[2,64,64]{2,1,0:T(8,128)S(1)} copy-done((f32[2,64,64]{2,1,0:T(8,128)S(1)}, f32[2,64,64]{2,1,0:T(8,128)}, u32[]{:S(2)}) %copy-start.2) | copy-done | bytes 32792
  2.1 1.0 %copy-done.4 = s32[4,32760]{1,0:T(4,128)S(1)} copy-done((s32[4,32760]{1,0:T(4,128)S(1)}, s32[4,32760]{1,0:T(4,128)}, u32[]{:S(2)}) %copy-start.4) | copy-done | bytes 524184
  3.1 0.9 %copy-done.6 = f32[16,4096]{1,0:T(8,128)S(1)} copy-done((f32[16,4096]{1,0:T(8,128)S(1)}, f32[16,4096]{1,0:T(8,128)}, u32[]{:S(2)}) %copy-start.6) | copy-done | bytes 262168
  4.1 0.8 %copy-done.7 = f32[3,4096]{1,0:T(4,128)S(1)} copy-done((f32[3,4096]{1,0:T(4,128)S(1)}, f32[3,4096]{1,0:T(4,128)}, u32[]{:S(2)}) %copy-start.7) | copy-done | bytes 49176
  4.9 0.7 copy-done.8
  5.6 3.6 %shard_map.82 = (f32[960,128]{1,0:T(8,128)S(1)}, f32[960,128]{1,0:T(8,128)S(1)}, f32[512,128]{1,0:T(8,128)}, f32[960,128]{1,0:T(8,128)S(1)}, f32[48,128]{1,0:T(8,128)S(1)}, /*index=5*/s32[32,128]{1,0:T(8,128)S(1)}) custom-call(s32[1]{0:T(128)} %bitcast.refs_0_.dev_ref, f32[3,4096]{1,0:T(4,128)S(1)} %copy-done.7, f32[16,4096]{1,0:T(8,128)S(1)} %copy-done.6, ...), custom_call_target="tpu_custom_call" | custom-call | tf_op jit(solution)/shard_map/pallas_call | solution.py:446
  9.2 16.6 %all-to-all-start = ((f32[32,16,128]{2,1,0:T(8,128)}), f32[32,16,128]{2,1,0:T(8,128)S(1)}, u32[]{:S(2)}, u32[]{:S(2)}) async-start(f32[32,16,128]{2,1,0:T(8,128)} %bitcast.2), calls=%async_computation | async-start | bytes 524288 | tf_op jit(solution)/shard_map/all_to_all | solution.py:486
  25.9 4.0 %collective-permute-start = (f32[960,128]{1,0:T(8,128)S(1)}, f32[960,128]{1,0:T(8,128)S(1)}, u32[]{:S(2)}, u32[]{:S(2)}) collective-permute-start(f32[960,128]{1,0:T(8,128)S(1)} %get-tuple-element.14.refs_2_), channel_id=1, source_target_pairs={{0,1},{1,2},{2,3},{3,4},{4,5},{5,6},{6,7},{7,8},{8,9},{9,10},{10,1... | collective-permute-start | bytes 1474568 | tf_op jit(solution)/shard_map/ppermute | solution.py:484
  29.8 1.9 %collective-permute-start.1 = (f32[960,128]{1,0:T(8,128)S(1)}, f32[960,128]{1,0:T(8,128)S(1)}, u32[]{:S(2)}, u32[]{:S(2)}) collective-permute-start(f32[960,128]{1,0:T(8,128)S(1)} %get-tuple-element.15), channel_id=1, source_target_pairs={{1,0},{2,1},{3,2},{4,3},{5,4},{6,5},{7,6},{8,7},{9,8},{10,9},{11,1... | collective-permute-start | bytes 1474568 | tf_op jit(solution)/shard_map/ppermute | solution.py:485
  31.8 6.2 %all-to-all-done = f32[32,16,128]{2,1,0:T(8,128)S(1)} async-done(((f32[32,16,128]{2,1,0:T(8,128)}), f32[32,16,128]{2,1,0:T(8,128)S(1)}, u32[]{:S(2)}, u32[]{:S(2)}) %all-to-all-start) | async-done | bytes 262176 | tf_op jit(solution)/shard_map/all_to_all | solution.py:486
  38.0 0.0 copy-done.3
  38.0 8.1 %shard_map.83.refs_5_ = f32[256,128]{1,0:T(8,128)} custom-call(s32[1]{0:T(128)} %bitcast.refs_0_.dev_ref, f32[48,128]{1,0:T(8,128)S(1)} %get-tuple-element.11.refs_1_.counts_ref, f32[512,128]{1,0:T(8,128)S(1)} %bitcast.6, f32[2,64,64]{2,1,0:T(8,128)S(1)} %copy-done.3, f32[256,128]{1,0:T(8,128)S(1)} %copy-done.5), custom_call_target="tpu_custom_call" | custom-call | tf_op jit(solution)/shard_map/pallas_call | solution.py:446
  46.1 8.7 %all-to-all-start.1 = ((f32[16,16,128]{2,1,0:T(8,128)}), f32[16,16,128]{2,1,0:T(8,128)S(1)}, u32[]{:S(2)}, u32[]{:S(2)}) async-start(f32[16,16,128]{2,1,0:T(8,128)} %bitcast.4), calls=%async_computation.1 | async-start | bytes 262144 | tf_op jit(solution)/shard_map/all_to_all | solution.py:535
  54.8 0.0 collective-permute-done.before_ref.refs_3_
  54.8 0.0 collective-permute-done.1.after_ref.refs_4_
  54.8 0.0 copy-start.9
  54.8 1.9 %shard_map.84.terms_ref = f32[960,128]{1,0:T(8,128)S(1)} custom-call(s32[1]{0:T(128)} %bitcast.refs_0_.dev_ref, f32[48,128]{1,0:T(8,128)S(1)} %get-tuple-element.11.refs_1_.counts_ref, f32[960,128]{1,0:T(8,128)S(1)} %get-tuple-element.13.local_ref, f32[960,128]{1,0:T(8,128)S(1)} %collective-permute-done.before_ref.refs_3_, ...), custom_call_target="tpu_custom_call" | custom-call | tf_op jit(solution)/shard_map/pallas_call | solution.py:446
  56.7 0.0 copy-done.9
  56.7 11.8 %shard_map.85.near_a_ref = f32[16,2048]{1,0:T(8,128)S(1)} custom-call(s32[1]{0:T(128)} %bitcast.refs_0_.dev_ref, s32[12,32]{1,0:T(8,128)S(1)} %copy-done.9, f32[960,128]{1,0:T(8,128)S(1)} %get-tuple-element.14.refs_2_, f32[960,128]{1,0:T(8,128)S(1)} %collective-permute-done.before_ref.refs_3_, f32[960,128]{1,0:T(8,128)S(1)} %collective-permute-done.1.after_ref.refs_4_), custom_call_target="tpu_custom_call" | custom-call | flops 314572800 | bytes 8388608 | tf_op jit(solution)/shard_map/pallas_call | solution.py:446
  68.6 12.1 %shard_map.86.near_b_ref = f32[16,2048]{1,0:T(8,128)S(1)} custom-call(s32[1]{0:T(128)} %bitcast.refs_0_.dev_ref, s32[12,32]{1,0:T(8,128)S(1)} %copy-done.9, f32[960,128]{1,0:T(8,128)S(1)} %get-tuple-element.14.refs_2_, f32[960,128]{1,0:T(8,128)S(1)} %collective-permute-done.before_ref.refs_3_, f32[960,128]{1,0:T(8,128)S(1)} %collective-permute-done.1.after_ref.refs_4_, ...), custom_call_target="tpu_custom_call" | custom-call | flops 314572800 | bytes 8388608 | tf_op jit(solution)/shard_map/pallas_call | solution.py:446
  80.7 0.0 all-to-all-done.1
  80.7 0.0 copy-done.1
  80.7 2.8 %shard_map.87 = f32[16,4096]{1,0:T(8,128)} custom-call(f32[256,128]{1,0:T(8,128)S(1)} %bitcast.7, f32[960,128]{1,0:T(8,128)S(1)} %shard_map.84.terms_ref, f32[2,64,64]{2,1,0:T(8,128)S(1)} %copy-done.3, f32[64,4096]{1,0:T(8,128)S(1)} %copy-done.1, s32[32,128]{1,0:T(8,128)S(1)} %get-tuple-element.16.inverse_ref, f32[16,2048]{1,0:T(8,128)S(1)} %shard_map.85.near_a_ref, ...), custom_call_target="tpu_custom_call" | custom-call | tf_op jit(solution)/shard_map/pallas_call | solution.py:446
  (10 shorter events, 0.0 us)
Async XLA Ops:
  0.0 1.2 %copy-start = (f32[64,4096]{1,0:T(8,128)S(1)}, f32[64,4096]{1,0:T(8,128)}, u32[]{:S(2)}) copy-start(f32[64,4096]{1,0:T(8,128)} %basis_ref.1) | copy-start | bytes 3145732
  1.2 0.8 %copy-start.2 = (f32[2,64,64]{2,1,0:T(8,128)S(1)}, f32[2,64,64]{2,1,0:T(8,128)}, u32[]{:S(2)}) copy-start(f32[2,64,64]{2,1,0:T(8,128)} %transfer_ref.1) | copy-start | bytes 98308
  2.1 1.0 %copy-start.4 = (s32[4,32760]{1,0:T(4,128)S(1)}, s32[4,32760]{1,0:T(4,128)}, u32[]{:S(2)}) copy-start(s32[4,32760]{1,0:T(4,128)} %refs_6_.1) | copy-start | bytes 1572484
  3.1 0.9 %copy-start.6 = (f32[16,4096]{1,0:T(8,128)S(1)}, f32[16,4096]{1,0:T(8,128)}, u32[]{:S(2)}) copy-start(f32[16,4096]{1,0:T(8,128)} %refs_2_.1) | copy-start | bytes 786436
  4.1 0.8 %copy-start.7 = (f32[3,4096]{1,0:T(4,128)S(1)}, f32[3,4096]{1,0:T(4,128)}, u32[]{:S(2)}) copy-start(f32[3,4096]{1,0:T(4,128)} %refs_1_.3) | copy-start | bytes 147460
  4.9 0.7 copy-start.8
  9.2 28.7 %copy-start.3 = (f32[2,64,64]{2,1,0:T(8,128)S(1)}, f32[2,64,64]{2,1,0:T(8,128)}, u32[]{:S(2)}) copy-start(f32[2,64,64]{2,1,0:T(8,128)} %transfer_ref.1) | copy-start | bytes 98308
  9.2 28.7 %copy-start.5 = (f32[256,128]{1,0:T(8,128)S(1)}, f32[256,128]{1,0:T(8,128)}, u32[]{:S(2)}) copy-start(f32[256,128]{1,0:T(8,128)} %constant.6.clone.refs_4_.stack_ref) | copy-start | bytes 393220
  9.2 28.7 %all-to-all-start = ((f32[32,16,128]{2,1,0:T(8,128)}), f32[32,16,128]{2,1,0:T(8,128)S(1)}, u32[]{:S(2)}, u32[]{:S(2)}) async-start(f32[32,16,128]{2,1,0:T(8,128)} %bitcast.2), calls=%async_computation | async-start | bytes 524288 | tf_op jit(solution)/shard_map/all_to_all | solution.py:486
  25.9 28.9 %collective-permute-start = (f32[960,128]{1,0:T(8,128)S(1)}, f32[960,128]{1,0:T(8,128)S(1)}, u32[]{:S(2)}, u32[]{:S(2)}) collective-permute-start(f32[960,128]{1,0:T(8,128)S(1)} %get-tuple-element.14.refs_2_), channel_id=1, source_target_pairs={{0,1},{1,2},{2,3},{3,4},{4,5},{5,6},{6,7},{7,8},{8,9},{9,10},{10,1... | collective-permute-start | bytes 1474568 | tf_op jit(solution)/shard_map/ppermute | solution.py:484
  29.8 25.0 %collective-permute-start.1 = (f32[960,128]{1,0:T(8,128)S(1)}, f32[960,128]{1,0:T(8,128)S(1)}, u32[]{:S(2)}, u32[]{:S(2)}) collective-permute-start(f32[960,128]{1,0:T(8,128)S(1)} %get-tuple-element.15), channel_id=1, source_target_pairs={{1,0},{2,1},{3,2},{4,3},{5,4},{6,5},{7,6},{8,7},{9,8},{10,9},{11,1... | collective-permute-start | bytes 1474568 | tf_op jit(solution)/shard_map/ppermute | solution.py:485
  46.1 34.6 %all-to-all-start.1 = ((f32[16,16,128]{2,1,0:T(8,128)}), f32[16,16,128]{2,1,0:T(8,128)S(1)}, u32[]{:S(2)}, u32[]{:S(2)}) async-start(f32[16,16,128]{2,1,0:T(8,128)} %bitcast.4), calls=%async_computation.1 | async-start | bytes 262144 | tf_op jit(solution)/shard_map/all_to_all | solution.py:535
  54.8 1.9 %copy-start.9 = (s32[12,32]{1,0:T(8,128)S(1)}, s32[12,32]{1,0:T(8,128)}, u32[]{:S(2)}) copy-start(s32[12,32]{1,0:T(8,128)} %refs_1_.5) | copy-start | bytes 4612
  68.5 12.2 %copy-start.1 = (f32[64,4096]{1,0:T(8,128)S(1)}, f32[64,4096]{1,0:T(8,128)}, u32[]{:S(2)}) copy-start(f32[64,4096]{1,0:T(8,128)} %basis_ref.1) | copy-start | bytes 3145732

commit v2 on v1

--- a/solution.py
+++ b/solution.py
@@ -12,10 +12,10 @@
 OFFSETS = (2, 3, -3, -2)
 DELTA = 0.05
 PROXY = 0.35
-HIGHEST = lax.Precision.HIGHEST
 GROUP = 16
 LANES = 128
 VMEM_BYTES = 50 * 1024 * 1024
+FIRST_BYTES = 61 * 1024 * 1024
 
 
 def coupling_stack():
@@ -30,16 +30,31 @@
     return np.concatenate([table, table], axis=1).astype(np.float32)
 
 
+def halves(value):
+    high = value.astype(jnp.bfloat16)
+    return high, (value - high.astype(jnp.float32)).astype(jnp.bfloat16)
+
+
+def bf16_dot(left, right, dims):
+    return lax.dot_general(left, right, (dims, ((), ())), preferred_element_type=jnp.float32)
+
+
+def summed(product, rows, columns):
+    return product[:rows, :columns] + (product[:rows, columns:] + product[rows:, :columns])
+
+
 def dot(left, right):
-    return lax.dot_general(
-        left, right, (((1,), (0,)), ((), ())), precision=HIGHEST, preferred_element_type=jnp.float32
-    )
+    both = bf16_dot(
+        jnp.concatenate(halves(left), axis=0), jnp.concatenate(halves(right), axis=1), ((1,), (0,))
+    )
+    return summed(both, left.shape[0], right.shape[1])
 
 
 def dot_t(left, right):
-    return lax.dot_general(
-        left, right, (((1,), (1,)), ((), ())), precision=HIGHEST, preferred_element_type=jnp.float32
-    )
+    both = bf16_dot(
+        jnp.concatenate(halves(left), axis=0), jnp.concatenate(halves(right), axis=0), ((1,), (1,))
+    )
+    return summed(both, left.shape[0], right.shape[0])
 
 
 def first_half(shape):
@@ -65,25 +80,35 @@
 
 def up(values, matrix):
     count, rows, lanes = values.shape
-    paired = values.reshape(count // 2, 2, rows, lanes)
-    both = packed(paired[:, 0], paired[:, 1]).reshape(count // 2 * rows, lanes)
+    both = paired(values).reshape(count // 2 * rows, lanes)
     return dot(both, matrix).reshape(count // 2, rows, lanes)
 
 
-def down(parents, transfer_ref, half):
-    count, rows, lanes = parents.shape
-    matrix = transfer_ref[half]
+def down(parent, matrix):
     doubled = jnp.concatenate([matrix, matrix], axis=0)
-    flat = parents.reshape(count * rows, lanes)[:, : lanes // 2]
-    return dot_t(flat, doubled).reshape(count, rows, lanes)
-
-
-def down_all(parents, transfer_ref):
-    count, rows, lanes = parents.shape
-    children = jnp.stack(
-        [down(parents, transfer_ref, 0), down(parents, transfer_ref, 1)], axis=1
-    )
-    return children.reshape(2 * count, rows, lanes)
+    return dot_t(parent[:, : LANES // 2], doubled)
+
+
+def down_matrix(transfer_ref):
+    both = jnp.concatenate([transfer_ref[0], transfer_ref[1]], axis=0)
+    zero = jnp.zeros(both.shape, jnp.float32)
+    return jnp.concatenate(
+        [jnp.concatenate([both, zero], axis=1), jnp.concatenate([zero, both], axis=1)], axis=0
+    )
+
+
+def down_pairs(pairs, matrix):
+    count, rows, lanes = pairs.shape
+    both = dot_t(pairs.reshape(count * rows, lanes), matrix).reshape(count, rows, 2 * lanes)
+    return jnp.stack([both[:, :, :lanes], both[:, :, lanes:]], axis=1).reshape(
+        2 * count, rows, lanes
+    )
+
+
+def paired(values):
+    count, rows, lanes = values.shape
+    pairs = values.reshape(count // 2, 2, rows, lanes)
+    return packed(pairs[:, 0], pairs[:, 1])
 
 
 def level_starts(total_leaves, levels):
@@ -94,20 +119,46 @@
     total_leaves,
     levels,
     dev_ref,
+    points_in,
+    charges_in,
+    basis_in,
+    ordering_in,
+    transfer_in,
+    coupling_in,
+    pay_right_ref,
+    pay_left_ref,
+    message_ref,
+    local_ref,
+    counts_ref,
+    inverse_ref,
     points_ref,
     charges_ref,
     basis_ref,
     ordering_ref,
     transfer_ref,
     coupling_ref,
-    pay_right_ref,
-    pay_left_ref,
-    message_ref,
-    local_ref,
-    counts_ref,
-    inverse_ref,
+    arrived,
 ):
     device = dev_ref[0]
+    moves = [
+        (charges_in, charges_ref),
+        (ordering_in, ordering_ref),
+        (points_in, points_ref),
+        (transfer_in, transfer_ref),
+    ]
+    quarter = basis_in.shape[1] // 4
+    for part in range(4):
+        cols = pl.ds(part * quarter, quarter)
+        moves.append((basis_in.at[:, cols], basis_ref.at[:, cols]))
+    moves.append((coupling_in, coupling_ref))
+    copies = [
+        pltpu.make_async_copy(source, target, arrived.at[slot])
+        for slot, (source, target) in enumerate(moves)
+    ]
+    for copy in copies:
+        copy.start()
+    for copy in copies[:3]:
+        copy.wait()
     rhs = charges_ref.shape[0]
     leaves = ordering_ref.shape[0]
     data_rows = pay_right_ref.shape[0] - 12 * rhs
@@ -122,6 +173,8 @@
     zero = jnp.zeros((rhs, LANES), jnp.float32)
     expansions = []
     for pair in range(leaves // 2):
+        if pair % (leaves // 8) == 0:
+            copies[4 + pair // (leaves // 8)].wait()
         gathered = []
         for leaf in (2 * pair, 2 * pair + 1):
             ids = jnp.broadcast_to(ordering_ref[leaf : leaf + 1, :], (rhs, LANES))
@@ -138,6 +191,7 @@
         both = dot_t(left, jnp.concatenate([part, part], axis=0))
         expansions.append(both.reshape(2, rhs, LANES))
     current = jnp.concatenate(expansions, axis=0)
+    copies[3].wait()
     matrix = up_matrix(transfer_ref)
     base = 0
     edge = data_rows
@@ -152,6 +206,7 @@
     message = packed(current[0], current[1])
     for peer in range(message_ref.shape[0] // rhs):
         message_ref[peer * rhs : (peer + 1) * rhs, :] = message
+    copies[8].wait()
     lane = lax.broadcasted_iota(jnp.int32, (1, LANES), 1)
     starts = level_starts(total_leaves, levels)
     last = starts[-1] // LANES * LANES
@@ -232,7 +287,7 @@
         axes = [
             jnp.broadcast_to(columns[:, axis : axis + 1], (LANES, LANES)) for axis in range(3)
         ]
-        total = jnp.zeros((LANES, 2 * rhs), jnp.float32)
+        total = jnp.zeros((2 * rhs, LANES), jnp.float32)
         for pair in range(entries // 2):
             highs, lows, sides = [], [], []
             for entry in (2 * pair, 2 * pair + 1):
@@ -252,16 +307,13 @@
                 sides.append(weights[source, :, :])
             side = jnp.concatenate(sides, axis=1)
             for piece in (jnp.concatenate(highs, axis=1), jnp.concatenate(lows, axis=1)):
-                total = total + lax.dot_general(
-                    piece, side, (((1,), (1,)), ((), ())), preferred_element_type=jnp.float32
-                )
-        turned = jnp.transpose(total)
+                total = total + bf16_dot(side, piece, ((1,), (1,)))
         out_ref[:, pl.ds(pl.multiple_of(step * LANES, LANES), LANES)] = (
-            turned[0:rhs, :] + turned[rhs : 2 * rhs, :]
+            total[0:rhs, :] + total[rhs : 2 * rhs, :]
         )
         return carry
 
-    lax.fori_loop(0, targets, one, 0)
+    lax.fori_loop(0, targets, one, 0, unroll=4)
 
 
 def couple(window, count, level, lane0, counts_ref, x_ref, row0, rows):
@@ -279,7 +331,6 @@
     dev_ref, counts_ref, local_ref, before_ref, after_ref, stack_ref, out_ref, x_ref
 ):
     device = dev_ref[0]
-    rhs = (before_ref.shape[0] - local_ref.shape[0] // 60 * 48) // 12
     rhs = local_ref.shape[0] // 60
     edge = before_ref.shape[0] - 12 * rhs
     base = 0
@@ -297,7 +348,9 @@
         couple(window, count, level, lane0, counts_ref, x_ref, base, rhs)
         base += count * rhs
         edge += 3 * rhs
-    out_ref[...] = dot(x_ref[...], stack_ref[...])
+    terms = dot(x_ref[...], stack_ref[...])
+    pairs = paired(terms.reshape(-1, rhs, LANES))
+    out_ref[...] = pairs.reshape(out_ref.shape)
 
 
 def upper_kernel(
@@ -307,6 +360,7 @@
     gathered_ref,
     transfer_ref,
     stack_ref,
+    _,
     out_ref,
     x_ref,
     top_ref,
@@ -395,13 +449,16 @@
         start, count = spans[level - 4]
         return terms[start : start + count * rhs].reshape(count, rhs, LANES)
 
-    current = term(11)
+    current = term(11)[0]
     for level in (10, 9):
-        current = term(level) + down(current, transfer_ref, (group >> (level - 9)) & 1)
-    for level in (8, 7, 6, 5, 4):
-        current = term(level) + down_all(current, transfer_ref)
-    paired = current.reshape(GROUP, 2, rhs, LANES)
-    out_ref[...] = packed(paired[:, 0], paired[:, 1]).reshape(GROUP * rhs, LANES)
+        child = (group >> (level - 9)) & 1
+        current = term(level)[0] + down(current, transfer_ref[child])
+    both = jnp.concatenate([transfer_ref[0], transfer_ref[1]], axis=0)
+    current = (dot_t(current[:, :half], both) + paired(term(8))[0])[None]
+    matrix = down_matrix(transfer_ref)
+    for level in (7, 6, 5, 4):
+        current = paired(term(level)) + down_pairs(current, matrix)
+    out_ref[...] = current.reshape(out_ref.shape)
 
 
 def final_kernel(
@@ -412,14 +469,14 @@
     total = parts_ref[0:rhs, :]
     for sender in range(1, GROUP):
         total = total + parts_ref[sender * rhs : (sender + 1) * rhs, :]
-    left, right = unpacked(total)
-    current = jnp.stack([left, right])
+    current = total[None]
+    matrix = down_matrix(transfer_ref)
     base = terms_ref.shape[0]
     for level in (3, 2, 1, 0):
-        count = leaves >> level
+        count = leaves >> level + 1
         base -= count * rhs
         mine = terms_ref[base : base + count * rhs, :].reshape(count, rhs, LANES)
-        current = mine + down_all(current, transfer_ref)
+        current = mine + down_pairs(current, matrix)
     lane = lax.broadcasted_iota(jnp.int32, (rhs, LANES), 1)
     low = lane < LANES // 2
     zero = jnp.zeros((rhs, LANES), jnp.float32)
@@ -427,7 +484,7 @@
         rows, sides = [], []
         for slot in range(4):
             leaf = 4 * four + slot
-            value = jnp.where(low if slot % 2 == 0 else ~low, current[leaf], 0.0)
+            value = jnp.where(low if slot % 2 == 0 else ~low, current[leaf // 2], 0.0)
             rows.append(jnp.concatenate([value, zero] if slot < 2 else [zero, value], axis=1))
             sides.append(basis_ref[:, leaf * LANES : (leaf + 1) * LANES])
         far = dot(jnp.concatenate(rows, axis=0), jnp.concatenate(sides, axis=0))
@@ -440,18 +497,19 @@
             out_ref[:, leaf * LANES : (leaf + 1) * LANES] = value + near_ref[:, at : at + LANES]
 
 
-def call(kernel, outs, scalars, operands, scratch=(), cost=None):
+def call(kernel, outs, scalars, operands, scratch=(), cost=None, kept=(), limit=VMEM_BYTES):
     smem = pl.BlockSpec(memory_space=pltpu.SMEM)
     vmem = pl.BlockSpec(memory_space=pltpu.VMEM)
+    hbm = pl.BlockSpec(memory_space=pltpu.HBM)
     return pl.pallas_call(
         kernel,
         out_shape=outs,
-        in_specs=[smem] * len(scalars) + [vmem] * len(operands),
+        in_specs=[smem] * len(scalars) + [vmem] * len(operands) + [hbm] * len(kept),
         out_specs=jax.tree.map(lambda _: vmem, outs),
         scratch_shapes=list(scratch),
         cost_estimate=cost,
-        compiler_params=pltpu.CompilerParams(vmem_limit_bytes=VMEM_BYTES),
-    )(*scalars, *operands)
+        compiler_params=pltpu.CompilerParams(vmem_limit_bytes=limit),
+    )(*scalars, *operands, *kept)
 
 
 def local(points, charges, basis, transfer, near_list, coupling_list, ordering):
@@ -468,6 +526,7 @@
     pay_rows = leaves * 24 + 12 * rhs
     local_rows = (leaves * 2 - 4) * rhs
 
+    inputs = [points, charges, basis, ids, transfer, coupling_list]
     pay_right, pay_left, message, local_terms, counts, inverse = call(
         lambda *refs: prepare_kernel(total_leaves, levels, *refs),
         [
@@ -479,7 +538,13 @@
             jax.ShapeDtypeStruct((leaves, LANES), jnp.int32),
         ],
         [device],
-        [points, charges, basis, ids, transfer, coupling_list],
+        [],
+        [
+            *[pltpu.VMEM(array.shape, array.dtype) for array in inputs],
+            pltpu.SemaphoreType.DMA((len(inputs) + 3,)),
+        ],
+        kept=inputs,
+        limit=FIRST_BYTES,
     )
     before = lax.ppermute(pay_right, "leaf", [(i, (i + 1) % devices) for i in range(devices)])
     after = lax.ppermute(pay_left, "leaf", [((i + 1) % devices, i) for i in range(devices)])
@@ -497,7 +562,7 @@
             lambda *refs: near_kernel(total_leaves, first, *refs),
             jax.ShapeDtypeStruct((rhs, count * LANES), f32),
             [device, near_list],
-            [pay_right, before, after, *extra],
+            [pay_right, before, after],
             [
                 pltpu.VMEM((3 * leaves, 8, LANES), f32),
                 pltpu.VMEM((3 * leaves, 2 * rhs, LANES), jnp.bfloat16),
@@ -507,12 +572,13 @@
                 bytes_accessed=8 << 20,
                 transcendentals=count * 12 * 128 * 128,
             ),
+            kept=extra,
         )
 
     near_a = near(0, leaves // 2, [])
     terms = call(
         local_kernel,
-        jax.ShapeDtypeStruct((local_rows, LANES), f32),
+        jax.ShapeDtypeStruct((local_rows // 2, LANES), f32),
         [device, counts],
         [local_terms, before, after, stack],
         [pltpu.VMEM((local_rows, 2 * LANES), f32)],
@@ -531,6 +597,7 @@
                 for step in range(5)
             ],
         ],
+        kept=[near_a],
     )
     parts = lax.all_to_all(
         spread,

time: 84.1 us -> 69 us (0.82)
  Pallas kernels: 40.4 us -> 29 us
  local copies, waits for them, and re-layouts: 5.63 us -> 0.06 us
  starting transfers between devices: 31.2 us -> 35.8 us
  waiting for transfers between devices: 6.21 us -> 3.62 us
    pallas_call x6, Pallas kernels: 40.4 us -> 29 us  [call(): pl.pallas_call(kernel, out_shape=outs, in_specs=[smem] * len(scalars) + [...]
    ppermute x1, starting transfers between devices: 1.92 us -> 8.91 us  [local(): lax.ppermute(pay_left, 'leaf', [((i + 1) % devices, i) for i in range(dev...]
    unnamed x20 -> x16, local copies, waits for them, and re-layouts: 5.63 us -> 0.06 us
    all_to_all x1, starting transfers between devices: 16.6 us -> 11.4 us  [local(): lax.all_to_all(message, 'leaf', 0, 0, axis_index_groups=[[g * GROUP + i f...]
    all_to_all x1, starting transfers between devices: 8.71 us -> 13.5 us  [local(): lax.all_to_all(spread, 'leaf', 0, 0, axis_index_groups=[[g * GROUP + i fo...]
    all_to_all x1, waiting for transfers between devices: 6.2 us -> 3.62 us  [local(): lax.all_to_all(message, 'leaf', 0, 0, axis_index_groups=[[g * GROUP + i f...]
    ppermute x1, starting transfers between devices: 3.96 us -> 1.92 us  [local(): lax.ppermute(pay_right, 'leaf', [(i, (i + 1) % devices) for i in range(de...]
  transfers between devices with their start and end apart: 4 -> 4, of which waited for: 1 -> 1; matrix products, arithmetic and copies ran while one was open for 0% -> 0% of each run, Pallas kernels for 41% -> 25%
where the time goes in v2:
time: 69 us; the launch traced here: 68.6 us
  starting transfers between devices  35.8 us (52%)
  Pallas kernels  29 us (42%)
  waiting for transfers between devices  3.62 us (5%)
    pallas_call x6, Pallas kernels, call(): pl.pallas_call(kernel, out_shape=outs, in_specs=[smem] * len(scalars) + [...  29 us
    all_to_all x1, starting transfers between devices, local(): lax.all_to_all(spread, 'leaf', 0, 0, axis_index_groups=[[g * GROUP + i fo...  13.5 us
    all_to_all x1, starting transfers between devices, local(): lax.all_to_all(message, 'leaf', 0, 0, axis_index_groups=[[g * GROUP + i f...  11.4 us
    ppermute x1, starting transfers between devices, local(): lax.ppermute(pay_left, 'leaf', [((i + 1) % devices, i) for i in range(dev...  8.91 us
    all_to_all x1, waiting for transfers between devices, local(): lax.all_to_all(message, 'leaf', 0, 0, axis_index_groups=[[g * GROUP + i f...  3.62 us
    ppermute x1, starting transfers between devices, local(): lax.ppermute(pay_right, 'leaf', [(i, (i + 1) % devices) for i in range(de...  1.92 us
  transfers between devices with their start and end apart: 4, of which 1 were waited for; matrix products, arithmetic and copies ran while one was open for 0% of the time, Pallas kernels for 25%

profile of v2, /device:TPU:1, one launch (start us, length us, event | category | flops | bytes accessed | tf_op | source)
XLA Modules:
  0.0 68.6 jit_solution(13555760501522349810)
XLA Ops:
  0.0 4.8 %shard_map.82 = (f32[960,128]{1,0:T(8,128)}, f32[960,128]{1,0:T(8,128)}, f32[512,128]{1,0:T(8,128)}, f32[960,128]{1,0:T(8,128)}, f32[48,128]{1,0:T(8,128)}, /*index=5*/s32[32,128]{1,0:T(8,128)}) custom-call(s32[1]{0:T(128)} %bitcast.refs_0_.dev_ref, f32[3,4096]{1,0:T(4,128)} %refs_1_.3, f32[16,4096]{1,0:T(8,128)} %refs_2_.1, f32[64,4096]{1,0:T(8,128)} %basis_ref.1, ...), custom_call_target="tpu_custom_call" | custom-call | tf_op jit(solution)/shard_map/pallas_call | solution.py:504
  4.8 0.0 copy-start.6
  4.8 8.9 %collective-permute-start.1 = (f32[960,128]{1,0:T(8,128)}, f32[960,128]{1,0:T(8,128)S(1)}, u32[]{:S(2)}, u32[]{:S(2)}) collective-permute-start(f32[960,128]{1,0:T(8,128)} %get-tuple-element.14), channel_id=1, source_target_pairs={{1,0},{2,1},{3,2},{4,3},{5,4},{6,5},{7,6},{8,7},{9,8},{10,9},{11,1... | collective-permute-start | bytes 1474568 | tf_op jit(solution)/shard_map/ppermute | solution.py:550
  13.7 1.9 %collective-permute-start = (f32[960,128]{1,0:T(8,128)}, f32[960,128]{1,0:T(8,128)S(1)}, u32[]{:S(2)}, u32[]{:S(2)}) collective-permute-start(f32[960,128]{1,0:T(8,128)} %get-tuple-element.13.refs_2_), channel_id=1, source_target_pairs={{0,1},{1,2},{2,3},{3,4},{4,5},{5,6},{6,7},{7,8},{8,9},{9,10},{10,1... | collective-permute-start | bytes 1474568 | tf_op jit(solution)/shard_map/ppermute | solution.py:549
  15.7 0.0 copy-start.7
  15.7 11.4 %all-to-all-start = ((f32[32,16,128]{2,1,0:T(8,128)}), f32[32,16,128]{2,1,0:T(8,128)S(1)}, u32[]{:S(2)}, u32[]{:S(2)}) async-start(f32[32,16,128]{2,1,0:T(8,128)} %bitcast.8), calls=%async_computation | async-start | bytes 524288 | tf_op jit(solution)/shard_map/all_to_all | solution.py:551
  27.1 0.0 copy-start.1
  27.1 0.0 copy-start.2
  27.1 0.0 copy-start.4
  27.1 0.0 collective-permute-done.1.refs_4_.after_ref
  27.1 0.0 collective-permute-done.refs_3_.before_ref
  27.2 7.9 %shard_map.83.refs_5_.near_a_ref = f32[16,2048]{1,0:T(8,128)S(1)} custom-call(s32[1]{0:T(128)} %bitcast.refs_0_.dev_ref, s32[12,32]{1,0:T(8,128)S(1)} %copy-done.7, f32[960,128]{1,0:T(8,128)S(1)} %copy-done.6, f32[960,128]{1,0:T(8,128)S(1)} %collective-permute-done.refs_3_.before_ref, f32[960,128]{1,0:T(8,128)S(1)} %collective-permute-done.1.refs_4_.after_ref), custom_call_target="tpu_custom_call" | custom-call | flops 314572800 | bytes 8388608 | tf_op jit(solution)/shard_map/pallas_call | solution.py:504
  35.1 3.6 %all-to-all-done = f32[32,16,128]{2,1,0:T(8,128)S(1)} async-done(((f32[32,16,128]{2,1,0:T(8,128)}), f32[32,16,128]{2,1,0:T(8,128)S(1)}, u32[]{:S(2)}, u32[]{:S(2)}) %all-to-all-start) | async-done | bytes 262176 | tf_op jit(solution)/shard_map/all_to_all | solution.py:551
  38.7 0.0 copy-done.1
  38.7 5.2 %shard_map.84.refs_5_ = f32[256,128]{1,0:T(8,128)} custom-call(s32[1]{0:T(128)} %bitcast.refs_0_.dev_ref, f32[48,128]{1,0:T(8,128)S(1)} %copy-done.4, f32[512,128]{1,0:T(8,128)S(1)} %bitcast.6, f32[2,64,64]{2,1,0:T(8,128)S(1)} %copy-done.1, f32[256,128]{1,0:T(8,128)S(1)} %copy-done.2, f32[16,2048]{1,0:T(8,128)S(1)} %shard_map.83.refs_5_.near_a_ref), custom_call_target="tpu_custom_call" | custom-call | tf_op jit(solution)/shard_map/pallas_call | solution.py:504
  43.9 13.5 %all-to-all-start.1 = ((f32[16,16,128]{2,1,0:T(8,128)}), f32[16,16,128]{2,1,0:T(8,128)S(1)}, u32[]{:S(2)}, u32[]{:S(2)}) async-start(f32[16,16,128]{2,1,0:T(8,128)} %bitcast.4), calls=%async_computation.1 | async-start | bytes 262144 | tf_op jit(solution)/shard_map/all_to_all | solution.py:602
  57.4 0.0 copy-done.3
  57.4 1.4 %shard_map.85.terms_ref = f32[480,128]{1,0:T(8,128)S(1)} custom-call(s32[1]{0:T(128)} %bitcast.refs_0_.dev_ref, f32[48,128]{1,0:T(8,128)S(1)} %copy-done.4, f32[960,128]{1,0:T(8,128)S(1)} %copy-done.3, f32[960,128]{1,0:T(8,128)S(1)} %collective-permute-done.refs_3_.before_ref, f32[960,128]{1,0:T(8,128)S(1)} %collective-permute-done.1.refs_4_.after_ref, ...), custom_call_target="tpu_custom_call" | custom-call | tf_op jit(solution)/shard_map/pallas_call | solution.py:504
  58.8 0.0 copy-start
  58.8 7.9 %shard_map.86.near_b_ref = f32[16,2048]{1,0:T(8,128)S(1)} custom-call(s32[1]{0:T(128)} %bitcast.refs_0_.dev_ref, s32[12,32]{1,0:T(8,128)S(1)} %copy-done.7, f32[960,128]{1,0:T(8,128)S(1)} %copy-done.6, f32[960,128]{1,0:T(8,128)S(1)} %collective-permute-done.refs_3_.before_ref, f32[960,128]{1,0:T(8,128)S(1)} %collective-permute-done.1.refs_4_.after_ref, ...), custom_call_target="tpu_custom_call" | custom-call | flops 314572800 | bytes 8388608 | tf_op jit(solution)/shard_map/pallas_call | solution.py:504
  66.7 0.0 all-to-all-done.1
  66.7 0.0 copy-done
  66.8 0.0 copy-done.5
  66.8 1.8 %shard_map.87 = f32[16,4096]{1,0:T(8,128)} custom-call(f32[256,128]{1,0:T(8,128)S(1)} %bitcast.7, f32[480,128]{1,0:T(8,128)S(1)} %shard_map.85.terms_ref, f32[2,64,64]{2,1,0:T(8,128)S(1)} %copy-done.1, f32[64,4096]{1,0:T(8,128)S(1)} %copy-done, s32[32,128]{1,0:T(8,128)S(1)} %copy-done.5, f32[16,2048]{1,0:T(8,128)S(1)} %shard_map.83.refs_5_.near_a_ref, ...), custom_call_target="tpu_custom_call" | custom-call | tf_op jit(solution)/shard_map/pallas_call | solution.py:504
  (6 shorter events, 0.0 us)
Async XLA Ops:
  4.8 22.4 %copy-start.6 = (f32[960,128]{1,0:T(8,128)S(1)}, f32[960,128]{1,0:T(8,128)}, u32[]{:S(2)}) copy-start(f32[960,128]{1,0:T(8,128)} %get-tuple-element.13.refs_2_) | copy-start | bytes 1474564
  4.8 22.3 %collective-permute-start.1 = (f32[960,128]{1,0:T(8,128)}, f32[960,128]{1,0:T(8,128)S(1)}, u32[]{:S(2)}, u32[]{:S(2)}) collective-permute-start(f32[960,128]{1,0:T(8,128)} %get-tuple-element.14), channel_id=1, source_target_pairs={{1,0},{2,1},{3,2},{4,3},{5,4},{6,5},{7,6},{8,7},{9,8},{10,9},{11,1... | collective-permute-start | bytes 1474568 | tf_op jit(solution)/shard_map/ppermute | solution.py:550
  13.7 13.4 %collective-permute-start = (f32[960,128]{1,0:T(8,128)}, f32[960,128]{1,0:T(8,128)S(1)}, u32[]{:S(2)}, u32[]{:S(2)}) collective-permute-start(f32[960,128]{1,0:T(8,128)} %get-tuple-element.13.refs_2_), channel_id=1, source_target_pairs={{0,1},{1,2},{2,3},{3,4},{4,5},{5,6},{6,7},{7,8},{8,9},{9,10},{10,1... | collective-permute-start | bytes 1474568 | tf_op jit(solution)/shard_map/ppermute | solution.py:549
  15.7 11.5 %copy-start.7 = (s32[12,32]{1,0:T(8,128)S(1)}, s32[12,32]{1,0:T(8,128)}, u32[]{:S(2)}) copy-start(s32[12,32]{1,0:T(8,128)} %refs_1_.5) | copy-start | bytes 4612
  15.7 23.0 %all-to-all-start = ((f32[32,16,128]{2,1,0:T(8,128)}), f32[32,16,128]{2,1,0:T(8,128)S(1)}, u32[]{:S(2)}, u32[]{:S(2)}) async-start(f32[32,16,128]{2,1,0:T(8,128)} %bitcast.8), calls=%async_computation | async-start | bytes 524288 | tf_op jit(solution)/shard_map/all_to_all | solution.py:551
  27.1 11.6 %copy-start.1 = (f32[2,64,64]{2,1,0:T(8,128)S(1)}, f32[2,64,64]{2,1,0:T(8,128)}, u32[]{:S(2)}) copy-start(f32[2,64,64]{2,1,0:T(8,128)} %transfer_ref.1) | copy-start | bytes 98308
  27.1 11.6 %copy-start.2 = (f32[256,128]{1,0:T(8,128)S(1)}, f32[256,128]{1,0:T(8,128)}, u32[]{:S(2)}) copy-start(f32[256,128]{1,0:T(8,128)} %constant.6.clone.refs_4_.stack_ref) | copy-start | bytes 393220
  27.1 11.6 %copy-start.4 = (f32[48,128]{1,0:T(8,128)S(1)}, f32[48,128]{1,0:T(8,128)}, u32[]{:S(2)}) copy-start(f32[48,128]{1,0:T(8,128)} %get-tuple-element.11.refs_1_.counts_ref) | copy-start | bytes 73732
  38.7 18.7 %copy-start.3 = (f32[960,128]{1,0:T(8,128)S(1)}, f32[960,128]{1,0:T(8,128)}, u32[]{:S(2)}) copy-start(f32[960,128]{1,0:T(8,128)} %get-tuple-element.15.local_ref) | copy-start | bytes 1474564
  43.9 22.8 %all-to-all-start.1 = ((f32[16,16,128]{2,1,0:T(8,128)}), f32[16,16,128]{2,1,0:T(8,128)S(1)}, u32[]{:S(2)}, u32[]{:S(2)}) async-start(f32[16,16,128]{2,1,0:T(8,128)} %bitcast.4), calls=%async_computation.1 | async-start | bytes 262144 | tf_op jit(solution)/shard_map/all_to_all | solution.py:602
  58.8 7.9 %copy-start = (f32[64,4096]{1,0:T(8,128)S(1)}, f32[64,4096]{1,0:T(8,128)}, u32[]{:S(2)}) copy-start(f32[64,4096]{1,0:T(8,128)} %basis_ref.1) | copy-start | bytes 3145732
  58.8 7.9 %copy-start.5 = (s32[32,128]{1,0:T(8,128)S(1)}, s32[32,128]{1,0:T(8,128)}, u32[]{:S(2)}) copy-start(s32[32,128]{1,0:T(8,128)} %get-tuple-element.16.inverse_ref) | copy-start | bytes 49156

commit v3 on v2

--- a/solution.py
+++ b/solution.py
@@ -131,50 +131,64 @@
     local_ref,
     counts_ref,
     inverse_ref,
+    paths_ref,
     points_ref,
     charges_ref,
     basis_ref,
     ordering_ref,
     transfer_ref,
     coupling_ref,
+    data_ref,
+    edge_ref,
     arrived,
 ):
     device = dev_ref[0]
     moves = [
         (charges_in, charges_ref),
+        (points_in, points_ref),
         (ordering_in, ordering_ref),
-        (points_in, points_ref),
         (transfer_in, transfer_ref),
+        (basis_in, basis_ref),
+        (coupling_in, coupling_ref),
     ]
-    quarter = basis_in.shape[1] // 4
-    for part in range(4):
-        cols = pl.ds(part * quarter, quarter)
-        moves.append((basis_in.at[:, cols], basis_ref.at[:, cols]))
-    moves.append((coupling_in, coupling_ref))
     copies = [
         pltpu.make_async_copy(source, target, arrived.at[slot])
         for slot, (source, target) in enumerate(moves)
     ]
     for copy in copies:
         copy.start()
-    for copy in copies[:3]:
-        copy.wait()
     rhs = charges_ref.shape[0]
     leaves = ordering_ref.shape[0]
-    data_rows = pay_right_ref.shape[0] - 12 * rhs
-    block = data_rows // leaves
-    filler = jnp.zeros((block - rhs - 3, LANES), jnp.float32)
+    data_rows = leaves * (rhs + 3)
+    copies[0].wait()
+    copies[1].wait()
     for leaf in range(leaves):
         cols = slice(leaf * LANES, (leaf + 1) * LANES)
-        rows = slice(leaf * block, (leaf + 1) * block)
-        value = jnp.concatenate([charges_ref[:, cols], points_ref[:, cols], filler], axis=0)
-        pay_right_ref[rows, :] = value
-        pay_left_ref[rows, :] = value
+        data_ref[leaf * rhs : (leaf + 1) * rhs, :] = charges_ref[:, cols]
+        for axis in range(3):
+            at = leaves * (rhs + axis) + leaf
+            data_ref[at : at + 1, :] = points_ref[axis : axis + 1, cols]
+    sent = [
+        pltpu.make_async_copy(
+            data_ref, target.at[pl.ds(0, data_rows), :], arrived.at[len(moves) + slot]
+        )
+        for slot, target in enumerate((pay_right_ref, pay_left_ref))
+    ]
+    for copy in sent:
+        copy.start()
+    copies[2].wait()
+    slots = lax.broadcasted_iota(jnp.int32, (LANES, LANES), 0)
+    numbers = lax.broadcasted_iota(jnp.int32, (16, LANES), 1).astype(jnp.float32)
+    numbers = numbers.astype(jnp.bfloat16)
+    for leaf in range(leaves):
+        hit = jnp.where(ordering_ref[leaf : leaf + 1, :] == slots, 1.0, 0.0).astype(jnp.bfloat16)
+        found = bf16_dot(numbers, hit, ((1,), (1,)))
+        inverse_ref[leaf : leaf + 1, :] = found[0:1].astype(jnp.int32)
     zero = jnp.zeros((rhs, LANES), jnp.float32)
     expansions = []
+    for copy in copies[3:]:
+        copy.wait()
     for pair in range(leaves // 2):
-        if pair % (leaves // 8) == 0:
-            copies[4 + pair // (leaves // 8)].wait()
         gathered = []
         for leaf in (2 * pair, 2 * pair + 1):
             ids = jnp.broadcast_to(ordering_ref[leaf : leaf + 1, :], (rhs, LANES))
@@ -191,22 +205,37 @@
         both = dot_t(left, jnp.concatenate([part, part], axis=0))
         expansions.append(both.reshape(2, rhs, LANES))
     current = jnp.concatenate(expansions, axis=0)
-    copies[3].wait()
     matrix = up_matrix(transfer_ref)
+    path = matrix
+    for level in range(5, 10):
+        paths_ref[:, (level - 5) * LANES : (level - 4) * LANES] = path
+        if level < 9:
+            bit = ((device % GROUP) >> (level - 5)) & 1
+            path = dot(path[:, : LANES // 2], twice(transfer_ref[bit]))
     base = 0
-    edge = data_rows
+    lasts, firsts = [], []
     for level in range(4):
         count = leaves >> level
         local_ref[base : base + count * rhs, :] = current.reshape(count * rhs, LANES)
-        pay_right_ref[edge : edge + 3 * rhs, :] = current[count - 3 :].reshape(3 * rhs, LANES)
-        pay_left_ref[edge : edge + 3 * rhs, :] = current[:3].reshape(3 * rhs, LANES)
+        lasts.append(current[count - 3 :])
+        firsts.append(current[:3])
         base += count * rhs
-        edge += 3 * rhs
         current = up(current, matrix)
+    for slot, edges in enumerate((lasts, firsts)):
+        edge_ref[slot] = paired(jnp.concatenate(edges, axis=0)).reshape(6 * rhs, LANES)
+    ends = [
+        pltpu.make_async_copy(
+            edge_ref.at[slot],
+            target.at[pl.ds(data_rows, 6 * rhs), :],
+            arrived.at[len(moves) + 2 + slot],
+        )
+        for slot, target in enumerate((pay_right_ref, pay_left_ref))
+    ]
+    for copy in ends:
+        copy.start()
     message = packed(current[0], current[1])
     for peer in range(message_ref.shape[0] // rhs):
         message_ref[peer * rhs : (peer + 1) * rhs, :] = message
-    copies[8].wait()
     lane = lax.broadcasted_iota(jnp.int32, (1, LANES), 1)
     starts = level_starts(total_leaves, levels)
     last = starts[-1] // LANES * LANES
@@ -236,58 +265,55 @@
             counts_ref[4 * level + slot : 4 * level + slot + 1, :] = jnp.sum(
                 hits, axis=0, keepdims=True
             )
-    slots = lax.broadcasted_iota(jnp.int32, (LANES, LANES), 0)
-    numbers = lax.broadcasted_iota(jnp.int32, (8, LANES), 1).astype(jnp.float32)
-    numbers = numbers.astype(jnp.bfloat16)
-    for leaf in range(leaves):
-        hit = jnp.where(ordering_ref[leaf : leaf + 1, :] == slots, 1.0, 0.0).astype(jnp.bfloat16)
-        found = lax.dot_general(
-            numbers, hit, (((1,), (1,)), ((), ())), preferred_element_type=jnp.float32
-        )
-        inverse_ref[leaf : leaf + 1, :] = found[0:1].astype(jnp.int32)
+    for copy in sent + ends:
+        copy.wait()
 
 
 def near_kernel(
-    total_leaves,
-    first,
-    dev_ref,
-    near_ref,
-    own_ref,
-    before_ref,
-    after_ref,
-    *rest,
+    total_leaves, first, dev_ref, near_ref, own_ref, before_ref, after_ref, *rest
 ):
     out_ref, places, weights = rest[-3:]
     rhs = out_ref.shape[0]
     leaves = near_ref.shape[1]
     entries = near_ref.shape[0]
     targets = out_ref.shape[1] // LANES
-    block = (own_ref.shape[0] - 12 * rhs) // leaves
     for part, ref in enumerate((before_ref, own_ref, after_ref)):
+        rows = slice(part * leaves, (part + 1) * leaves)
+        axes = [
+            ref[leaves * (rhs + axis) : leaves * (rhs + axis + 1), :] - 0.5 for axis in range(3)
+        ]
+        for axis in range(3):
+            places[axis, rows, :] = axes[axis]
+        places[3, rows, :] = axes[1] * axes[1] + axes[2] * axes[2]
 
         def fill(leaf, carry, part=part, ref=ref):
-            rows = pl.multiple_of(leaf * block, 8)
-            charge = ref[pl.ds(rows, rhs), :] * (0.25 / math.pi)
-            high = charge.astype(jnp.bfloat16)
-            low = (charge - high.astype(jnp.float32)).astype(jnp.bfloat16)
-            weights[part * leaves + leaf, 0:rhs, :] = high
-            weights[part * leaves + leaf, rhs : 2 * rhs, :] = low
-            places[part * leaves + leaf, :, :] = ref[pl.ds(rows + rhs, 8), :]
+            charge = ref[pl.ds(pl.multiple_of(leaf * rhs, rhs), rhs), :] * (0.25 / math.pi)
+            weights[part * leaves + leaf] = jnp.concatenate(halves(charge), axis=0)
             return carry
 
-        lax.fori_loop(0, leaves, fill, 0, unroll=4)
+        lax.fori_loop(0, leaves, fill, 0, unroll=8)
 
     device = dev_ref[0]
     half_cycle = total_leaves // 2
+
+    def row_of(kind, slot):
+        return places[kind, pl.ds(slot, 1), :]
 
     def one(step, carry):
         leaf = step + first
         target = device * leaves + leaf
-        columns = jnp.transpose(places[leaves + leaf, :, :])
-        axes = [
-            jnp.broadcast_to(columns[:, axis : axis + 1], (LANES, LANES)) for axis in range(3)
+        here = [row_of(kind, leaves + leaf) for kind in range(4)]
+        size = here[0] * here[0] + (here[3] + DELTA * DELTA)
+        table = jnp.concatenate(
+            [-2.0 * here[0], -2.0 * here[1], -2.0 * here[2], size]
+            + [jnp.zeros((4, LANES), jnp.float32)],
+            axis=0,
+        )
+        columns = jnp.transpose(table)
+        ax, ay, az, size = [
+            jnp.broadcast_to(columns[:, kind : kind + 1], (LANES, LANES)) for kind in range(4)
         ]
-        total = jnp.zeros((2 * rhs, LANES), jnp.float32)
+        total = jnp.zeros((2 * rhs, 2 * LANES), jnp.float32)
         for pair in range(entries // 2):
             highs, lows, sides = [], [], []
             for entry in (2 * pair, 2 * pair + 1):
@@ -295,25 +321,26 @@
                     (near_ref[entry, leaf] - target + half_cycle) & (total_leaves - 1)
                 ) - half_cycle
                 source = leaves + leaf + window
-                shift = window.astype(jnp.float32) * (1.0 / leaves)
-                place = places[source, :, :]
-                dx = axes[0] - (place[0:1, :] + shift)
-                dy = axes[1] - place[1:2, :]
-                dz = axes[2] - place[2:3, :]
-                value = lax.rsqrt(dx * dx + dy * dy + (dz * dz + DELTA * DELTA))
-                high = value.astype(jnp.bfloat16)
+                qx = row_of(0, source) + window.astype(jnp.float32) * (1.0 / leaves)
+                squared = qx * qx + row_of(3, source)
+                value = lax.rsqrt(
+                    ((size + squared) + ax * qx) + (ay * row_of(1, source) + az * row_of(2, source))
+                )
+                high, low = halves(value)
                 highs.append(high)
-                lows.append((value - high.astype(jnp.float32)).astype(jnp.bfloat16))
-                sides.append(weights[source, :, :])
-            side = jnp.concatenate(sides, axis=1)
-            for piece in (jnp.concatenate(highs, axis=1), jnp.concatenate(lows, axis=1)):
-                total = total + bf16_dot(side, piece, ((1,), (1,)))
+                lows.append(low)
+                sides.append(weights[source])
+            piece = jnp.concatenate(
+                [jnp.concatenate(highs, axis=1), jnp.concatenate(lows, axis=1)], axis=0
+            )
+            total = total + bf16_dot(jnp.concatenate(sides, axis=1), piece, ((1,), (1,)))
+        half = total[:, :LANES] + total[:, LANES:]
         out_ref[:, pl.ds(pl.multiple_of(step * LANES, LANES), LANES)] = (
-            total[0:rhs, :] + total[rhs : 2 * rhs, :]
+            half[0:rhs, :] + half[rhs : 2 * rhs, :]
         )
         return carry
 
-    lax.fori_loop(0, targets, one, 0, unroll=4)
+    lax.fori_loop(0, targets, one, 0, unroll=8)
 
 
 def couple(window, count, level, lane0, counts_ref, x_ref, row0, rows):
@@ -328,29 +355,31 @@
 
 
 def local_kernel(
-    dev_ref, counts_ref, local_ref, before_ref, after_ref, stack_ref, out_ref, x_ref
+    dev_ref, counts_ref, local_ref, before_ref, after_ref, stack_ref, out_ref, x_ref, edge_ref
 ):
     device = dev_ref[0]
     rhs = local_ref.shape[0] // 60
-    edge = before_ref.shape[0] - 12 * rhs
+    start = before_ref.shape[0] - 6 * rhs
+    for side, ref in enumerate((before_ref, after_ref)):
+        for pair in range(6):
+            both = ref[start + pair * rhs : start + (pair + 1) * rhs, :]
+            edge_ref[side, 2 * pair], edge_ref[side, 2 * pair + 1] = unpacked(both)
     base = 0
     for level in range(4):
         count = 32 >> level
 
-        def window(t, slot, count=count, base=base, edge=edge):
+        def window(t, slot, count=count, base=base, level=level):
             if t < 0:
-                return before_ref[edge + (t + 3) * rhs : edge + (t + 4) * rhs, :]
+                return edge_ref[0, 3 * level + t + 3]
             if t >= count:
-                return after_ref[edge + (t - count) * rhs : edge + (t - count + 1) * rhs, :]
+                return edge_ref[1, 3 * level + t - count]
             return local_ref[base + t * rhs : base + (t + 1) * rhs, :]
 
         lane0 = (device * count) & (LANES - 1)
         couple(window, count, level, lane0, counts_ref, x_ref, base, rhs)
         base += count * rhs
-        edge += 3 * rhs
     terms = dot(x_ref[...], stack_ref[...])
-    pairs = paired(terms.reshape(-1, rhs, LANES))
-    out_ref[...] = pairs.reshape(out_ref.shape)
+    out_ref[...] = paired(terms.reshape(-1, rhs, LANES)).reshape(out_ref.shape)
 
 
 def upper_kernel(
@@ -360,6 +389,7 @@
     gathered_ref,
     transfer_ref,
     stack_ref,
+    paths_ref,
     _,
     out_ref,
     x_ref,
@@ -371,14 +401,10 @@
     group = device // GROUP
     rhs = out_ref.shape[0] // GROUP
     groups = gathered_ref.shape[0] // rhs
-    bits = [(index >> bit) & 1 for bit in range(4)]
     matrix = up_matrix(transfer_ref)
     half = LANES // 2
 
-    path = dot(dot(transfer_ref[bits[0]], transfer_ref[bits[1]]),
-               dot(transfer_ref[bits[2]], transfer_ref[bits[3]]))
-    whole = dot(matrix[:, :half], twice(path))
-    level9 = dot(gathered_ref[...], whole).reshape(groups, rhs, LANES)
+    level9 = dot(gathered_ref[...], paths_ref[:, 4 * LANES :]).reshape(groups, rhs, LANES)
     level10 = up(level9, matrix)
     level11 = up(level10, matrix)
     top_ref[0:groups] = level9
@@ -399,7 +425,7 @@
     for step in (-1, 0, 1):
         for side, value in enumerate(unpacked(beside[step + 2])):
             place(sparse[0], 2 * GROUP, step * 2 * GROUP + 2 * index + side, value)
-    current = dot(jnp.concatenate(beside, axis=0), matrix)
+    nearby = dot(jnp.concatenate(beside, axis=0), paths_ref[:, : 4 * LANES])
     for level in range(5, 9):
         count = 2 * GROUP >> (level - 4)
         reach = (-1, 0, 1) if count >= 3 else (-2, -1, 0, 1, 2)
@@ -408,10 +434,8 @@
                 sparse[level - 4],
                 count,
                 step * count + (index >> (level - 5)),
-                current[(step + 2) * rhs : (step + 3) * rhs],
+                nearby[(step + 2) * rhs : (step + 3) * rhs, (level - 5) * LANES :][:, :LANES],
             )
-        if level < 8:
-            current = dot(current[:, :half], twice(transfer_ref[bits[level - 5]]))
 
     row0 = 0
     spans = []
@@ -497,7 +521,7 @@
             out_ref[:, leaf * LANES : (leaf + 1) * LANES] = value + near_ref[:, at : at + LANES]
 
 
-def call(kernel, outs, scalars, operands, scratch=(), cost=None, kept=(), limit=VMEM_BYTES):
+def call(kernel, outs, scalars, operands, scratch=(), cost=None, kept=(), limit=VMEM_BYTES, far=0):
     smem = pl.BlockSpec(memory_space=pltpu.SMEM)
     vmem = pl.BlockSpec(memory_space=pltpu.VMEM)
     hbm = pl.BlockSpec(memory_space=pltpu.HBM)
@@ -505,7 +529,7 @@
         kernel,
         out_shape=outs,
         in_specs=[smem] * len(scalars) + [vmem] * len(operands) + [hbm] * len(kept),
-        out_specs=jax.tree.map(lambda _: vmem, outs),
+        out_specs=[hbm] * far + [vmem] * (len(outs) - far) if isinstance(outs, list) else vmem,
         scratch_shapes=list(scratch),
         cost_estimate=cost,
         compiler_params=pltpu.CompilerParams(vmem_limit_bytes=limit),
@@ -523,11 +547,12 @@
     f32 = jnp.float32
     ids = ordering.reshape(leaves, LANES)
     stack = jnp.asarray(coupling_stack())
-    pay_rows = leaves * 24 + 12 * rhs
+    data_rows = leaves * (rhs + 3)
+    pay_rows = data_rows + 6 * rhs
     local_rows = (leaves * 2 - 4) * rhs
 
     inputs = [points, charges, basis, ids, transfer, coupling_list]
-    pay_right, pay_left, message, local_terms, counts, inverse = call(
+    pay_right, pay_left, message, local_terms, counts, inverse, paths = call(
         lambda *refs: prepare_kernel(total_leaves, levels, *refs),
         [
             jax.ShapeDtypeStruct((pay_rows, LANES), f32),
@@ -536,15 +561,19 @@
             jax.ShapeDtypeStruct((local_rows, LANES), f32),
             jax.ShapeDtypeStruct((4 * levels, LANES), f32),
             jax.ShapeDtypeStruct((leaves, LANES), jnp.int32),
+            jax.ShapeDtypeStruct((LANES, 5 * LANES), f32),
         ],
         [device],
         [],
         [
             *[pltpu.VMEM(array.shape, array.dtype) for array in inputs],
-            pltpu.SemaphoreType.DMA((len(inputs) + 3,)),
+            pltpu.VMEM((data_rows, LANES), f32),
+            pltpu.VMEM((2, 6 * rhs, LANES), f32),
+            pltpu.SemaphoreType.DMA((len(inputs) + 4,)),
         ],
         kept=inputs,
         limit=FIRST_BYTES,
+        far=2,
     )
     before = lax.ppermute(pay_right, "leaf", [(i, (i + 1) % devices) for i in range(devices)])
     after = lax.ppermute(pay_left, "leaf", [((i + 1) % devices, i) for i in range(devices)])
@@ -564,7 +593,7 @@
             [device, near_list],
             [pay_right, before, after],
             [
-                pltpu.VMEM((3 * leaves, 8, LANES), f32),
+                pltpu.VMEM((4, 3 * leaves, LANES), f32),
                 pltpu.VMEM((3 * leaves, 2 * rhs, LANES), jnp.bfloat16),
             ],
             pl.CostEstimate(
@@ -581,14 +610,14 @@
         jax.ShapeDtypeStruct((local_rows // 2, LANES), f32),
         [device, counts],
         [local_terms, before, after, stack],
-        [pltpu.VMEM((local_rows, 2 * LANES), f32)],
+        [pltpu.VMEM((local_rows, 2 * LANES), f32), pltpu.VMEM((2, 12, rhs, LANES), f32)],
     )
     upper_rows = (4 * GROUP - 2 + 3) * rhs
     spread = call(
         lambda *refs: upper_kernel(total_leaves, *refs),
         jax.ShapeDtypeStruct((GROUP * rhs, LANES), f32),
         [device, counts],
-        [gathered, transfer, stack],
+        [gathered, transfer, stack, paths],
         [
             pltpu.VMEM((upper_rows, 2 * LANES), f32),
             pltpu.VMEM((2 * groups, rhs, LANES), f32),

time: 69 us -> 70.6 us (1.023)
  waiting for transfers between devices: 3.62 us -> 7.25 us
  Pallas kernels: 29 us -> 25.7 us
  starting transfers between devices: 35.8 us -> 37.1 us
    ppermute x1, starting transfers between devices: 8.91 us -> 2.86 us  [local(): lax.ppermute(pay_left, 'leaf', [((i + 1) % devices, i) for i in range(dev...]
    all_to_all x1, starting transfers between devices: 11.4 us -> 16.7 us  [local(): lax.all_to_all(message, 'leaf', 0, 0, axis_index_groups=[[g * GROUP + i f...]
    ppermute x1, waiting for transfers between devices: 0.01 us -> 3.75 us  [local(): lax.ppermute(pay_right, 'leaf', [(i, (i + 1) % devices) for i in range(de...]
    all_to_all x1, waiting for transfers between devices: 3.62 us -> 0.01 us  [local(): lax.all_to_all(message, 'leaf', 0, 0, axis_index_groups=[[g * GROUP + i f...]
    ppermute x1, waiting for transfers between devices: 0.01 us -> 3.49 us  [local(): lax.ppermute(pay_left, 'leaf', [((i + 1) % devices, i) for i in range(dev...]
    pallas_call x6, Pallas kernels: 29 us -> 25.7 us  [call(): pl.pallas_call(kernel, out_shape=outs, in_specs=[smem] * len(scalars) + [...]
    ppermute x1, starting transfers between devices: 1.92 us -> 3.15 us  [local(): lax.ppermute(pay_right, 'leaf', [(i, (i + 1) % devices) for i in range(de...]
    all_to_all x1, starting transfers between devices: 13.5 us -> 14.4 us  [local(): lax.all_to_all(spread, 'leaf', 0, 0, axis_index_groups=[[g * GROUP + i fo...]
  transfers between devices with their start and end apart: 4 -> 4, of which waited for: 1 -> 2; matrix products, arithmetic and copies ran while one was open for 0% -> 0% of each run, Pallas kernels for 25% -> 21%
where the time goes in v3:
time: 70.6 us; the launch traced here: 70.3 us
  starting transfers between devices  37.1 us (53%)
  Pallas kernels  25.7 us (36%)
  waiting for transfers between devices  7.25 us (10%)
    pallas_call x6, Pallas kernels, call(): pl.pallas_call(kernel, out_shape=outs, in_specs=[smem] * len(scalars) + [...  25.7 us
    all_to_all x1, starting transfers between devices, local(): lax.all_to_all(message, 'leaf', 0, 0, axis_index_groups=[[g * GROUP + i f...  16.7 us
    all_to_all x1, starting transfers between devices, local(): lax.all_to_all(spread, 'leaf', 0, 0, axis_index_groups=[[g * GROUP + i fo...  14.4 us
    ppermute x1, waiting for transfers between devices, local(): lax.ppermute(pay_right, 'leaf', [(i, (i + 1) % devices) for i in range(de...  3.75 us
    ppermute x1, waiting for transfers between devices, local(): lax.ppermute(pay_left, 'leaf', [((i + 1) % devices, i) for i in range(dev...  3.49 us
    ppermute x1, starting transfers between devices, local(): lax.ppermute(pay_right, 'leaf', [(i, (i + 1) % devices) for i in range(de...  3.15 us
    ppermute x1, starting transfers between devices, local(): lax.ppermute(pay_left, 'leaf', [((i + 1) % devices, i) for i in range(dev...  2.86 us
  transfers between devices with their start and end apart: 4, of which 2 were waited for; matrix products, arithmetic and copies ran while one was open for 0% of the time, Pallas kernels for 21%

profile of v3, /device:TPU:1, one launch (start us, length us, event | category | flops | bytes accessed | tf_op | source)
XLA Modules:
  0.0 70.3 jit_solution(5970160114436288747)
XLA Ops:
  0.0 4.9 %shard_map.82 = (f32[704,128]{1,0:T(8,128)}, f32[704,128]{1,0:T(8,128)}, f32[512,128]{1,0:T(8,128)}, f32[960,128]{1,0:T(8,128)}, f32[48,128]{1,0:T(8,128)}, /*index=5*/s32[32,128]{1,0:T(8,128)}, f32[128,640]{1,0:T(8,128)}) custom-call(s32[1]{0:T(128)} %bitcast.refs_0_.dev_ref, f32[3,4096]{1,0:T(4,128)} %refs_1_.3, f32[16,4096]{1,0:T(8,128)} %refs_2_.1, ...), custom_call_target="tpu_custom_call" | custom-call | tf_op jit(solution)/shard_map/pallas_call | solution.py:528
  5.0 0.0 copy-start.7
  5.0 0.0 copy-start.8
  5.0 16.7 %all-to-all-start = ((f32[32,16,128]{2,1,0:T(8,128)}), f32[32,16,128]{2,1,0:T(8,128)S(1)}, u32[]{:S(2)}, u32[]{:S(2)}) async-start(f32[32,16,128]{2,1,0:T(8,128)} %bitcast.8), calls=%async_computation | async-start | bytes 524288 | tf_op jit(solution)/shard_map/all_to_all | solution.py:580
  21.6 2.9 %collective-permute-start.1 = (f32[704,128]{1,0:T(8,128)}, f32[704,128]{1,0:T(8,128)S(1)}, u32[]{:S(2)}, u32[]{:S(2)}) collective-permute-start(f32[704,128]{1,0:T(8,128)} %get-tuple-element.16), channel_id=1, source_target_pairs={{1,0},{2,1},{3,2},{4,3},{5,4},{6,5},{7,6},{8,7},{9,8},{10,9},{11,1... | collective-permute-start | bytes 1081352 | tf_op jit(solution)/shard_map/ppermute | solution.py:579
  24.5 0.0 copy-done.7
  24.5 0.0 copy-start.1
  24.5 0.0 copy-start.2
  24.5 0.0 copy-start.4
  24.6 0.0 copy-start.5
  24.6 3.1 %collective-permute-start = (f32[704,128]{1,0:T(8,128)S(1)}, f32[704,128]{1,0:T(8,128)S(1)}, u32[]{:S(2)}, u32[]{:S(2)}) collective-permute-start(f32[704,128]{1,0:T(8,128)S(1)} %copy-done.7), channel_id=1, source_target_pairs={{0,1},{1,2},{2,3},{3,4},{4,5},{5,6},{6,7},{7,8},{8,9},{9,10},{10,1... | collective-permute-start | bytes 1081352 | tf_op jit(solution)/shard_map/ppermute | solution.py:578
  27.7 3.5 %collective-permute-done.1.refs_4_.after_ref = f32[704,128]{1,0:T(8,128)S(1)} collective-permute-done((f32[704,128]{1,0:T(8,128)}, f32[704,128]{1,0:T(8,128)S(1)}, u32[]{:S(2)}, u32[]{:S(2)}) %collective-permute-start.1) | collective-permute-done | bytes 360480 | tf_op jit(solution)/shard_map/ppermute | solution.py:579
  31.2 3.7 %collective-permute-done.refs_3_.before_ref = f32[704,128]{1,0:T(8,128)S(1)} collective-permute-done((f32[704,128]{1,0:T(8,128)S(1)}, f32[704,128]{1,0:T(8,128)S(1)}, u32[]{:S(2)}, u32[]{:S(2)}) %collective-permute-start) | collective-permute-done | bytes 360480 | tf_op jit(solution)/shard_map/ppermute | solution.py:578
  35.0 0.0 copy-done.8
  35.0 6.7 %shard_map.83.refs_6_.near_a_ref = f32[16,2048]{1,0:T(8,128)S(1)} custom-call(s32[1]{0:T(128)} %bitcast.refs_0_.dev_ref, s32[12,32]{1,0:T(8,128)S(1)} %copy-done.8, f32[704,128]{1,0:T(8,128)S(1)} %copy-done.7, f32[704,128]{1,0:T(8,128)S(1)} %collective-permute-done.refs_3_.before_ref, f32[704,128]{1,0:T(8,128)S(1)} %collective-permute-done.1.refs_4_.after_ref), custom_call_target="tpu_custom_call" | custom-call | flops 314572800 | bytes 8388608 | tf_op jit(solution)/shard_map/pallas_call | solution.py:528
  41.7 0.0 all-to-all-done
  41.7 0.0 copy-done.1
  41.8 4.1 %shard_map.84.refs_5_ = f32[256,128]{1,0:T(8,128)} custom-call(s32[1]{0:T(128)} %bitcast.refs_0_.dev_ref, f32[48,128]{1,0:T(8,128)S(1)} %copy-done.5, f32[512,128]{1,0:T(8,128)S(1)} %bitcast.6, f32[2,64,64]{2,1,0:T(8,128)S(1)} %copy-done.1, f32[256,128]{1,0:T(8,128)S(1)} %copy-done.2, f32[128,640]{1,0:T(8,128)S(1)} %copy-done.4, ...), custom_call_target="tpu_custom_call" | custom-call | tf_op jit(solution)/shard_map/pallas_call | solution.py:528
  45.8 14.4 %all-to-all-start.1 = ((f32[16,16,128]{2,1,0:T(8,128)}), f32[16,16,128]{2,1,0:T(8,128)S(1)}, u32[]{:S(2)}, u32[]{:S(2)}) async-start(f32[16,16,128]{2,1,0:T(8,128)} %bitcast.4), calls=%async_computation.1 | async-start | bytes 262144 | tf_op jit(solution)/shard_map/all_to_all | solution.py:631
  60.2 1.4 %shard_map.85.terms_ref = f32[480,128]{1,0:T(8,128)S(1)} custom-call(s32[1]{0:T(128)} %bitcast.refs_0_.dev_ref, f32[48,128]{1,0:T(8,128)S(1)} %copy-done.5, f32[960,128]{1,0:T(8,128)S(1)} %copy-done.3, f32[704,128]{1,0:T(8,128)S(1)} %collective-permute-done.refs_3_.before_ref, f32[704,128]{1,0:T(8,128)S(1)} %collective-permute-done.1.refs_4_.after_ref, ...), custom_call_target="tpu_custom_call" | custom-call | tf_op jit(solution)/shard_map/pallas_call | solution.py:528
  61.7 0.0 copy-start
  61.7 6.7 %shard_map.86.near_b_ref = f32[16,2048]{1,0:T(8,128)S(1)} custom-call(s32[1]{0:T(128)} %bitcast.refs_0_.dev_ref, s32[12,32]{1,0:T(8,128)S(1)} %copy-done.8, f32[704,128]{1,0:T(8,128)S(1)} %copy-done.7, f32[704,128]{1,0:T(8,128)S(1)} %collective-permute-done.refs_3_.before_ref, f32[704,128]{1,0:T(8,128)S(1)} %collective-permute-done.1.refs_4_.after_ref, ...), custom_call_target="tpu_custom_call" | custom-call | flops 314572800 | bytes 8388608 | tf_op jit(solution)/shard_map/pallas_call | solution.py:528
  68.4 0.0 all-to-all-done.1
  68.5 1.8 %shard_map.87 = f32[16,4096]{1,0:T(8,128)} custom-call(f32[256,128]{1,0:T(8,128)S(1)} %bitcast.7, f32[480,128]{1,0:T(8,128)S(1)} %shard_map.85.terms_ref, f32[2,64,64]{2,1,0:T(8,128)S(1)} %copy-done.1, f32[64,4096]{1,0:T(8,128)S(1)} %copy-done, s32[32,128]{1,0:T(8,128)S(1)} %copy-done.6, f32[16,2048]{1,0:T(8,128)S(1)} %shard_map.83.refs_6_.near_a_ref, ...), custom_call_target="tpu_custom_call" | custom-call | tf_op jit(solution)/shard_map/pallas_call | solution.py:528
  (8 shorter events, 0.0 us)
Async XLA Ops:
  5.0 19.6 %copy-start.7 = (f32[704,128]{1,0:T(8,128)S(1)}, f32[704,128]{1,0:T(8,128)}, u32[]{:S(2)}) copy-start(f32[704,128]{1,0:T(8,128)} %get-tuple-element.15.refs_2_) | copy-start | bytes 1081348
  5.0 30.0 %copy-start.8 = (s32[12,32]{1,0:T(8,128)S(1)}, s32[12,32]{1,0:T(8,128)}, u32[]{:S(2)}) copy-start(s32[12,32]{1,0:T(8,128)} %refs_1_.5) | copy-start | bytes 4612
  5.0 36.7 %all-to-all-start = ((f32[32,16,128]{2,1,0:T(8,128)}), f32[32,16,128]{2,1,0:T(8,128)S(1)}, u32[]{:S(2)}, u32[]{:S(2)}) async-start(f32[32,16,128]{2,1,0:T(8,128)} %bitcast.8), calls=%async_computation | async-start | bytes 524288 | tf_op jit(solution)/shard_map/all_to_all | solution.py:580
  21.6 9.6 %collective-permute-start.1 = (f32[704,128]{1,0:T(8,128)}, f32[704,128]{1,0:T(8,128)S(1)}, u32[]{:S(2)}, u32[]{:S(2)}) collective-permute-start(f32[704,128]{1,0:T(8,128)} %get-tuple-element.16), channel_id=1, source_target_pairs={{1,0},{2,1},{3,2},{4,3},{5,4},{6,5},{7,6},{8,7},{9,8},{10,9},{11,1... | collective-permute-start | bytes 1081352 | tf_op jit(solution)/shard_map/ppermute | solution.py:579
  24.5 17.2 %copy-start.1 = (f32[2,64,64]{2,1,0:T(8,128)S(1)}, f32[2,64,64]{2,1,0:T(8,128)}, u32[]{:S(2)}) copy-start(f32[2,64,64]{2,1,0:T(8,128)} %transfer_ref.1) | copy-start | bytes 98308
  24.5 17.2 %copy-start.2 = (f32[256,128]{1,0:T(8,128)S(1)}, f32[256,128]{1,0:T(8,128)}, u32[]{:S(2)}) copy-start(f32[256,128]{1,0:T(8,128)} %constant.6.clone.refs_4_.stack_ref) | copy-start | bytes 393220
  24.5 17.2 %copy-start.4 = (f32[128,640]{1,0:T(8,128)S(1)}, f32[128,640]{1,0:T(8,128)}, u32[]{:S(2)}) copy-start(f32[128,640]{1,0:T(8,128)} %get-tuple-element.14.refs_5_) | copy-start | bytes 983044
  24.6 17.2 %copy-start.5 = (f32[48,128]{1,0:T(8,128)S(1)}, f32[48,128]{1,0:T(8,128)}, u32[]{:S(2)}) copy-start(f32[48,128]{1,0:T(8,128)} %get-tuple-element.12.refs_1_.counts_ref) | copy-start | bytes 73732
  24.6 10.4 %collective-permute-start = (f32[704,128]{1,0:T(8,128)S(1)}, f32[704,128]{1,0:T(8,128)S(1)}, u32[]{:S(2)}, u32[]{:S(2)}) collective-permute-start(f32[704,128]{1,0:T(8,128)S(1)} %copy-done.7), channel_id=1, source_target_pairs={{0,1},{1,2},{2,3},{3,4},{4,5},{5,6},{6,7},{7,8},{8,9},{9,10},{10,1... | collective-permute-start | bytes 1081352 | tf_op jit(solution)/shard_map/ppermute | solution.py:578
  41.7 18.5 %copy-start.3 = (f32[960,128]{1,0:T(8,128)S(1)}, f32[960,128]{1,0:T(8,128)}, u32[]{:S(2)}) copy-start(f32[960,128]{1,0:T(8,128)} %get-tuple-element.17.local_ref) | copy-start | bytes 1474564
  45.8 22.6 %all-to-all-start.1 = ((f32[16,16,128]{2,1,0:T(8,128)}), f32[16,16,128]{2,1,0:T(8,128)S(1)}, u32[]{:S(2)}, u32[]{:S(2)}) async-start(f32[16,16,128]{2,1,0:T(8,128)} %bitcast.4), calls=%async_computation.1 | async-start | bytes 262144 | tf_op jit(solution)/shard_map/all_to_all | solution.py:631
  61.7 6.8 %copy-start = (f32[64,4096]{1,0:T(8,128)S(1)}, f32[64,4096]{1,0:T(8,128)}, u32[]{:S(2)}) copy-start(f32[64,4096]{1,0:T(8,128)} %basis_ref.1) | copy-start | bytes 3145732
  61.7 6.8 %copy-start.6 = (s32[32,128]{1,0:T(8,128)S(1)}, s32[32,128]{1,0:T(8,128)}, u32[]{:S(2)}) copy-start(s32[32,128]{1,0:T(8,128)} %get-tuple-element.18.inverse_ref) | copy-start | bytes 49156

commit v4 on v3

--- a/solution.py
+++ b/solution.py
@@ -115,41 +115,31 @@
     return [2 * total_leaves - 2 * (total_leaves >> level) for level in range(levels)]
 
 
-def prepare_kernel(
-    total_leaves,
-    levels,
-    dev_ref,
+def expand_kernel(
     points_in,
     charges_in,
     basis_in,
     ordering_in,
     transfer_in,
-    coupling_in,
     pay_right_ref,
     pay_left_ref,
     message_ref,
     local_ref,
-    counts_ref,
-    inverse_ref,
-    paths_ref,
     points_ref,
     charges_ref,
     basis_ref,
     ordering_ref,
     transfer_ref,
-    coupling_ref,
     data_ref,
     edge_ref,
     arrived,
 ):
-    device = dev_ref[0]
     moves = [
         (charges_in, charges_ref),
         (points_in, points_ref),
         (ordering_in, ordering_ref),
         (transfer_in, transfer_ref),
         (basis_in, basis_ref),
-        (coupling_in, coupling_ref),
     ]
     copies = [
         pltpu.make_async_copy(source, target, arrived.at[slot])
@@ -176,17 +166,9 @@
     ]
     for copy in sent:
         copy.start()
-    copies[2].wait()
-    slots = lax.broadcasted_iota(jnp.int32, (LANES, LANES), 0)
-    numbers = lax.broadcasted_iota(jnp.int32, (16, LANES), 1).astype(jnp.float32)
-    numbers = numbers.astype(jnp.bfloat16)
-    for leaf in range(leaves):
-        hit = jnp.where(ordering_ref[leaf : leaf + 1, :] == slots, 1.0, 0.0).astype(jnp.bfloat16)
-        found = bf16_dot(numbers, hit, ((1,), (1,)))
-        inverse_ref[leaf : leaf + 1, :] = found[0:1].astype(jnp.int32)
     zero = jnp.zeros((rhs, LANES), jnp.float32)
     expansions = []
-    for copy in copies[3:]:
+    for copy in copies[2:]:
         copy.wait()
     for pair in range(leaves // 2):
         gathered = []
@@ -206,12 +188,6 @@
         expansions.append(both.reshape(2, rhs, LANES))
     current = jnp.concatenate(expansions, axis=0)
     matrix = up_matrix(transfer_ref)
-    path = matrix
-    for level in range(5, 10):
-        paths_ref[:, (level - 5) * LANES : (level - 4) * LANES] = path
-        if level < 9:
-            bit = ((device % GROUP) >> (level - 5)) & 1
-            path = dot(path[:, : LANES // 2], twice(transfer_ref[bit]))
     base = 0
     lasts, firsts = [], []
     for level in range(4):
@@ -236,6 +212,37 @@
     message = packed(current[0], current[1])
     for peer in range(message_ref.shape[0] // rhs):
         message_ref[peer * rhs : (peer + 1) * rhs, :] = message
+    for copy in sent + ends:
+        copy.wait()
+
+
+def tables_kernel(
+    total_leaves,
+    levels,
+    dev_ref,
+    ordering_ref,
+    transfer_ref,
+    coupling_ref,
+    _,
+    counts_ref,
+    inverse_ref,
+    paths_ref,
+):
+    device = dev_ref[0]
+    leaves = ordering_ref.shape[0]
+    slots = lax.broadcasted_iota(jnp.int32, (LANES, LANES), 0)
+    numbers = lax.broadcasted_iota(jnp.int32, (16, LANES), 1).astype(jnp.float32)
+    numbers = numbers.astype(jnp.bfloat16)
+    for leaf in range(leaves):
+        hit = jnp.where(ordering_ref[leaf : leaf + 1, :] == slots, 1.0, 0.0).astype(jnp.bfloat16)
+        found = bf16_dot(numbers, hit, ((1,), (1,)))
+        inverse_ref[leaf : leaf + 1, :] = found[0:1].astype(jnp.int32)
+    path = up_matrix(transfer_ref)
+    for level in range(5, 10):
+        paths_ref[:, (level - 5) * LANES : (level - 4) * LANES] = path
+        if level < 9:
+            bit = ((device % GROUP) >> (level - 5)) & 1
+            path = dot(path[:, : LANES // 2], twice(transfer_ref[bit]))
     lane = lax.broadcasted_iota(jnp.int32, (1, LANES), 1)
     starts = level_starts(total_leaves, levels)
     last = starts[-1] // LANES * LANES
@@ -265,18 +272,15 @@
             counts_ref[4 * level + slot : 4 * level + slot + 1, :] = jnp.sum(
                 hits, axis=0, keepdims=True
             )
-    for copy in sent + ends:
-        copy.wait()
 
 
 def near_kernel(
-    total_leaves, first, dev_ref, near_ref, own_ref, before_ref, after_ref, *rest
+    total_leaves, dev_ref, near_ref, own_ref, before_ref, after_ref, *rest
 ):
     out_ref, places, weights = rest[-3:]
     rhs = out_ref.shape[0]
     leaves = near_ref.shape[1]
     entries = near_ref.shape[0]
-    targets = out_ref.shape[1] // LANES
     for part, ref in enumerate((before_ref, own_ref, after_ref)):
         rows = slice(part * leaves, (part + 1) * leaves)
         axes = [
@@ -299,8 +303,7 @@
     def row_of(kind, slot):
         return places[kind, pl.ds(slot, 1), :]
 
-    def one(step, carry):
-        leaf = step + first
+    def one(leaf, carry):
         target = device * leaves + leaf
         here = [row_of(kind, leaves + leaf) for kind in range(4)]
         size = here[0] * here[0] + (here[3] + DELTA * DELTA)
@@ -335,12 +338,12 @@
             )
             total = total + bf16_dot(jnp.concatenate(sides, axis=1), piece, ((1,), (1,)))
         half = total[:, :LANES] + total[:, LANES:]
-        out_ref[:, pl.ds(pl.multiple_of(step * LANES, LANES), LANES)] = (
+        out_ref[:, pl.ds(pl.multiple_of(leaf * LANES, LANES), LANES)] = (
             half[0:rhs, :] + half[rhs : 2 * rhs, :]
         )
         return carry
 
-    lax.fori_loop(0, targets, one, 0, unroll=8)
+    lax.fori_loop(0, leaves, one, 0, unroll=8)
 
 
 def couple(window, count, level, lane0, counts_ref, x_ref, row0, rows):
@@ -390,7 +393,6 @@
     transfer_ref,
     stack_ref,
     paths_ref,
-    _,
     out_ref,
     x_ref,
     top_ref,
@@ -486,7 +488,7 @@
 
 
 def final_kernel(
-    parts_ref, terms_ref, transfer_ref, basis_ref, inverse_ref, near_a_ref, near_b_ref, out_ref
+    parts_ref, terms_ref, transfer_ref, basis_ref, inverse_ref, near_ref, out_ref
 ):
     rhs = out_ref.shape[0]
     leaves = inverse_ref.shape[0]
@@ -516,9 +518,8 @@
             leaf = 4 * four + slot
             ids = jnp.broadcast_to(inverse_ref[leaf : leaf + 1, :], (rhs, LANES))
             value = jnp.take_along_axis(far[slot * rhs : (slot + 1) * rhs], ids, axis=1)
-            near_ref = near_a_ref if leaf < leaves // 2 else near_b_ref
-            at = leaf % (leaves // 2) * LANES
-            out_ref[:, leaf * LANES : (leaf + 1) * LANES] = value + near_ref[:, at : at + LANES]
+            cols = slice(leaf * LANES, (leaf + 1) * LANES)
+            out_ref[:, cols] = value + near_ref[:, cols]
 
 
 def call(kernel, outs, scalars, operands, scratch=(), cost=None, kept=(), limit=VMEM_BYTES, far=0):
@@ -551,19 +552,16 @@
     pay_rows = data_rows + 6 * rhs
     local_rows = (leaves * 2 - 4) * rhs
 
-    inputs = [points, charges, basis, ids, transfer, coupling_list]
-    pay_right, pay_left, message, local_terms, counts, inverse, paths = call(
-        lambda *refs: prepare_kernel(total_leaves, levels, *refs),
+    inputs = [points, charges, basis, ids, transfer]
+    pay_right, pay_left, message, local_terms = call(
+        expand_kernel,
         [
             jax.ShapeDtypeStruct((pay_rows, LANES), f32),
             jax.ShapeDtypeStruct((pay_rows, LANES), f32),
             jax.ShapeDtypeStruct((groups * rhs, LANES), f32),
             jax.ShapeDtypeStruct((local_rows, LANES), f32),
-            jax.ShapeDtypeStruct((4 * levels, LANES), f32),
-            jax.ShapeDtypeStruct((leaves, LANES), jnp.int32),
-            jax.ShapeDtypeStruct((LANES, 5 * LANES), f32),
         ],
-        [device],
+        [],
         [],
         [
             *[pltpu.VMEM(array.shape, array.dtype) for array in inputs],
@@ -575,6 +573,18 @@
         limit=FIRST_BYTES,
         far=2,
     )
+    counts, inverse, paths = call(
+        lambda *refs: tables_kernel(total_leaves, levels, *refs),
+        [
+            jax.ShapeDtypeStruct((4 * levels, LANES), f32),
+            jax.ShapeDtypeStruct((leaves, LANES), jnp.int32),
+            jax.ShapeDtypeStruct((LANES, 5 * LANES), f32),
+        ],
+        [device],
+        [ids, transfer, coupling_list],
+        cost=pl.CostEstimate(flops=1 << 28, bytes_accessed=2 << 20, transcendentals=0),
+        kept=[message],
+    )
     before = lax.ppermute(pay_right, "leaf", [(i, (i + 1) % devices) for i in range(devices)])
     after = lax.ppermute(pay_left, "leaf", [((i + 1) % devices, i) for i in range(devices)])
     gathered = lax.all_to_all(
@@ -586,25 +596,6 @@
         tiled=True,
     )
 
-    def near(first, count, extra):
-        return call(
-            lambda *refs: near_kernel(total_leaves, first, *refs),
-            jax.ShapeDtypeStruct((rhs, count * LANES), f32),
-            [device, near_list],
-            [pay_right, before, after],
-            [
-                pltpu.VMEM((4, 3 * leaves, LANES), f32),
-                pltpu.VMEM((3 * leaves, 2 * rhs, LANES), jnp.bfloat16),
-            ],
-            pl.CostEstimate(
-                flops=count * 12 * 128 * 128 * 100,
-                bytes_accessed=8 << 20,
-                transcendentals=count * 12 * 128 * 128,
-            ),
-            kept=extra,
-        )
-
-    near_a = near(0, leaves // 2, [])
     terms = call(
         local_kernel,
         jax.ShapeDtypeStruct((local_rows // 2, LANES), f32),
@@ -626,7 +617,6 @@
                 for step in range(5)
             ],
         ],
-        kept=[near_a],
     )
     parts = lax.all_to_all(
         spread,
@@ -636,12 +626,27 @@
         axis_index_groups=[[g * GROUP + i for i in range(GROUP)] for g in range(groups)],
         tiled=True,
     )
-    near_b = near(leaves // 2, leaves // 2, [spread])
+    near = call(
+        lambda *refs: near_kernel(total_leaves, *refs),
+        jax.ShapeDtypeStruct((rhs, leaves * LANES), f32),
+        [device, near_list],
+        [pay_right, before, after],
+        [
+            pltpu.VMEM((4, 3 * leaves, LANES), f32),
+            pltpu.VMEM((3 * leaves, 2 * rhs, LANES), jnp.bfloat16),
+        ],
+        pl.CostEstimate(
+            flops=leaves * 12 * 128 * 128 * 100,
+            bytes_accessed=8 << 20,
+            transcendentals=leaves * 12 * 128 * 128,
+        ),
+        kept=[spread],
+    )
     return call(
         final_kernel,
         jax.ShapeDtypeStruct(charges.shape, f32),
         [],
-        [parts, terms, transfer, basis, inverse, near_a, near_b],
+        [parts, terms, transfer, basis, inverse, near],
     )
 
 

time: 70.6 us -> 62.2 us (0.88)
  starting transfers between devices: 37.1 us -> 31.3 us
  waiting for transfers between devices: 7.25 us -> 4.96 us
    all_to_all x1, starting transfers between devices: 14.4 us -> 8.73 us  [local(): lax.all_to_all(spread, 'leaf', 0, 0, axis_index_groups=[[g * GROUP + i fo...]
    all_to_all x1, waiting for transfers between devices: 0.01 us -> 4.95 us  [local(): lax.all_to_all(message, 'leaf', 0, 0, axis_index_groups=[[g * GROUP + i f...]
    ppermute x1, waiting for transfers between devices: 3.75 us -> 0.01 us  [local(): lax.ppermute(pay_right, 'leaf', [(i, (i + 1) % devices) for i in range(de...]
    ppermute x1, waiting for transfers between devices: 3.49 us -> 0.01 us  [local(): lax.ppermute(pay_left, 'leaf', [((i + 1) % devices, i) for i in range(dev...]
    ppermute x1, starting transfers between devices: 2.86 us -> 1.92 us  [local(): lax.ppermute(pay_left, 'leaf', [((i + 1) % devices, i) for i in range(dev...]
    ppermute x1, starting transfers between devices: 3.15 us -> 3.96 us  [local(): lax.ppermute(pay_right, 'leaf', [(i, (i + 1) % devices) for i in range(de...]
  transfers between devices with their start and end apart: 4 -> 4, of which waited for: 2 -> 1; matrix products, arithmetic and copies ran while one was open for 0% -> 0% of each run, Pallas kernels for 21% -> 31%
where the time goes in v4:
time: 62.2 us; the launch traced here: 61.9 us
  starting transfers between devices  31.3 us (50%)
  Pallas kernels  25.4 us (41%)
  waiting for transfers between devices  4.96 us (8%)
    pallas_call x6, Pallas kernels, call(): pl.pallas_call(kernel, out_shape=outs, in_specs=[smem] * len(scalars) + [...  25.4 us
    all_to_all x1, starting transfers between devices, local(): lax.all_to_all(message, 'leaf', 0, 0, axis_index_groups=[[g * GROUP + i f...  16.6 us
    all_to_all x1, starting transfers between devices, local(): lax.all_to_all(spread, 'leaf', 0, 0, axis_index_groups=[[g * GROUP + i fo...  8.73 us
    all_to_all x1, waiting for transfers between devices, local(): lax.all_to_all(message, 'leaf', 0, 0, axis_index_groups=[[g * GROUP + i f...  4.95 us
    ppermute x1, starting transfers between devices, local(): lax.ppermute(pay_right, 'leaf', [(i, (i + 1) % devices) for i in range(de...  3.96 us
    ppermute x1, starting transfers between devices, local(): lax.ppermute(pay_left, 'leaf', [((i + 1) % devices, i) for i in range(dev...  1.92 us
  transfers between devices with their start and end apart: 4, of which 1 were waited for; matrix products, arithmetic and copies ran while one was open for 0% of the time, Pallas kernels for 31%

profile of v4, /device:TPU:1, one launch (start us, length us, event | category | flops | bytes accessed | tf_op | source)
XLA Modules:
  0.0 61.9 jit_solution(7276829697390981462)
XLA Ops:
  0.0 4.3 %shard_map.82 = (f32[704,128]{1,0:T(8,128)}, f32[704,128]{1,0:T(8,128)}, f32[512,128]{1,0:T(8,128)}, f32[960,128]{1,0:T(8,128)}) custom-call(f32[3,4096]{1,0:T(4,128)} %points_in.1, f32[16,4096]{1,0:T(8,128)} %charges_in.1, f32[64,4096]{1,0:T(8,128)} %basis_ref.1, s32[32,128]{1,0:T(8,128)} %bitcast.9, f32[2,64,64]{2,1,0:T(8,128)} %transfer_ref.1), custom_call_target="tpu_custom_call" | custom-call | tf_op jit(solution)/shard_map/pallas_call | solution.py:529
  4.3 0.0 copy-start.1
  4.3 0.0 copy-start.4
  4.3 0.0 copy-start.5
  4.3 16.6 %all-to-all-start = ((f32[32,16,128]{2,1,0:T(8,128)}), f32[32,16,128]{2,1,0:T(8,128)S(1)}, u32[]{:S(2)}, u32[]{:S(2)}) async-start(f32[32,16,128]{2,1,0:T(8,128)} %bitcast.8), calls=%async_computation | async-start | bytes 524288 | tf_op jit(solution)/shard_map/all_to_all | solution.py:590
  21.0 4.0 %collective-permute-start = (f32[704,128]{1,0:T(8,128)}, f32[704,128]{1,0:T(8,128)S(1)}, u32[]{:S(2)}, u32[]{:S(2)}) collective-permute-start(f32[704,128]{1,0:T(8,128)} %get-tuple-element.16.refs_2_), channel_id=1, source_target_pairs={{0,1},{1,2},{2,3},{3,4},{4,5},{5,6},{6,7},{7,8},{8,9},{9,10},{10,1... | collective-permute-start | bytes 1081352 | tf_op jit(solution)/shard_map/ppermute | solution.py:588
  24.9 1.9 %collective-permute-start.1 = (f32[704,128]{1,0:T(8,128)}, f32[704,128]{1,0:T(8,128)S(1)}, u32[]{:S(2)}, u32[]{:S(2)}) collective-permute-start(f32[704,128]{1,0:T(8,128)} %get-tuple-element.17), channel_id=1, source_target_pairs={{1,0},{2,1},{3,2},{4,3},{5,4},{6,5},{7,6},{8,7},{9,8},{10,9},{11,1... | collective-permute-start | bytes 1081352 | tf_op jit(solution)/shard_map/ppermute | solution.py:589
  26.9 0.0 copy-done.6
  26.9 0.0 copy-done.1
  26.9 0.0 copy-done.4
  26.9 0.0 copy-done.5
  26.9 0.0 copy-start.2
  26.9 1.2 %shard_map.83 = (f32[48,128]{1,0:T(8,128)S(1)}, s32[32,128]{1,0:T(8,128)S(1)}, f32[128,640]{1,0:T(8,128)S(1)}) custom-call(s32[1]{0:T(128)} %bitcast.refs_0_.dev_ref, s32[32,128]{1,0:T(8,128)S(1)} %bitcast.10, f32[2,64,64]{2,1,0:T(8,128)S(1)} %copy-done.1, s32[4,32760]{1,0:T(4,128)S(1)} %copy-done.6, f32[512,128]{1,0:T(8,128)S(1)} %copy-done.4), custom_call_target="tpu_custom_call" | custom-call | flops 268435456 | bytes 2097152 | tf_op jit(solution)/shard_map/pallas_call | solution.py:529
  28.1 4.9 %all-to-all-done = f32[32,16,128]{2,1,0:T(8,128)S(1)} async-done(((f32[32,16,128]{2,1,0:T(8,128)}), f32[32,16,128]{2,1,0:T(8,128)S(1)}, u32[]{:S(2)}, u32[]{:S(2)}) %all-to-all-start) | async-done | bytes 262176 | tf_op jit(solution)/shard_map/all_to_all | solution.py:590
  33.1 4.1 %shard_map.84.refs_5_ = f32[256,128]{1,0:T(8,128)} custom-call(s32[1]{0:T(128)} %bitcast.refs_0_.dev_ref, f32[48,128]{1,0:T(8,128)S(1)} %get-tuple-element.13.refs_1_.counts_ref, f32[512,128]{1,0:T(8,128)S(1)} %bitcast.6, f32[2,64,64]{2,1,0:T(8,128)S(1)} %copy-done.1, f32[256,128]{1,0:T(8,128)S(1)} %copy-done.2, f32[128,640]{1,0:T(8,128)S(1)} %get-tuple-element.14.refs_5_), custom_call_target="tpu_custom_call" | custom-call | tf_op jit(solution)/shard_map/pallas_call | solution.py:529
  37.2 8.7 %all-to-all-start.1 = ((f32[16,16,128]{2,1,0:T(8,128)}), f32[16,16,128]{2,1,0:T(8,128)S(1)}, u32[]{:S(2)}, u32[]{:S(2)}) async-start(f32[16,16,128]{2,1,0:T(8,128)} %bitcast.4), calls=%async_computation.1 | async-start | bytes 262144 | tf_op jit(solution)/shard_map/all_to_all | solution.py:621
  45.9 0.0 collective-permute-done.before_ref.refs_3_
  45.9 0.0 collective-permute-done.1.after_ref.refs_4_
  45.9 0.0 copy-start.8
  46.0 1.4 %shard_map.85.terms_ref = f32[480,128]{1,0:T(8,128)S(1)} custom-call(s32[1]{0:T(128)} %bitcast.refs_0_.dev_ref, f32[48,128]{1,0:T(8,128)S(1)} %get-tuple-element.13.refs_1_.counts_ref, f32[960,128]{1,0:T(8,128)S(1)} %copy-done.3, f32[704,128]{1,0:T(8,128)S(1)} %collective-permute-done.before_ref.refs_3_, ...), custom_call_target="tpu_custom_call" | custom-call | tf_op jit(solution)/shard_map/pallas_call | solution.py:529
  47.4 0.0 copy-start
  47.4 12.6 %shard_map.86.near_ref = f32[16,4096]{1,0:T(8,128)S(1)} custom-call(s32[1]{0:T(128)} %bitcast.refs_0_.dev_ref, s32[12,32]{1,0:T(8,128)S(1)} %copy-done.8, f32[704,128]{1,0:T(8,128)S(1)} %copy-done.7, f32[704,128]{1,0:T(8,128)S(1)} %collective-permute-done.before_ref.refs_3_, f32[704,128]{1,0:T(8,128)S(1)} %collective-permute-done.1.after_ref.refs_4_, ...), custom_call_target="tpu_custom_call" | custom-call | flops 629145600 | bytes 8388608 | tf_op jit(solution)/shard_map/pallas_call | solution.py:529
  60.1 0.0 all-to-all-done.1
  60.1 1.8 %shard_map.87 = f32[16,4096]{1,0:T(8,128)} custom-call(f32[256,128]{1,0:T(8,128)S(1)} %bitcast.7, f32[480,128]{1,0:T(8,128)S(1)} %shard_map.85.terms_ref, f32[2,64,64]{2,1,0:T(8,128)S(1)} %copy-done.1, f32[64,4096]{1,0:T(8,128)S(1)} %copy-done, s32[32,128]{1,0:T(8,128)S(1)} %get-tuple-element.18.inverse_ref, f32[16,4096]{1,0:T(8,128)S(1)} %shard_map.86.near_ref), custom_call_target="tpu_custom_call" | custom-call | tf_op jit(solution)/shard_map/pallas_call | solution.py:529
  (8 shorter events, 0.0 us)
Async XLA Ops:
  0.0 26.9 %copy-start.6 = (s32[4,32760]{1,0:T(4,128)S(1)}, s32[4,32760]{1,0:T(4,128)}, u32[]{:S(2)}) copy-start(s32[4,32760]{1,0:T(4,128)} %refs_3_.2) | copy-start | bytes 1572484
  4.3 22.6 %copy-start.1 = (f32[2,64,64]{2,1,0:T(8,128)S(1)}, f32[2,64,64]{2,1,0:T(8,128)}, u32[]{:S(2)}) copy-start(f32[2,64,64]{2,1,0:T(8,128)} %transfer_ref.1) | copy-start | bytes 98308
  4.3 22.6 %copy-start.4 = (f32[512,128]{1,0:T(8,128)S(1)}, f32[512,128]{1,0:T(8,128)}, u32[]{:S(2)}) copy-start(f32[512,128]{1,0:T(8,128)} %get-tuple-element.12.refs_4_) | copy-start | bytes 786436
  4.3 22.6 %copy-start.5 = (s32[4096]{0:T(1024)S(1)}, s32[4096]{0:T(1024)}, u32[]{:S(2)}) copy-start(s32[4096]{0:T(1024)} %param.14) | copy-start | bytes 49156
  4.3 28.8 %all-to-all-start = ((f32[32,16,128]{2,1,0:T(8,128)}), f32[32,16,128]{2,1,0:T(8,128)S(1)}, u32[]{:S(2)}, u32[]{:S(2)}) async-start(f32[32,16,128]{2,1,0:T(8,128)} %bitcast.8), calls=%async_computation | async-start | bytes 524288 | tf_op jit(solution)/shard_map/all_to_all | solution.py:590
  21.0 24.9 %collective-permute-start = (f32[704,128]{1,0:T(8,128)}, f32[704,128]{1,0:T(8,128)S(1)}, u32[]{:S(2)}, u32[]{:S(2)}) collective-permute-start(f32[704,128]{1,0:T(8,128)} %get-tuple-element.16.refs_2_), channel_id=1, source_target_pairs={{0,1},{1,2},{2,3},{3,4},{4,5},{5,6},{6,7},{7,8},{8,9},{9,10},{10,1... | collective-permute-start | bytes 1081352 | tf_op jit(solution)/shard_map/ppermute | solution.py:588
  24.9 21.0 %collective-permute-start.1 = (f32[704,128]{1,0:T(8,128)}, f32[704,128]{1,0:T(8,128)S(1)}, u32[]{:S(2)}, u32[]{:S(2)}) collective-permute-start(f32[704,128]{1,0:T(8,128)} %get-tuple-element.17), channel_id=1, source_target_pairs={{1,0},{2,1},{3,2},{4,3},{5,4},{6,5},{7,6},{8,7},{9,8},{10,9},{11,1... | collective-permute-start | bytes 1081352 | tf_op jit(solution)/shard_map/ppermute | solution.py:589
  26.9 6.2 %copy-start.2 = (f32[256,128]{1,0:T(8,128)S(1)}, f32[256,128]{1,0:T(8,128)}, u32[]{:S(2)}) copy-start(f32[256,128]{1,0:T(8,128)} %constant.6.clone.refs_4_.stack_ref) | copy-start | bytes 393220
  33.1 12.8 %copy-start.3 = (f32[960,128]{1,0:T(8,128)S(1)}, f32[960,128]{1,0:T(8,128)}, u32[]{:S(2)}) copy-start(f32[960,128]{1,0:T(8,128)} %get-tuple-element.15.local_ref) | copy-start | bytes 1474564
  37.2 22.9 %all-to-all-start.1 = ((f32[16,16,128]{2,1,0:T(8,128)}), f32[16,16,128]{2,1,0:T(8,128)S(1)}, u32[]{:S(2)}, u32[]{:S(2)}) async-start(f32[16,16,128]{2,1,0:T(8,128)} %bitcast.4), calls=%async_computation.1 | async-start | bytes 262144 | tf_op jit(solution)/shard_map/all_to_all | solution.py:621
  45.9 1.4 %copy-start.7 = (f32[704,128]{1,0:T(8,128)S(1)}, f32[704,128]{1,0:T(8,128)}, u32[]{:S(2)}) copy-start(f32[704,128]{1,0:T(8,128)} %get-tuple-element.16.refs_2_) | copy-start | bytes 1081348
  45.9 1.4 %copy-start.8 = (s32[12,32]{1,0:T(8,128)S(1)}, s32[12,32]{1,0:T(8,128)}, u32[]{:S(2)}) copy-start(s32[12,32]{1,0:T(8,128)} %refs_1_.1) | copy-start | bytes 4612
  47.4 12.7 %copy-start = (f32[64,4096]{1,0:T(8,128)S(1)}, f32[64,4096]{1,0:T(8,128)}, u32[]{:S(2)}) copy-start(f32[64,4096]{1,0:T(8,128)} %basis_ref.1) | copy-start | bytes 3145732

commit v5 on v4

--- a/solution.py
+++ b/solution.py
@@ -14,6 +14,7 @@
 PROXY = 0.35
 GROUP = 16
 LANES = 128
+TOP = GROUP.bit_length() + 4
 VMEM_BYTES = 50 * 1024 * 1024
 FIRST_BYTES = 61 * 1024 * 1024
 
@@ -116,30 +117,24 @@
 
 
 def expand_kernel(
-    points_in,
     charges_in,
+    ordering_in,
     basis_in,
-    ordering_in,
     transfer_in,
-    pay_right_ref,
-    pay_left_ref,
+    local_out,
     message_ref,
+    charges_ref,
+    ordering_ref,
+    basis_ref,
+    transfer_ref,
     local_ref,
-    points_ref,
-    charges_ref,
-    basis_ref,
-    ordering_ref,
-    transfer_ref,
-    data_ref,
-    edge_ref,
     arrived,
 ):
     moves = [
         (charges_in, charges_ref),
-        (points_in, points_ref),
         (ordering_in, ordering_ref),
+        (basis_in, basis_ref),
         (transfer_in, transfer_ref),
-        (basis_in, basis_ref),
     ]
     copies = [
         pltpu.make_async_copy(source, target, arrived.at[slot])
@@ -147,29 +142,12 @@
     ]
     for copy in copies:
         copy.start()
+    for copy in copies:
+        copy.wait()
     rhs = charges_ref.shape[0]
     leaves = ordering_ref.shape[0]
-    data_rows = leaves * (rhs + 3)
-    copies[0].wait()
-    copies[1].wait()
-    for leaf in range(leaves):
-        cols = slice(leaf * LANES, (leaf + 1) * LANES)
-        data_ref[leaf * rhs : (leaf + 1) * rhs, :] = charges_ref[:, cols]
-        for axis in range(3):
-            at = leaves * (rhs + axis) + leaf
-            data_ref[at : at + 1, :] = points_ref[axis : axis + 1, cols]
-    sent = [
-        pltpu.make_async_copy(
-            data_ref, target.at[pl.ds(0, data_rows), :], arrived.at[len(moves) + slot]
-        )
-        for slot, target in enumerate((pay_right_ref, pay_left_ref))
-    ]
-    for copy in sent:
-        copy.start()
     zero = jnp.zeros((rhs, LANES), jnp.float32)
     expansions = []
-    for copy in copies[2:]:
-        copy.wait()
     for pair in range(leaves // 2):
         gathered = []
         for leaf in (2 * pair, 2 * pair + 1):
@@ -189,30 +167,22 @@
     current = jnp.concatenate(expansions, axis=0)
     matrix = up_matrix(transfer_ref)
     base = 0
-    lasts, firsts = [], []
+    sent = []
     for level in range(4):
-        count = leaves >> level
-        local_ref[base : base + count * rhs, :] = current.reshape(count * rhs, LANES)
-        lasts.append(current[count - 3 :])
-        firsts.append(current[:3])
-        base += count * rhs
+        size = (leaves >> level) * rhs
+        local_ref[base : base + size, :] = current.reshape(size, LANES)
+        rows = pl.ds(base, size)
+        copy = pltpu.make_async_copy(
+            local_ref.at[rows, :], local_out.at[rows, :], arrived.at[len(moves) + level]
+        )
+        copy.start()
+        sent.append(copy)
+        base += size
         current = up(current, matrix)
-    for slot, edges in enumerate((lasts, firsts)):
-        edge_ref[slot] = paired(jnp.concatenate(edges, axis=0)).reshape(6 * rhs, LANES)
-    ends = [
-        pltpu.make_async_copy(
-            edge_ref.at[slot],
-            target.at[pl.ds(data_rows, 6 * rhs), :],
-            arrived.at[len(moves) + 2 + slot],
-        )
-        for slot, target in enumerate((pay_right_ref, pay_left_ref))
-    ]
-    for copy in ends:
-        copy.start()
     message = packed(current[0], current[1])
     for peer in range(message_ref.shape[0] // rhs):
         message_ref[peer * rhs : (peer + 1) * rhs, :] = message
-    for copy in sent + ends:
+    for copy in sent:
         copy.wait()
 
 
@@ -220,16 +190,38 @@
     total_leaves,
     levels,
     dev_ref,
+    points_ref,
+    charges_ref,
     ordering_ref,
     transfer_ref,
     coupling_ref,
-    _,
+    local_ref,
+    pay_right_ref,
+    pay_left_ref,
     counts_ref,
     inverse_ref,
     paths_ref,
 ):
     device = dev_ref[0]
+    rhs = charges_ref.shape[0]
     leaves = ordering_ref.shape[0]
+    for leaf in range(leaves):
+        cols = slice(leaf * LANES, (leaf + 1) * LANES)
+        for ref in (pay_right_ref, pay_left_ref):
+            ref[leaf * rhs : (leaf + 1) * rhs, :] = charges_ref[:, cols]
+            for axis in range(3):
+                at = leaves * (rhs + axis) + leaf
+                ref[at : at + 1, :] = points_ref[axis : axis + 1, cols]
+    for ref, skip in ((pay_right_ref, True), (pay_left_ref, False)):
+        edges = []
+        base = 0
+        for level in range(4):
+            count = leaves >> level
+            start = base + (count - 3) * rhs if skip else base
+            edges.append(local_ref[start : start + 3 * rhs, :].reshape(3, rhs, LANES))
+            base += count * rhs
+        pairs = paired(jnp.concatenate(edges, axis=0))
+        ref[leaves * (rhs + 3) :, :] = pairs.reshape(6 * rhs, LANES)
     slots = lax.broadcasted_iota(jnp.int32, (LANES, LANES), 0)
     numbers = lax.broadcasted_iota(jnp.int32, (16, LANES), 1).astype(jnp.float32)
     numbers = numbers.astype(jnp.bfloat16)
@@ -238,9 +230,9 @@
         found = bf16_dot(numbers, hit, ((1,), (1,)))
         inverse_ref[leaf : leaf + 1, :] = found[0:1].astype(jnp.int32)
     path = up_matrix(transfer_ref)
-    for level in range(5, 10):
+    for level in range(5, TOP + 1):
         paths_ref[:, (level - 5) * LANES : (level - 4) * LANES] = path
-        if level < 9:
+        if level < TOP:
             bit = ((device % GROUP) >> (level - 5)) & 1
             path = dot(path[:, : LANES // 2], twice(transfer_ref[bit]))
     lane = lax.broadcasted_iota(jnp.int32, (1, LANES), 1)
@@ -275,12 +267,14 @@
 
 
 def near_kernel(
-    total_leaves, dev_ref, near_ref, own_ref, before_ref, after_ref, *rest
+    total_leaves, dev_ref, near_in, own_ref, before_ref, after_ref, *rest
 ):
-    out_ref, places, weights = rest[-3:]
+    out_ref, places, weights, near_ref, arrived = rest[-5:]
+    copy = pltpu.make_async_copy(near_in, near_ref, arrived)
+    copy.start()
     rhs = out_ref.shape[0]
-    leaves = near_ref.shape[1]
-    entries = near_ref.shape[0]
+    leaves = near_in.shape[1]
+    entries = near_in.shape[0]
     for part, ref in enumerate((before_ref, own_ref, after_ref)):
         rows = slice(part * leaves, (part + 1) * leaves)
         axes = [
@@ -297,6 +291,7 @@
 
         lax.fori_loop(0, leaves, fill, 0, unroll=8)
 
+    copy.wait()
     device = dev_ref[0]
     half_cycle = total_leaves // 2
 
@@ -343,7 +338,7 @@
         )
         return carry
 
-    lax.fori_loop(0, leaves, one, 0, unroll=8)
+    lax.fori_loop(0, leaves, one, 0, unroll=16)
 
 
 def couple(window, count, level, lane0, counts_ref, x_ref, row0, rows):
@@ -358,8 +353,20 @@
 
 
 def local_kernel(
-    dev_ref, counts_ref, local_ref, before_ref, after_ref, stack_ref, out_ref, x_ref, edge_ref
+    dev_ref,
+    counts_in,
+    local_ref,
+    before_ref,
+    after_ref,
+    stack_ref,
+    out_ref,
+    x_ref,
+    edge_ref,
+    counts_ref,
+    arrived,
 ):
+    copy = pltpu.make_async_copy(counts_in, counts_ref, arrived)
+    copy.start()
     device = dev_ref[0]
     rhs = local_ref.shape[0] // 60
     start = before_ref.shape[0] - 6 * rhs
@@ -367,6 +374,7 @@
         for pair in range(6):
             both = ref[start + pair * rhs : start + (pair + 1) * rhs, :]
             edge_ref[side, 2 * pair], edge_ref[side, 2 * pair + 1] = unpacked(both)
+    copy.wait()
     base = 0
     for level in range(4):
         count = 32 >> level
@@ -387,8 +395,9 @@
 
 def upper_kernel(
     total_leaves,
+    levels,
     dev_ref,
-    counts_ref,
+    counts_in,
     gathered_ref,
     transfer_ref,
     stack_ref,
@@ -396,8 +405,12 @@
     out_ref,
     x_ref,
     top_ref,
+    counts_ref,
+    arrived,
     *sparse,
 ):
+    copy = pltpu.make_async_copy(counts_in, counts_ref, arrived)
+    copy.start()
     device = dev_ref[0]
     index = device % GROUP
     group = device // GROUP
@@ -406,12 +419,13 @@
     matrix = up_matrix(transfer_ref)
     half = LANES // 2
 
-    level9 = dot(gathered_ref[...], paths_ref[:, 4 * LANES :]).reshape(groups, rhs, LANES)
-    level10 = up(level9, matrix)
-    level11 = up(level10, matrix)
-    top_ref[0:groups] = level9
-    top_ref[groups : groups + groups // 2] = level10
-    top_ref[groups + groups // 2 : groups + groups // 2 + groups // 4] = level11
+    current = dot(gathered_ref[...], paths_ref[:, (TOP - 5) * LANES :]).reshape(groups, rhs, LANES)
+    base = 0
+    for level in range(TOP, levels):
+        top_ref[base : base + current.shape[0]] = current
+        base += current.shape[0]
+        if level < levels - 1:
+            current = up(current, matrix)
 
     beside = [
         gathered_ref[pl.ds(pl.multiple_of(((group + step) & (groups - 1)) * rhs, 8), rhs), :]
@@ -427,8 +441,8 @@
     for step in (-1, 0, 1):
         for side, value in enumerate(unpacked(beside[step + 2])):
             place(sparse[0], 2 * GROUP, step * 2 * GROUP + 2 * index + side, value)
-    nearby = dot(jnp.concatenate(beside, axis=0), paths_ref[:, : 4 * LANES])
-    for level in range(5, 9):
+    nearby = dot(jnp.concatenate(beside, axis=0), paths_ref[:, : (TOP - 5) * LANES])
+    for level in range(5, TOP):
         count = 2 * GROUP >> (level - 4)
         reach = (-1, 0, 1) if count >= 3 else (-2, -1, 0, 1, 2)
         for step in reach:
@@ -439,27 +453,33 @@
                 nearby[(step + 2) * rhs : (step + 3) * rhs, (level - 5) * LANES :][:, :LANES],
             )
 
+    starts = level_starts(total_leaves, levels)
+    last = starts[-1] // LANES * LANES
+
+    def lane_of(level, cluster):
+        return cluster + starts[level] - last if starts[level] >= last else cluster & (LANES - 1)
+
+    copy.wait()
     row0 = 0
     spans = []
-    for level in range(4, 9):
+    for level in range(4, TOP):
         count = 2 * GROUP >> (level - 4)
         ref = sparse[level - 4]
-        lane0 = (group * count) & (LANES - 1)
+        lane0 = lane_of(level, group * count)
         couple(
             lambda t, slot, ref=ref: ref[t + 3], count, level, lane0, counts_ref, x_ref, row0, rhs
         )
         spans.append((row0, count))
         row0 += count * rhs
-    lane_base = LANES // 2
     top_base = 0
-    for level in range(9, 12):
-        clusters = groups >> (level - 9)
-        cluster = group >> (level - 9)
+    for level in range(TOP, levels):
+        clusters = groups >> (level - TOP)
+        cluster = group >> (level - TOP)
         couple(
             lambda t, slot: top_ref[top_base + ((cluster + t) & (clusters - 1))],
             1,
             level,
-            lane_base + cluster,
+            lane_of(level, cluster),
             counts_ref,
             x_ref,
             row0,
@@ -467,7 +487,6 @@
         )
         spans.append((row0, 1))
         row0 += rhs
-        lane_base += clusters
         top_base += clusters
     terms = dot(x_ref[...], stack_ref[...])
 
@@ -475,14 +494,14 @@
         start, count = spans[level - 4]
         return terms[start : start + count * rhs].reshape(count, rhs, LANES)
 
-    current = term(11)[0]
-    for level in (10, 9):
-        child = (group >> (level - 9)) & 1
+    current = term(levels - 1)[0]
+    for level in range(levels - 2, TOP - 1, -1):
+        child = (group >> (level - TOP)) & 1
         current = term(level)[0] + down(current, transfer_ref[child])
     both = jnp.concatenate([transfer_ref[0], transfer_ref[1]], axis=0)
-    current = (dot_t(current[:, :half], both) + paired(term(8))[0])[None]
+    current = (dot_t(current[:, :half], both) + paired(term(TOP - 1))[0])[None]
     matrix = down_matrix(transfer_ref)
-    for level in (7, 6, 5, 4):
+    for level in range(TOP - 2, 3, -1):
         current = paired(term(level)) + down_pairs(current, matrix)
     out_ref[...] = current.reshape(out_ref.shape)
 
@@ -548,42 +567,39 @@
     f32 = jnp.float32
     ids = ordering.reshape(leaves, LANES)
     stack = jnp.asarray(coupling_stack())
-    data_rows = leaves * (rhs + 3)
-    pay_rows = data_rows + 6 * rhs
+    pay_rows = leaves * (rhs + 3) + 6 * rhs
     local_rows = (leaves * 2 - 4) * rhs
 
-    inputs = [points, charges, basis, ids, transfer]
-    pay_right, pay_left, message, local_terms = call(
+    inputs = [charges, ids, basis, transfer]
+    local_terms, message = call(
         expand_kernel,
         [
-            jax.ShapeDtypeStruct((pay_rows, LANES), f32),
-            jax.ShapeDtypeStruct((pay_rows, LANES), f32),
+            jax.ShapeDtypeStruct((local_rows, LANES), f32),
             jax.ShapeDtypeStruct((groups * rhs, LANES), f32),
-            jax.ShapeDtypeStruct((local_rows, LANES), f32),
         ],
         [],
         [],
         [
             *[pltpu.VMEM(array.shape, array.dtype) for array in inputs],
-            pltpu.VMEM((data_rows, LANES), f32),
-            pltpu.VMEM((2, 6 * rhs, LANES), f32),
+            pltpu.VMEM((local_rows, LANES), f32),
             pltpu.SemaphoreType.DMA((len(inputs) + 4,)),
         ],
         kept=inputs,
         limit=FIRST_BYTES,
-        far=2,
-    )
-    counts, inverse, paths = call(
+        far=1,
+    )
+    pay_right, pay_left, counts, inverse, paths = call(
         lambda *refs: tables_kernel(total_leaves, levels, *refs),
         [
+            jax.ShapeDtypeStruct((pay_rows, LANES), f32),
+            jax.ShapeDtypeStruct((pay_rows, LANES), f32),
             jax.ShapeDtypeStruct((4 * levels, LANES), f32),
             jax.ShapeDtypeStruct((leaves, LANES), jnp.int32),
-            jax.ShapeDtypeStruct((LANES, 5 * LANES), f32),
+            jax.ShapeDtypeStruct((LANES, (TOP - 4) * LANES), f32),
         ],
         [device],
-        [ids, transfer, coupling_list],
+        [points, charges, ids, transfer, coupling_list, local_terms],
         cost=pl.CostEstimate(flops=1 << 28, bytes_accessed=2 << 20, transcendentals=0),
-        kept=[message],
     )
     before = lax.ppermute(pay_right, "leaf", [(i, (i + 1) % devices) for i in range(devices)])
     after = lax.ppermute(pay_left, "leaf", [((i + 1) % devices, i) for i in range(devices)])
@@ -599,22 +615,29 @@
     terms = call(
         local_kernel,
         jax.ShapeDtypeStruct((local_rows // 2, LANES), f32),
-        [device, counts],
-        [local_terms, before, after, stack],
-        [pltpu.VMEM((local_rows, 2 * LANES), f32), pltpu.VMEM((2, 12, rhs, LANES), f32)],
-    )
-    upper_rows = (4 * GROUP - 2 + 3) * rhs
+        [device],
+        [counts, local_terms, before, after, stack],
+        [
+            pltpu.VMEM((local_rows, 2 * LANES), f32),
+            pltpu.VMEM((2, 12, rhs, LANES), f32),
+            pltpu.SMEM(counts.shape, f32),
+            pltpu.SemaphoreType.DMA,
+        ],
+    )
+    upper_rows = (4 * GROUP - 2 + levels - TOP) * rhs
     spread = call(
-        lambda *refs: upper_kernel(total_leaves, *refs),
+        lambda *refs: upper_kernel(total_leaves, levels, *refs),
         jax.ShapeDtypeStruct((GROUP * rhs, LANES), f32),
-        [device, counts],
-        [gathered, transfer, stack, paths],
+        [device],
+        [counts, gathered, transfer, stack, paths],
         [
             pltpu.VMEM((upper_rows, 2 * LANES), f32),
             pltpu.VMEM((2 * groups, rhs, LANES), f32),
+            pltpu.SMEM(counts.shape, f32),
+            pltpu.SemaphoreType.DMA,
             *[
                 pltpu.VMEM(((2 * GROUP >> step) + 7, rhs, LANES), f32)
-                for step in range(5)
+                for step in range(TOP - 4)
             ],
         ],
     )
@@ -629,11 +652,13 @@
     near = call(
         lambda *refs: near_kernel(total_leaves, *refs),
         jax.ShapeDtypeStruct((rhs, leaves * LANES), f32),
-        [device, near_list],
-        [pay_right, before, after],
+        [device],
+        [near_list, pay_right, before, after],
         [
             pltpu.VMEM((4, 3 * leaves, LANES), f32),
             pltpu.VMEM((3 * leaves, 2 * rhs, LANES), jnp.bfloat16),
+            pltpu.SMEM(near_list.shape, jnp.int32),
+            pltpu.SemaphoreType.DMA,
         ],
         pl.CostEstimate(
             flops=leaves * 12 * 128 * 128 * 100,

time: 62.2 us -> 61.2 us (0.984)
  Pallas kernels: 25.4 us -> 24.4 us
    pallas_call x6, Pallas kernels: 25.4 us -> 24.4 us  [call(): pl.pallas_call(kernel, out_shape=outs, in_specs=[smem] * len(scalars) + [...]
  transfers between devices with their start and end apart: 4 -> 4, of which waited for: 1 -> 1; matrix products, arithmetic and copies ran while one was open for 0% -> 0% of each run, Pallas kernels for 31% -> 30%
where the time goes in v5:
time: 61.2 us; the launch traced here: 60.9 us
  starting transfers between devices  31.4 us (51%)
  Pallas kernels  24.4 us (40%)
  waiting for transfers between devices  4.86 us (8%)
    pallas_call x6, Pallas kernels, call(): pl.pallas_call(kernel, out_shape=outs, in_specs=[smem] * len(scalars) + [...  24.4 us
    all_to_all x1, starting transfers between devices, local(): lax.all_to_all(message, 'leaf', 0, 0, axis_index_groups=[[g * GROUP + i f...  16.7 us
    all_to_all x1, starting transfers between devices, local(): lax.all_to_all(spread, 'leaf', 0, 0, axis_index_groups=[[g * GROUP + i fo...  8.84 us
    all_to_all x1, waiting for transfers between devices, local(): lax.all_to_all(message, 'leaf', 0, 0, axis_index_groups=[[g * GROUP + i f...  4.86 us
    ppermute x1, starting transfers between devices, local(): lax.ppermute(pay_right, 'leaf', [(i, (i + 1) % devices) for i in range(de...  3.96 us
    ppermute x1, starting transfers between devices, local(): lax.ppermute(pay_left, 'leaf', [((i + 1) % devices, i) for i in range(dev...  1.92 us
  transfers between devices with their start and end apart: 4, of which 1 were waited for; matrix products, arithmetic and copies ran while one was open for 0% of the time, Pallas kernels for 30%

profile of v5, /device:TPU:1, one launch (start us, length us, event | category | flops | bytes accessed | tf_op | source)
XLA Modules:
  0.0 60.9 jit_solution(12673540814394721801)
XLA Ops:
  0.0 0.0 copy-start.7
  0.0 4.0 %shard_map.82 = (f32[960,128]{1,0:T(8,128)}, f32[512,128]{1,0:T(8,128)}) custom-call(f32[16,4096]{1,0:T(8,128)} %refs_2_.1, s32[32,128]{1,0:T(8,128)} %bitcast.8, f32[64,4096]{1,0:T(8,128)} %basis_ref.1, f32[2,64,64]{2,1,0:T(8,128)} %transfer_ref.1), custom_call_target="tpu_custom_call" | custom-call | tf_op jit(solution)/shard_map/pallas_call | solution.py:548
  4.1 0.0 copy-start.1
  4.1 0.0 copy-start.6
  4.1 16.7 %all-to-all-start = ((f32[32,16,128]{2,1,0:T(8,128)}), f32[32,16,128]{2,1,0:T(8,128)S(1)}, u32[]{:S(2)}, u32[]{:S(2)}) async-start(f32[32,16,128]{2,1,0:T(8,128)} %bitcast.10), calls=%async_computation | async-start | bytes 524288 | tf_op jit(solution)/shard_map/all_to_all | solution.py:606
  20.7 0.0 copy-done.2
  20.8 0.0 copy-done.3
  20.8 0.0 copy-done.5
  20.8 0.0 copy-done.7
  20.8 0.0 copy-start.4
  20.8 1.3 %shard_map.83 = (f32[704,128]{1,0:T(8,128)S(1)}, f32[704,128]{1,0:T(8,128)S(1)}, f32[48,128]{1,0:T(8,128)S(1)}, s32[32,128]{1,0:T(8,128)S(1)}, f32[128,640]{1,0:T(8,128)S(1)}) custom-call(s32[1]{0:T(128)} %bitcast.refs_0_.dev_ref, f32[3,4096]{1,0:T(4,128)S(1)} %copy-done.7, f32[16,4096]{1,0:T(8,128)S(1)} %copy-done.2, s32[32,128]{1,0:T(8,128)S(1)} %bitcast.9, ...), custom_call_target="tpu_custom_call" | custom-call | flops 268435456 | bytes 2097152 | tf_op jit(solution)/shard_map/pallas_call | solution.py:548
  22.1 4.0 %collective-permute-start = (f32[704,128]{1,0:T(8,128)S(1)}, f32[704,128]{1,0:T(8,128)S(1)}, u32[]{:S(2)}, u32[]{:S(2)}) collective-permute-start(f32[704,128]{1,0:T(8,128)S(1)} %get-tuple-element.16.refs_2_), channel_id=1, source_target_pairs={{0,1},{1,2},{2,3},{3,4},{4,5},{5,6},{6,7},{7,8},{8,9},{9,10},{10,1... | collective-permute-start | bytes 1081352 | tf_op jit(solution)/shard_map/ppermute | solution.py:604
  26.0 1.9 %collective-permute-start.1 = (f32[704,128]{1,0:T(8,128)S(1)}, f32[704,128]{1,0:T(8,128)S(1)}, u32[]{:S(2)}, u32[]{:S(2)}) collective-permute-start(f32[704,128]{1,0:T(8,128)S(1)} %get-tuple-element.17), channel_id=1, source_target_pairs={{1,0},{2,1},{3,2},{4,3},{5,4},{6,5},{7,6},{8,7},{9,8},{10,9},{11,1... | collective-permute-start | bytes 1081352 | tf_op jit(solution)/shard_map/ppermute | solution.py:605
  28.0 4.9 %all-to-all-done = f32[32,16,128]{2,1,0:T(8,128)S(1)} async-done(((f32[32,16,128]{2,1,0:T(8,128)}), f32[32,16,128]{2,1,0:T(8,128)S(1)}, u32[]{:S(2)}, u32[]{:S(2)}) %all-to-all-start) | async-done | bytes 262176 | tf_op jit(solution)/shard_map/all_to_all | solution.py:606
  32.8 4.2 %shard_map.84.refs_5_ = f32[256,128]{1,0:T(8,128)} custom-call(s32[1]{0:T(128)} %bitcast.refs_0_.dev_ref, f32[48,128]{1,0:T(8,128)S(1)} %get-tuple-element.13.refs_1_.counts_in, f32[512,128]{1,0:T(8,128)S(1)} %bitcast.6, f32[2,64,64]{2,1,0:T(8,128)S(1)} %copy-done.3, f32[256,128]{1,0:T(8,128)S(1)} %copy-done.4, f32[128,640]{1,0:T(8,128)S(1)} %get-tuple-element.15.refs_5_), custom_call_target="tpu_custom_call" | custom-call | tf_op jit(solution)/shard_map/pallas_call | solution.py:548
  37.0 8.8 %all-to-all-start.1 = ((f32[16,16,128]{2,1,0:T(8,128)}), f32[16,16,128]{2,1,0:T(8,128)S(1)}, u32[]{:S(2)}, u32[]{:S(2)}) async-start(f32[16,16,128]{2,1,0:T(8,128)} %bitcast.4), calls=%async_computation.1 | async-start | bytes 262144 | tf_op jit(solution)/shard_map/all_to_all | solution.py:644
  45.9 0.0 collective-permute-done.before_ref.refs_3_
  45.9 0.0 collective-permute-done.1.after_ref.refs_4_
  45.9 1.4 %shard_map.85.terms_ref = f32[480,128]{1,0:T(8,128)S(1)} custom-call(s32[1]{0:T(128)} %bitcast.refs_0_.dev_ref, f32[48,128]{1,0:T(8,128)S(1)} %get-tuple-element.13.refs_1_.counts_in, f32[960,128]{1,0:T(8,128)S(1)} %copy-done.1, f32[704,128]{1,0:T(8,128)S(1)} %collective-permute-done.before_ref.refs_3_, ...), custom_call_target="tpu_custom_call" | custom-call | tf_op jit(solution)/shard_map/pallas_call | solution.py:548
  47.3 0.0 copy-start
  47.3 11.7 %shard_map.86.near_ref = f32[16,4096]{1,0:T(8,128)S(1)} custom-call(s32[1]{0:T(128)} %bitcast.refs_0_.dev_ref, s32[12,32]{1,0:T(8,128)S(1)} %copy-done.8, f32[704,128]{1,0:T(8,128)S(1)} %get-tuple-element.16.refs_2_, f32[704,128]{1,0:T(8,128)S(1)} %collective-permute-done.before_ref.refs_3_, f32[704,128]{1,0:T(8,128)S(1)} %collective-permute-done.1.after_ref.refs_4_, ...), custom_call_target="tpu_custom_call" | custom-call | flops 629145600 | bytes 8388608 | tf_op jit(solution)/shard_map/pallas_call | solution.py:548
  59.0 0.0 all-to-all-done.1
  59.0 0.0 copy-done
  59.1 1.8 %shard_map.87 = f32[16,4096]{1,0:T(8,128)} custom-call(f32[256,128]{1,0:T(8,128)S(1)} %bitcast.7, f32[480,128]{1,0:T(8,128)S(1)} %shard_map.85.terms_ref, f32[2,64,64]{2,1,0:T(8,128)S(1)} %copy-done.3, f32[64,4096]{1,0:T(8,128)S(1)} %copy-done, s32[32,128]{1,0:T(8,128)S(1)} %get-tuple-element.18.inverse_ref, f32[16,4096]{1,0:T(8,128)S(1)} %shard_map.86.near_ref), custom_call_target="tpu_custom_call" | custom-call | tf_op jit(solution)/shard_map/pallas_call | solution.py:548
  (8 shorter events, 0.0 us)
Async XLA Ops:
  0.0 20.7 %copy-start.2 = (f32[16,4096]{1,0:T(8,128)S(1)}, f32[16,4096]{1,0:T(8,128)}, u32[]{:S(2)}) copy-start(f32[16,4096]{1,0:T(8,128)} %refs_2_.1) | copy-start | bytes 786436
  0.0 20.7 %copy-start.3 = (f32[2,64,64]{2,1,0:T(8,128)S(1)}, f32[2,64,64]{2,1,0:T(8,128)}, u32[]{:S(2)}) copy-start(f32[2,64,64]{2,1,0:T(8,128)} %transfer_ref.1) | copy-start | bytes 98308
  0.0 20.8 %copy-start.5 = (s32[4,32760]{1,0:T(4,128)S(1)}, s32[4,32760]{1,0:T(4,128)}, u32[]{:S(2)}) copy-start(s32[4,32760]{1,0:T(4,128)} %refs_5_.1) | copy-start | bytes 1572484
  0.0 20.8 %copy-start.7 = (f32[3,4096]{1,0:T(4,128)S(1)}, f32[3,4096]{1,0:T(4,128)}, u32[]{:S(2)}) copy-start(f32[3,4096]{1,0:T(4,128)} %refs_1_.2) | copy-start | bytes 147460
  4.1 16.7 %copy-start.1 = (f32[960,128]{1,0:T(8,128)S(1)}, f32[960,128]{1,0:T(8,128)}, u32[]{:S(2)}) copy-start(f32[960,128]{1,0:T(8,128)} %get-tuple-element.12.refs_6_.local_ref) | copy-start | bytes 1474564
  4.1 16.7 %copy-start.6 = (s32[4096]{0:T(1024)S(1)}, s32[4096]{0:T(1024)}, u32[]{:S(2)}) copy-start(s32[4096]{0:T(1024)} %param.14) | copy-start | bytes 49156
  4.1 28.8 %all-to-all-start = ((f32[32,16,128]{2,1,0:T(8,128)}), f32[32,16,128]{2,1,0:T(8,128)S(1)}, u32[]{:S(2)}, u32[]{:S(2)}) async-start(f32[32,16,128]{2,1,0:T(8,128)} %bitcast.10), calls=%async_computation | async-start | bytes 524288 | tf_op jit(solution)/shard_map/all_to_all | solution.py:606
  20.8 12.0 %copy-start.4 = (f32[256,128]{1,0:T(8,128)S(1)}, f32[256,128]{1,0:T(8,128)}, u32[]{:S(2)}) copy-start(f32[256,128]{1,0:T(8,128)} %constant.6.clone.refs_4_.stack_ref) | copy-start | bytes 393220
  22.1 23.8 %collective-permute-start = (f32[704,128]{1,0:T(8,128)S(1)}, f32[704,128]{1,0:T(8,128)S(1)}, u32[]{:S(2)}, u32[]{:S(2)}) collective-permute-start(f32[704,128]{1,0:T(8,128)S(1)} %get-tuple-element.16.refs_2_), channel_id=1, source_target_pairs={{0,1},{1,2},{2,3},{3,4},{4,5},{5,6},{6,7},{7,8},{8,9},{9,10},{10,1... | collective-permute-start | bytes 1081352 | tf_op jit(solution)/shard_map/ppermute | solution.py:604
  26.0 19.8 %collective-permute-start.1 = (f32[704,128]{1,0:T(8,128)S(1)}, f32[704,128]{1,0:T(8,128)S(1)}, u32[]{:S(2)}, u32[]{:S(2)}) collective-permute-start(f32[704,128]{1,0:T(8,128)S(1)} %get-tuple-element.17), channel_id=1, source_target_pairs={{1,0},{2,1},{3,2},{4,3},{5,4},{6,5},{7,6},{8,7},{9,8},{10,9},{11,1... | collective-permute-start | bytes 1081352 | tf_op jit(solution)/shard_map/ppermute | solution.py:605
  37.0 22.0 %all-to-all-start.1 = ((f32[16,16,128]{2,1,0:T(8,128)}), f32[16,16,128]{2,1,0:T(8,128)S(1)}, u32[]{:S(2)}, u32[]{:S(2)}) async-start(f32[16,16,128]{2,1,0:T(8,128)} %bitcast.4), calls=%async_computation.1 | async-start | bytes 262144 | tf_op jit(solution)/shard_map/all_to_all | solution.py:644
  45.9 1.4 %copy-start.8 = (s32[12,32]{1,0:T(8,128)S(1)}, s32[12,32]{1,0:T(8,128)}, u32[]{:S(2)}) copy-start(s32[12,32]{1,0:T(8,128)} %refs_1_.3) | copy-start | bytes 4612
  47.3 11.7 %copy-start = (f32[64,4096]{1,0:T(8,128)S(1)}, f32[64,4096]{1,0:T(8,128)}, u32[]{:S(2)}) copy-start(f32[64,4096]{1,0:T(8,128)} %basis_ref.1) | copy-start | bytes 3145732

commit v6 on v5

--- a/solution.py
+++ b/solution.py
@@ -165,46 +165,40 @@
         both = dot_t(left, jnp.concatenate([part, part], axis=0))
         expansions.append(both.reshape(2, rhs, LANES))
     current = jnp.concatenate(expansions, axis=0)
-    matrix = up_matrix(transfer_ref)
-    base = 0
-    sent = []
-    for level in range(4):
-        size = (leaves >> level) * rhs
-        local_ref[base : base + size, :] = current.reshape(size, LANES)
-        rows = pl.ds(base, size)
-        copy = pltpu.make_async_copy(
-            local_ref.at[rows, :], local_out.at[rows, :], arrived.at[len(moves) + level]
-        )
-        copy.start()
-        sent.append(copy)
-        base += size
-        current = up(current, matrix)
-    message = packed(current[0], current[1])
+    local_ref[...] = current.reshape(local_ref.shape)
+    sent = pltpu.make_async_copy(local_ref, local_out, arrived.at[len(moves)])
+    sent.start()
+    one = jnp.concatenate([transfer_ref[0], transfer_ref[1]], axis=0)
+    two = dot(one, jnp.concatenate([transfer_ref[0], transfer_ref[1]], axis=1))
+    half = LANES // 2
+    quarters = [
+        two[low * half : (low + 1) * half, high * half : (high + 1) * half]
+        for high in range(2)
+        for low in range(2)
+    ]
+    four = dot(jnp.concatenate(quarters, axis=0), jnp.concatenate(quarters, axis=1))
+    path = jnp.concatenate([four[:, k * half : (k + 1) * half] for k in range(4)], axis=0)
+    pairs = paired(current).reshape(2, leaves // 4, rhs, LANES)
+    rows = jnp.concatenate([pairs[:, k] for k in range(leaves // 4)], axis=2)
+    above = dot(rows.reshape(2 * rhs, leaves // 4 * LANES), twice(path))
+    message = packed(above[:rhs], above[rhs:])
     for peer in range(message_ref.shape[0] // rhs):
         message_ref[peer * rhs : (peer + 1) * rhs, :] = message
-    for copy in sent:
-        copy.wait()
-
-
-def tables_kernel(
-    total_leaves,
-    levels,
-    dev_ref,
+    sent.wait()
+
+
+def payload_kernel(
     points_ref,
     charges_ref,
-    ordering_ref,
     transfer_ref,
-    coupling_ref,
-    local_ref,
+    lowest_ref,
+    _,
     pay_right_ref,
     pay_left_ref,
-    counts_ref,
-    inverse_ref,
-    paths_ref,
+    local_ref,
 ):
-    device = dev_ref[0]
     rhs = charges_ref.shape[0]
-    leaves = ordering_ref.shape[0]
+    leaves = charges_ref.shape[1] // LANES
     for leaf in range(leaves):
         cols = slice(leaf * LANES, (leaf + 1) * LANES)
         for ref in (pay_right_ref, pay_left_ref):
@@ -212,16 +206,37 @@
             for axis in range(3):
                 at = leaves * (rhs + axis) + leaf
                 ref[at : at + 1, :] = points_ref[axis : axis + 1, cols]
-    for ref, skip in ((pay_right_ref, True), (pay_left_ref, False)):
-        edges = []
-        base = 0
-        for level in range(4):
-            count = leaves >> level
-            start = base + (count - 3) * rhs if skip else base
-            edges.append(local_ref[start : start + 3 * rhs, :].reshape(3, rhs, LANES))
-            base += count * rhs
+    current = lowest_ref[...].reshape(leaves, rhs, LANES)
+    matrix = up_matrix(transfer_ref)
+    base = 0
+    lasts, firsts = [], []
+    for level in range(4):
+        count = leaves >> level
+        local_ref[base : base + count * rhs, :] = current.reshape(count * rhs, LANES)
+        lasts.append(current[count - 3 :])
+        firsts.append(current[:3])
+        base += count * rhs
+        if level < 3:
+            current = up(current, matrix)
+    for ref, edges in ((pay_right_ref, lasts), (pay_left_ref, firsts)):
         pairs = paired(jnp.concatenate(edges, axis=0))
         ref[leaves * (rhs + 3) :, :] = pairs.reshape(6 * rhs, LANES)
+
+
+def tables_kernel(
+    total_leaves,
+    levels,
+    dev_ref,
+    ordering_ref,
+    transfer_ref,
+    coupling_ref,
+    _,
+    counts_ref,
+    inverse_ref,
+    paths_ref,
+):
+    device = dev_ref[0]
+    leaves = ordering_ref.shape[0]
     slots = lax.broadcasted_iota(jnp.int32, (LANES, LANES), 0)
     numbers = lax.broadcasted_iota(jnp.int32, (16, LANES), 1).astype(jnp.float32)
     numbers = numbers.astype(jnp.bfloat16)
@@ -266,8 +281,35 @@
             )
 
 
+def inverse_distance(table, squared, qx, qy, qz):
+    columns = jnp.transpose(table)
+    ax, ay, az, size = [
+        jnp.broadcast_to(columns[:, kind : kind + 1], (LANES, LANES)) for kind in range(4)
+    ]
+    return lax.rsqrt(((size + squared) + ax * qx) + (ay * qy + az * qz))
+
+
+def own_kernel(points_ref, charges_ref, _, out_ref):
+    rhs = charges_ref.shape[0]
+    for leaf in range(charges_ref.shape[1] // LANES):
+        cols = slice(leaf * LANES, (leaf + 1) * LANES)
+        qx, qy, qz = [points_ref[axis : axis + 1, cols] - 0.5 for axis in range(3)]
+        squared = qx * qx + (qy * qy + qz * qz)
+        table = jnp.concatenate(
+            [-2.0 * qx, -2.0 * qy, -2.0 * qz, squared + DELTA * DELTA]
+            + [jnp.zeros((4, LANES), jnp.float32)],
+            axis=0,
+        )
+        value = inverse_distance(table, squared, qx, qy, qz)
+        piece = jnp.concatenate(halves(value), axis=0)
+        side = jnp.concatenate(halves(charges_ref[:, cols] * (0.25 / math.pi)), axis=0)
+        total = bf16_dot(side, piece, ((1,), (1,)))
+        half = total[:, :LANES] + total[:, LANES:]
+        out_ref[:, cols] = half[0:rhs, :] + half[rhs : 2 * rhs, :]
+
+
 def near_kernel(
-    total_leaves, dev_ref, near_in, own_ref, before_ref, after_ref, *rest
+    total_leaves, dev_ref, near_in, own_ref, before_ref, after_ref, itself_ref, *rest
 ):
     out_ref, places, weights, near_ref, arrived = rest[-5:]
     copy = pltpu.make_async_copy(near_in, near_ref, arrived)
@@ -314,7 +356,7 @@
         total = jnp.zeros((2 * rhs, 2 * LANES), jnp.float32)
         for pair in range(entries // 2):
             highs, lows, sides = [], [], []
-            for entry in (2 * pair, 2 * pair + 1):
+            for entry in range(2 * pair + 1, min(2 * pair + 3, entries)):
                 window = (
                     (near_ref[entry, leaf] - target + half_cycle) & (total_leaves - 1)
                 ) - half_cycle
@@ -333,9 +375,8 @@
             )
             total = total + bf16_dot(jnp.concatenate(sides, axis=1), piece, ((1,), (1,)))
         half = total[:, :LANES] + total[:, LANES:]
-        out_ref[:, pl.ds(pl.multiple_of(leaf * LANES, LANES), LANES)] = (
-            half[0:rhs, :] + half[rhs : 2 * rhs, :]
-        )
+        cols = pl.ds(pl.multiple_of(leaf * LANES, LANES), LANES)
+        out_ref[:, cols] = itself_ref[:, cols] + (half[0:rhs, :] + half[rhs : 2 * rhs, :])
         return carry
 
     lax.fori_loop(0, leaves, one, 0, unroll=16)
@@ -402,6 +443,7 @@
     transfer_ref,
     stack_ref,
     paths_ref,
+    _,
     out_ref,
     x_ref,
     top_ref,
@@ -545,10 +587,11 @@
     smem = pl.BlockSpec(memory_space=pltpu.SMEM)
     vmem = pl.BlockSpec(memory_space=pltpu.VMEM)
     hbm = pl.BlockSpec(memory_space=pltpu.HBM)
+    anywhere = pl.BlockSpec(memory_space=pl.ANY)
     return pl.pallas_call(
         kernel,
         out_shape=outs,
-        in_specs=[smem] * len(scalars) + [vmem] * len(operands) + [hbm] * len(kept),
+        in_specs=[smem] * len(scalars) + [vmem] * len(operands) + [anywhere] * len(kept),
         out_specs=[hbm] * far + [vmem] * (len(outs) - far) if isinstance(outs, list) else vmem,
         scratch_shapes=list(scratch),
         cost_estimate=cost,
@@ -571,35 +614,56 @@
     local_rows = (leaves * 2 - 4) * rhs
 
     inputs = [charges, ids, basis, transfer]
-    local_terms, message = call(
+    lowest, message = call(
         expand_kernel,
         [
-            jax.ShapeDtypeStruct((local_rows, LANES), f32),
+            jax.ShapeDtypeStruct((leaves * rhs, LANES), f32),
             jax.ShapeDtypeStruct((groups * rhs, LANES), f32),
         ],
         [],
         [],
         [
             *[pltpu.VMEM(array.shape, array.dtype) for array in inputs],
-            pltpu.VMEM((local_rows, LANES), f32),
-            pltpu.SemaphoreType.DMA((len(inputs) + 4,)),
+            pltpu.VMEM((leaves * rhs, LANES), f32),
+            pltpu.SemaphoreType.DMA((len(inputs) + 1,)),
         ],
         kept=inputs,
         limit=FIRST_BYTES,
         far=1,
     )
-    pay_right, pay_left, counts, inverse, paths = call(
+    counts, inverse, paths = call(
         lambda *refs: tables_kernel(total_leaves, levels, *refs),
         [
-            jax.ShapeDtypeStruct((pay_rows, LANES), f32),
-            jax.ShapeDtypeStruct((pay_rows, LANES), f32),
             jax.ShapeDtypeStruct((4 * levels, LANES), f32),
             jax.ShapeDtypeStruct((leaves, LANES), jnp.int32),
             jax.ShapeDtypeStruct((LANES, (TOP - 4) * LANES), f32),
         ],
         [device],
-        [points, charges, ids, transfer, coupling_list, local_terms],
+        [ids, transfer, coupling_list],
         cost=pl.CostEstimate(flops=1 << 28, bytes_accessed=2 << 20, transcendentals=0),
+        kept=[message],
+    )
+    pay_right, pay_left, local_terms = call(
+        payload_kernel,
+        [
+            jax.ShapeDtypeStruct((pay_rows, LANES), f32),
+            jax.ShapeDtypeStruct((pay_rows, LANES), f32),
+            jax.ShapeDtypeStruct((local_rows, LANES), f32),
+        ],
+        [],
+        [points, charges, transfer, lowest],
+        cost=pl.CostEstimate(flops=1 << 28, bytes_accessed=2 << 20, transcendentals=0),
+        kept=[paths],
+    )
+    itself = call(
+        own_kernel,
+        jax.ShapeDtypeStruct(charges.shape, f32),
+        [],
+        [points, charges],
+        cost=pl.CostEstimate(
+            flops=leaves * 128 * 128 * 100, bytes_accessed=1 << 20, transcendentals=0
+        ),
+        kept=[local_terms],
     )
     before = lax.ppermute(pay_right, "leaf", [(i, (i + 1) % devices) for i in range(devices)])
     after = lax.ppermute(pay_left, "leaf", [((i + 1) % devices, i) for i in range(devices)])
@@ -640,6 +704,7 @@
                 for step in range(TOP - 4)
             ],
         ],
+        kept=[itself],
     )
     parts = lax.all_to_all(
         spread,
@@ -653,7 +718,7 @@
         lambda *refs: near_kernel(total_leaves, *refs),
         jax.ShapeDtypeStruct((rhs, leaves * LANES), f32),
         [device],
-        [near_list, pay_right, before, after],
+        [near_list, pay_right, before, after, itself],
         [
             pltpu.VMEM((4, 3 * leaves, LANES), f32),
             pltpu.VMEM((3 * leaves, 2 * rhs, LANES), jnp.bfloat16),

time: 61.2 us -> 59.8 us (0.977)
  waiting for transfers between devices: 4.86 us -> 1.07 us
  Pallas kernels: 24.4 us -> 27 us
    all_to_all x1, waiting for transfers between devices: 4.86 us -> 1.06 us  [local(): lax.all_to_all(message, 'leaf', 0, 0, axis_index_groups=[[g * GROUP + i f...]
    pallas_call x6 -> x8, Pallas kernels: 24.4 us -> 27 us  [call(): pl.pallas_call(kernel, out_shape=outs, in_specs=[smem] * len(scalars) + [...]
  transfers between devices with their start and end apart: 4 -> 4, of which waited for: 1 -> 1; matrix products, arithmetic and copies ran while one was open for 0% -> 0% of each run, Pallas kernels for 30% -> 36%
where the time goes in v6:
time: 59.8 us; the launch traced here: 59.4 us
  starting transfers between devices  31.1 us (52%)
  Pallas kernels  27 us (45%)
  waiting for transfers between devices  1.07 us (2%)
    pallas_call x8, Pallas kernels, call(): pl.pallas_call(kernel, out_shape=outs, in_specs=[smem] * len(scalars) + [...  27 us
    all_to_all x1, starting transfers between devices, local(): lax.all_to_all(message, 'leaf', 0, 0, axis_index_groups=[[g * GROUP + i f...  16.6 us
    all_to_all x1, starting transfers between devices, local(): lax.all_to_all(spread, 'leaf', 0, 0, axis_index_groups=[[g * GROUP + i fo...  8.55 us
    ppermute x1, starting transfers between devices, local(): lax.ppermute(pay_right, 'leaf', [(i, (i + 1) % devices) for i in range(de...  3.96 us
    ppermute x1, starting transfers between devices, local(): lax.ppermute(pay_left, 'leaf', [((i + 1) % devices, i) for i in range(dev...  1.92 us
  transfers between devices with their start and end apart: 4, of which 1 were waited for; matrix products, arithmetic and copies ran while one was open for 0% of the time, Pallas kernels for 36%

profile of v6, /device:TPU:1, one launch (start us, length us, event | category | flops | bytes accessed | tf_op | source)
XLA Modules:
  0.0 59.4 jit_solution(8713943091939024378)
XLA Ops:
  0.0 3.7 %shard_map.82 = (f32[512,128]{1,0:T(8,128)}, f32[512,128]{1,0:T(8,128)}) custom-call(f32[16,4096]{1,0:T(8,128)} %charges_ref.3, s32[32,128]{1,0:T(8,128)} %bitcast.9, f32[64,4096]{1,0:T(8,128)} %basis_ref.1, f32[2,64,64]{2,1,0:T(8,128)} %transfer_ref.3), custom_call_target="tpu_custom_call" | custom-call | tf_op jit(solution)/shard_map/pallas_call | solution.py:591
  3.7 0.0 copy-start.2
  3.7 0.0 copy-start.6
  3.7 16.6 %all-to-all-start = ((f32[32,16,128]{2,1,0:T(8,128)}), f32[32,16,128]{2,1,0:T(8,128)S(1)}, u32[]{:S(2)}, u32[]{:S(2)}) async-start(f32[32,16,128]{2,1,0:T(8,128)} %bitcast.8), calls=%async_computation | async-start | bytes 524288 | tf_op jit(solution)/shard_map/all_to_all | solution.py:670
  20.4 0.0 copy-start.1
  20.5 0.0 copy-start.5
  20.5 0.0 copy-start.8
  20.5 1.2 %shard_map.83 = (f32[48,128]{1,0:T(8,128)S(1)}, s32[32,128]{1,0:T(8,128)S(1)}, f32[128,640]{1,0:T(8,128)S(1)}) custom-call(s32[1]{0:T(128)} %bitcast.refs_0_.dev_ref, s32[32,128]{1,0:T(8,128)S(1)} %bitcast.10, f32[2,64,64]{2,1,0:T(8,128)S(1)} %copy-done.2, s32[4,32760]{1,0:T(4,128)S(1)} %copy-done.7, f32[512,128]{1,0:T(8,128)S(1)} %copy-done.4), custom_call_target="tpu_custom_call" | custom-call | flops 268435456 | bytes 2097152 | tf_op jit(solution)/shard_map/pallas_call | solution.py:591
  21.7 0.0 copy-done.1
  21.7 0.6 %shard_map.84 = (f32[704,128]{1,0:T(8,128)S(1)}, f32[704,128]{1,0:T(8,128)S(1)}, f32[960,128]{1,0:T(8,128)S(1)}) custom-call(f32[3,4096]{1,0:T(4,128)S(1)} %copy-done.5, f32[16,4096]{1,0:T(8,128)S(1)} %copy-done.1, f32[2,64,64]{2,1,0:T(8,128)S(1)} %copy-done.2, f32[512,128]{1,0:T(8,128)S(1)} %copy-done.8, f32[128,640]{1,0:T(8,128)S(1)} %get-tuple-element.15._.refs_5_), custom_call_target="tpu_custom_call" | custom-call | flops 268435456 | bytes 2097152 | tf_op jit(solution)/shard_map/pallas_call | solution.py:591
  22.4 4.0 %collective-permute-start = (f32[704,128]{1,0:T(8,128)S(1)}, f32[704,128]{1,0:T(8,128)S(1)}, u32[]{:S(2)}, u32[]{:S(2)}) collective-permute-start(f32[704,128]{1,0:T(8,128)S(1)} %get-tuple-element.18.refs_2_), channel_id=1, source_target_pairs={{0,1},{1,2},{2,3},{3,4},{4,5},{5,6},{6,7},{7,8},{8,9},{9,10},{10,1... | collective-permute-start | bytes 1081352 | tf_op jit(solution)/shard_map/ppermute | solution.py:668
  26.3 1.9 %collective-permute-start.1 = (f32[704,128]{1,0:T(8,128)S(1)}, f32[704,128]{1,0:T(8,128)S(1)}, u32[]{:S(2)}, u32[]{:S(2)}) collective-permute-start(f32[704,128]{1,0:T(8,128)S(1)} %get-tuple-element.19), channel_id=1, source_target_pairs={{1,0},{2,1},{3,2},{4,3},{5,4},{6,5},{7,6},{8,7},{9,8},{10,9},{11,1... | collective-permute-start | bytes 1081352 | tf_op jit(solution)/shard_map/ppermute | solution.py:669
  28.3 0.0 copy-start.3
  28.3 3.2 %shard_map.85.refs_6_.refs_5_ = f32[16,4096]{1,0:T(8,128)S(1)} custom-call(f32[3,4096]{1,0:T(4,128)S(1)} %copy-done.5, f32[16,4096]{1,0:T(8,128)S(1)} %copy-done.1, f32[960,128]{1,0:T(8,128)S(1)} %get-tuple-element.17._.local_ref), custom_call_target="tpu_custom_call" | custom-call | flops 52428800 | bytes 1048576 | tf_op jit(solution)/shard_map/pallas_call | solution.py:591
  31.4 1.1 %all-to-all-done = f32[32,16,128]{2,1,0:T(8,128)S(1)} async-done(((f32[32,16,128]{2,1,0:T(8,128)}), f32[32,16,128]{2,1,0:T(8,128)S(1)}, u32[]{:S(2)}, u32[]{:S(2)}) %all-to-all-start) | async-done | bytes 262176 | tf_op jit(solution)/shard_map/all_to_all | solution.py:670
  32.5 4.2 %shard_map.86.refs_6_ = f32[256,128]{1,0:T(8,128)} custom-call(s32[1]{0:T(128)} %bitcast.refs_0_.dev_ref, f32[48,128]{1,0:T(8,128)S(1)} %get-tuple-element.14.refs_1_.counts_in, f32[512,128]{1,0:T(8,128)S(1)} %bitcast.6, f32[2,64,64]{2,1,0:T(8,128)S(1)} %copy-done.2, f32[256,128]{1,0:T(8,128)S(1)} %copy-done.3, f32[128,640]{1,0:T(8,128)S(1)} %get-tuple-element.15._.refs_5_, ...), custom_call_target="tpu_custom_call" | custom-call | tf_op jit(solution)/shard_map/pallas_call | solution.py:591
  36.7 8.6 %all-to-all-start.1 = ((f32[16,16,128]{2,1,0:T(8,128)}), f32[16,16,128]{2,1,0:T(8,128)S(1)}, u32[]{:S(2)}, u32[]{:S(2)}) async-start(f32[16,16,128]{2,1,0:T(8,128)} %bitcast.4), calls=%async_computation.1 | async-start | bytes 262144 | tf_op jit(solution)/shard_map/all_to_all | solution.py:709
  45.3 0.0 collective-permute-done.before_ref.refs_3_
  45.3 0.0 collective-permute-done.1.after_ref.refs_4_
  45.3 1.4 %shard_map.87.terms_ref = f32[480,128]{1,0:T(8,128)S(1)} custom-call(s32[1]{0:T(128)} %bitcast.refs_0_.dev_ref, f32[48,128]{1,0:T(8,128)S(1)} %get-tuple-element.14.refs_1_.counts_in, f32[960,128]{1,0:T(8,128)S(1)} %get-tuple-element.17._.local_ref, f32[704,128]{1,0:T(8,128)S(1)} %collective-permute-done.before_ref.refs_3_, ...), custom_call_target="tpu_custom_call" | custom-call | tf_op jit(solution)/shard_map/pallas_call | solution.py:591
  46.7 0.0 copy-start
  46.7 10.9 %shard_map.88.near_ref = f32[16,4096]{1,0:T(8,128)S(1)} custom-call(s32[1]{0:T(128)} %bitcast.refs_0_.dev_ref, s32[12,32]{1,0:T(8,128)S(1)} %copy-done.9, f32[704,128]{1,0:T(8,128)S(1)} %get-tuple-element.18.refs_2_, f32[704,128]{1,0:T(8,128)S(1)} %collective-permute-done.before_ref.refs_3_, f32[704,128]{1,0:T(8,128)S(1)} %collective-permute-done.1.after_ref.refs_4_, ...), custom_call_target="tpu_custom_call" | custom-call | flops 629145600 | bytes 8388608 | tf_op jit(solution)/shard_map/pallas_call | solution.py:591
  57.6 0.0 all-to-all-done.1
  57.6 1.8 %shard_map.89 = f32[16,4096]{1,0:T(8,128)} custom-call(f32[256,128]{1,0:T(8,128)S(1)} %bitcast.7, f32[480,128]{1,0:T(8,128)S(1)} %shard_map.87.terms_ref, f32[2,64,64]{2,1,0:T(8,128)S(1)} %copy-done.2, f32[64,4096]{1,0:T(8,128)S(1)} %copy-done, s32[32,128]{1,0:T(8,128)S(1)} %get-tuple-element.20.inverse_ref, f32[16,4096]{1,0:T(8,128)S(1)} %shard_map.88.near_ref), custom_call_target="tpu_custom_call" | custom-call | tf_op jit(solution)/shard_map/pallas_call | solution.py:591
  (12 shorter events, 0.0 us)
Async XLA Ops:
  0.0 20.4 %copy-start.7 = (s32[4,32760]{1,0:T(4,128)S(1)}, s32[4,32760]{1,0:T(4,128)}, u32[]{:S(2)}) copy-start(s32[4,32760]{1,0:T(4,128)} %refs_3_.2) | copy-start | bytes 1572484
  3.7 16.7 %copy-start.2 = (f32[2,64,64]{2,1,0:T(8,128)S(1)}, f32[2,64,64]{2,1,0:T(8,128)}, u32[]{:S(2)}) copy-start(f32[2,64,64]{2,1,0:T(8,128)} %transfer_ref.3) | copy-start | bytes 98308
  3.7 16.7 %copy-start.4 = (f32[512,128]{1,0:T(8,128)S(1)}, f32[512,128]{1,0:T(8,128)}, u32[]{:S(2)}) copy-start(f32[512,128]{1,0:T(8,128)} %get-tuple-element.13.refs_4_) | copy-start | bytes 786436
  3.7 16.7 %copy-start.6 = (s32[4096]{0:T(1024)S(1)}, s32[4096]{0:T(1024)}, u32[]{:S(2)}) copy-start(s32[4096]{0:T(1024)} %param.14) | copy-start | bytes 49156
  3.7 28.8 %all-to-all-start = ((f32[32,16,128]{2,1,0:T(8,128)}), f32[32,16,128]{2,1,0:T(8,128)S(1)}, u32[]{:S(2)}, u32[]{:S(2)}) async-start(f32[32,16,128]{2,1,0:T(8,128)} %bitcast.8), calls=%async_computation | async-start | bytes 524288 | tf_op jit(solution)/shard_map/all_to_all | solution.py:670
  20.4 1.2 %copy-start.1 = (f32[16,4096]{1,0:T(8,128)S(1)}, f32[16,4096]{1,0:T(8,128)}, u32[]{:S(2)}) copy-start(f32[16,4096]{1,0:T(8,128)} %charges_ref.3) | copy-start | bytes 786436
  20.5 1.2 %copy-start.5 = (f32[3,4096]{1,0:T(4,128)S(1)}, f32[3,4096]{1,0:T(4,128)}, u32[]{:S(2)}) copy-start(f32[3,4096]{1,0:T(4,128)} %points_ref.3) | copy-start | bytes 147460
  20.5 1.2 %copy-start.8 = (f32[512,128]{1,0:T(8,128)S(1)}, f32[512,128]{1,0:T(8,128)}, u32[]{:S(2)}) copy-start(f32[512,128]{1,0:T(8,128)} %get-tuple-element.16.lowest_ref) | copy-start | bytes 786436
  22.4 22.9 %collective-permute-start = (f32[704,128]{1,0:T(8,128)S(1)}, f32[704,128]{1,0:T(8,128)S(1)}, u32[]{:S(2)}, u32[]{:S(2)}) collective-permute-start(f32[704,128]{1,0:T(8,128)S(1)} %get-tuple-element.18.refs_2_), channel_id=1, source_target_pairs={{0,1},{1,2},{2,3},{3,4},{4,5},{5,6},{6,7},{7,8},{8,9},{9,10},{10,1... | collective-permute-start | bytes 1081352 | tf_op jit(solution)/shard_map/ppermute | solution.py:668
  26.3 18.9 %collective-permute-start.1 = (f32[704,128]{1,0:T(8,128)S(1)}, f32[704,128]{1,0:T(8,128)S(1)}, u32[]{:S(2)}, u32[]{:S(2)}) collective-permute-start(f32[704,128]{1,0:T(8,128)S(1)} %get-tuple-element.19), channel_id=1, source_target_pairs={{1,0},{2,1},{3,2},{4,3},{5,4},{6,5},{7,6},{8,7},{9,8},{10,9},{11,1... | collective-permute-start | bytes 1081352 | tf_op jit(solution)/shard_map/ppermute | solution.py:669
  28.3 4.2 %copy-start.3 = (f32[256,128]{1,0:T(8,128)S(1)}, f32[256,128]{1,0:T(8,128)}, u32[]{:S(2)}) copy-start(f32[256,128]{1,0:T(8,128)} %constant.6.clone.refs_4_.stack_ref) | copy-start | bytes 393220
  36.7 20.9 %all-to-all-start.1 = ((f32[16,16,128]{2,1,0:T(8,128)}), f32[16,16,128]{2,1,0:T(8,128)S(1)}, u32[]{:S(2)}, u32[]{:S(2)}) async-start(f32[16,16,128]{2,1,0:T(8,128)} %bitcast.4), calls=%async_computation.1 | async-start | bytes 262144 | tf_op jit(solution)/shard_map/all_to_all | solution.py:709
  45.3 1.4 %copy-start.9 = (s32[12,32]{1,0:T(8,128)S(1)}, s32[12,32]{1,0:T(8,128)}, u32[]{:S(2)}) copy-start(s32[12,32]{1,0:T(8,128)} %refs_1_.1) | copy-start | bytes 4612
  46.7 10.9 %copy-start = (f32[64,4096]{1,0:T(8,128)S(1)}, f32[64,4096]{1,0:T(8,128)}, u32[]{:S(2)}) copy-start(f32[64,4096]{1,0:T(8,128)} %basis_ref.1) | copy-start | bytes 3145732
